TPU v7x, 32 devices: a whole 2x2x4 slice. The times are simulated.
32 devices in a mesh: section: 4 (over x, core), dp: 8 (over z, y).
Axes of the slice: x: 2, y: 2, z: 4, core: 2. Of those that a mesh axis runs over, the one named last changes fastest.
Arguments:
- tokens: bfloat16 [2, 8, 1024, 768], P(None, 'dp'), may hold values from -6 to 6
- episodes: int32 [2, 8, 1024], P(None, 'dp'), may hold values from 0 to 7, never falling along the last dimension, each value on 1 to 512 neighbouring positions
- attn_gain: float32 [2, 768], replicated, may hold values from 0.5 to 1.5
- attn_shift: float32 [2, 768], replicated, may hold values from -2 to 2
- qkv_weight: bfloat16 [2, 768, 2304], replicated, may hold values from -0.21875 to 0.21875
- out_weight: bfloat16 [2, 768, 768], replicated, may hold values from -1.75 to 1.75
- out_bias: float32 [2, 768], replicated, may hold values from -2 to 2
- ffn_gain: float32 [2, 768], replicated, may hold values from 0.5 to 1.5
- ffn_shift: float32 [2, 768], replicated, may hold values from -2 to 2
- up_weight: bfloat16 [2, 768, 3072], replicated, may hold values from -0.21875 to 0.21875
- up_bias: float32 [2, 3072], replicated, may hold values from -2 to 2
- down_weight: bfloat16 [2, 3072, 768], replicated, may hold values from -0.109375 to 0.109375
- down_bias: float32 [2, 768], replicated, may hold values from -2 to 2
- cotangent: bfloat16 [2, 8, 1024, 768], P(None, 'dp'), may hold values from -6 to 6
Outputs:
- final_activations: float32 [2, 8, 1024, 768], P(None, 'dp', 'section')
- input_gradient: float32 [2, 8, 1024, 768], P(None, 'dp', 'section')
- grad_attn_gain: float32 [2, 768], P(None, 'dp')
- grad_attn_shift: float32 [2, 768], P(None, 'dp')
- grad_qkv: float32 [2, 768, 2304], P(None, 'dp')
- grad_out: float32 [2, 768, 768], P(None, 'dp')
- grad_out_bias: float32 [2, 768], P(None, 'dp')
- grad_ffn_gain: float32 [2, 768], P(None, 'dp')
- grad_ffn_shift: float32 [2, 768], P(None, 'dp')
- grad_up: float32 [2, 768, 3072], P(None, 'dp')
- grad_up_bias: float32 [2, 3072], P(None, 'dp')
- grad_down: float32 [2, 3072, 768], P(None, 'dp')
- grad_down_bias: float32 [2, 768], P(None, 'dp')
Inputs may be any that keep to these rules, and one draw needn't show every extreme that they name: `episodes`: in each window the ids never fall and each id covers 1 to 512 consecutive positions.
All inputs are finite; a program needn't handle non-finite values.
Results may differ from a plain program's by a relative error of at most 0.015.
Values may be sent and summed in bfloat16 or wider, within the bound.
No kernel may reach another device: no remote copies, remote signals or barrier semaphores. Data moves between devices by JAX's collectives and lax.ppermute only.
A program may use at most 640 MiB of HBM per device.

v0:
```python
from functools import partial

import jax
import jax.numpy as jnp
from jax import lax
from jax.experimental import pallas as pl
from jax.experimental.pallas import tpu as pltpu
from jax.sharding import PartitionSpec as P

BF = jnp.bfloat16
F32 = jnp.float32
EPS = 1e-05
MASKED = -1e30
D = 768
HALF = 384
PAIR = 128
HEAD_DIM = 64
FF = 3072
LENGTH = 1024
BLOCK = 256
ROWS = 512
PART = 96
GELU_A = 0.7978845608028654
GELU_B = GELU_A * 0.044715


def dot(a, b):
    return jnp.dot(a, b, preferred_element_type=F32)


def dot_nt(a, b):
    return lax.dot_general(a, b, (((1,), (1,)), ((), ())), preferred_element_type=F32)


def dot_tn(a, b):
    return lax.dot_general(a, b, (((0,), (0,)), ((), ())), preferred_element_type=F32)


def normalise(rows):
    center = rows - jnp.mean(rows, -1, keepdims=True)
    spread = lax.rsqrt(jnp.mean(center * center, -1, keepdims=True) + EPS)
    return center * spread, spread


def norm_low(rows, gain, shift):
    unit, _ = normalise(rows.astype(F32))
    return (unit * gain + shift).astype(BF)


def call(body, grid, in_specs, out_specs, out_shape, scratch, cost=None, deps=()):
    count = len(in_specs)

    def with_deps(sc, *refs):
        return body(sc, *refs[:count], *refs[count + len(deps) :])

    kernel = pl.pallas_call(
        with_deps,
        grid_spec=pltpu.PrefetchScalarGridSpec(
            num_scalar_prefetch=1,
            grid=grid,
            in_specs=list(in_specs) + [pl.BlockSpec(memory_space=pl.ANY)] * len(deps),
            out_specs=out_specs,
            scratch_shapes=scratch,
        ),
        out_shape=out_shape,
        compiler_params=pltpu.CompilerParams(vmem_limit_bytes=56 * 1024 * 1024),
        cost_estimate=None
        if cost is None
        else pl.CostEstimate(flops=int(cost[0]), bytes_accessed=int(cost[1]), transcendentals=0),
    )
    return lambda *args: kernel(*args, *deps)


def shape(dims, dtype):
    return jax.ShapeDtypeStruct(dims, dtype)


def whole(dims):
    count = len(dims)
    return pl.BlockSpec(dims, lambda i, sc: (0,) * count)


def at_layer(dims, layer):
    count = len(dims) - 1
    return pl.BlockSpec(dims, lambda i, sc: (layer,) + (0,) * count)


X, C, Y, Z = 0, 1, 2, 3


def in_order(own, other, block, core):
    return jnp.where(core == block % 2, own[block // 2], other[block // 2])


def episode_columns(ep_ref):
    row = jnp.broadcast_to(ep_ref[...].reshape(1, LENGTH).astype(F32), (PAIR, LENGTH))
    return row, row.T


def first_key(i):
    return max(0, i - 2) * BLOCK


def attn_fwd_body(sc, own, other, ep, gain, shift, wq, wk, wv, qkv, ctx, ctx_own, ctx_oth, lse, bias, vext, lse_cols):
    core = sc[C]
    own, other = own.at[0, :, 0], other.at[0, :, 0]
    for b in range(4):
        rows = slice(b * BLOCK, (b + 1) * BLOCK)
        normed = norm_low(in_order(own, other, b, core), gain[0], shift[0])
        qkv[rows, 0:HALF] = (dot(normed, wq[0]).astype(BF) * 0.125).astype(BF)
        qkv[rows, HALF : 2 * HALF] = dot(normed, wk[0]).astype(BF)
        qkv[rows, 2 * HALF : 3 * HALF] = dot(normed, wv[0]).astype(BF)
    ep_row, ep_col = episode_columns(ep)
    for i in range(4):
        lo, hi = first_key(i), (i + 1) * BLOCK
        key_at = lo + lax.broadcasted_iota(jnp.int32, (BLOCK, hi - lo), 1)
        row_at = i * BLOCK + lax.broadcasted_iota(jnp.int32, (BLOCK, hi - lo), 0)
        same = ep_col[i * BLOCK : hi, 0:1] == ep_row[0:1, lo:hi]
        bias[i, :, 0 : hi - lo] = jnp.where((key_at <= row_at) & same, 0.0, MASKED)
    vext[:, PAIR:] = jnp.ones((LENGTH, PAIR), BF)
    lane = lax.broadcasted_iota(jnp.int32, (BLOCK, PAIR), 1)

    @pl.loop(0, 3)
    def _(p):
        at = pl.multiple_of(p * PAIR, PAIR)
        vext[:, 0:PAIR] = qkv[:, pl.ds(2 * HALF + at, PAIR)]
        for i in range(4):
            lo, hi = first_key(i), (i + 1) * BLOCK
            rows = slice(i * BLOCK, hi)
            q = qkv[rows, pl.ds(at, PAIR)]
            k = qkv[lo:hi, pl.ds(HALF + at, PAIR)]
            outs = []
            for h in range(2):
                mine = (lane >= HEAD_DIM) if h else (lane < HEAD_DIM)
                s = dot_nt(jnp.where(mine, q, jnp.zeros_like(q)), k) + bias[i, :, 0 : hi - lo]
                top = jnp.max(s, -1, keepdims=True)
                prob = jnp.exp(s - top).astype(BF)
                o = dot(prob, vext[lo:hi, :])
                total = o[:, PAIR : PAIR + 1]
                outs.append(o[:, 0:PAIR] / total)
                lse_cols[rows, :] = jnp.where(lane == 2 * p + h, top + jnp.log(total), lse_cols[rows, :])
            ctx[rows, pl.ds(at, PAIR)] = jnp.where(lane < HEAD_DIM, outs[0], outs[1]).astype(BF)

    lse[...] = lse_cols[...].T[0:8]
    for b in range(4):
        piece = ctx[b * BLOCK : (b + 1) * BLOCK]

        @pl.when(core == b % 2)
        def _():
            ctx_own[b // 2] = piece

        @pl.when(core != b % 2)
        def _():
            ctx_oth[b // 2] = piece


def attention_forward(scalars, layer, own, own_spec, other, other_spec, episodes, ep_spec, gain, shift, w_qkv):
    columns = [pl.BlockSpec((1, D, HALF), partial(lambda j, i, sc: (layer, 0, 2 * j + sc[C]), j)) for j in range(3)]
    return call(
        attn_fwd_body,
        (1,),
        [own_spec, other_spec, ep_spec, at_layer((1, 1, D), layer), at_layer((1, 1, D), layer)] + columns,
        [
            whole((LENGTH, 3 * HALF)),
            whole((LENGTH, HALF)),
            whole((2, BLOCK, HALF)),
            whole((2, BLOCK, HALF)),
            whole((8, LENGTH)),
        ],
        [
            shape((LENGTH, 3 * HALF), BF),
            shape((LENGTH, HALF), BF),
            shape((2, BLOCK, HALF), BF),
            shape((2, BLOCK, HALF), BF),
            shape((8, LENGTH), F32),
        ],
        [
            pltpu.VMEM((4, BLOCK, 3 * BLOCK), F32),
            pltpu.VMEM((LENGTH, 2 * PAIR), BF),
            pltpu.VMEM((LENGTH, PAIR), F32),
        ],
        (1.8e9 + 2.4e9, 8e6),
    )(scalars, own, other, episodes, gain, shift, w_qkv, w_qkv, w_qkv)


def gelu_parts(u):
    cubic = GELU_B * (u * u)
    t = jnp.tanh(u * (GELU_A + cubic))
    half = 0.5 * t + 0.5
    active = u * half
    slope = half + (active * (1.0 - half)) * (6.0 * cubic + 2.0 * GELU_A)
    return active, slope


FT = 512


def ffn_fwd_body(last, sc, ctx_own, ctx_rcv, own, w_out, b_out, gain, shift, w_up, b_up, w_down, b_down, *rest):
    if last:
        s2, ctx_full, act, slope, keep, send, normed, acc = rest
    else:
        s2, ctx_full, act, slope, s3, normed, acc = rest
    t = pl.program_id(0)
    core = sc[C]

    @pl.when(t == 0)
    def _():
        a, b = ctx_own[...].reshape(ROWS, HALF), ctx_rcv[...].reshape(ROWS, HALF)
        both = jnp.concatenate([jnp.where(core == 0, a, b), jnp.where(core == 0, b, a)], 1)
        ctx_full[...] = both
        stream = own[0, :, 0].reshape(ROWS, D).astype(F32) + dot(both, w_out[0]) + b_out[0]
        low = stream.astype(BF)
        s2[...] = low
        normed[...] = norm_low(low, gain[0], shift[0])
        acc[...] = low.astype(F32) + b_down[0]

    u = dot(normed[...], w_up[0]) + b_up[0]
    a, d = gelu_parts(u)
    a = a.astype(BF)
    act[...] = a
    slope[...] = d.astype(BF)
    acc[...] += dot(a, w_down[0])

    @pl.when(t == FF // FT - 1)
    def _():
        if last:
            x = sc[X]
            keep[...] = acc[pl.ds(pl.multiple_of(x * BLOCK, BLOCK), BLOCK)]
            send[...] = acc[pl.ds(pl.multiple_of((1 - x) * BLOCK, BLOCK), BLOCK)].astype(BF)
        else:
            s3[...] = acc[...].reshape(2, BLOCK, D).astype(BF)


def ffn_forward(scalars, layer, last, ctx_own, ctx_rcv, own, own_spec, weights):
    w_out, b_out, gain, shift, w_up, b_up, w_down, b_down = weights
    vector = at_layer((1, 1, D), layer)
    out_specs = [
        whole((ROWS, D)),
        whole((ROWS, D)),
        pl.BlockSpec((ROWS, FT), lambda i, sc: (0, i)),
        pl.BlockSpec((ROWS, FT), lambda i, sc: (0, i)),
    ]
    out_shape = [shape((ROWS, D), BF), shape((ROWS, D), BF), shape((ROWS, FF), BF), shape((ROWS, FF), BF)]
    if last:
        out_specs += [whole((BLOCK, D)), whole((BLOCK, D))]
        out_shape += [shape((BLOCK, D), F32), shape((BLOCK, D), BF)]
    else:
        out_specs += [whole((2, BLOCK, D))]
        out_shape += [shape((2, BLOCK, D), BF)]
    return call(
        partial(ffn_fwd_body, last),
        (FF // FT,),
        [
            whole((2, BLOCK, HALF)),
            whole((2, BLOCK, HALF)),
            own_spec,
            at_layer((1, D, D), layer),
            vector,
            vector,
            vector,
            pl.BlockSpec((1, D, FT), lambda i, sc: (layer, 0, i)),
            pl.BlockSpec((1, 1, FT), lambda i, sc: (layer, 0, i)),
            pl.BlockSpec((1, FT, D), lambda i, sc: (layer, i, 0)),
            vector,
        ],
        out_specs,
        out_shape,
        [pltpu.VMEM((ROWS, D), BF), pltpu.VMEM((ROWS, D), F32)],
        (5.4e9, 20e6),
    )(scalars, ctx_own, ctx_rcv, own, w_out, b_out, gain, shift, w_up, b_up, w_down, b_down)


def norm_back(d_normed, rows, gain):
    unit, spread = normalise(rows)
    d_unit = d_normed * gain
    first = jnp.mean(d_unit, -1, keepdims=True)
    second = jnp.mean(d_unit * unit, -1, keepdims=True)
    d_rows = spread * (d_unit - first - unit * second)
    return d_rows, jnp.sum(d_normed * unit, 0, keepdims=True), jnp.sum(d_normed, 0, keepdims=True)


def attn_norm_body(last, sc, grad, part, part_rcv, own, gain, *outs):
    grad_rows = grad[...].reshape(ROWS, D).astype(F32)
    d_normed = part[...].reshape(ROWS, D) + part_rcv[...].reshape(ROWS, D).astype(F32)
    d_rows, g_gain, g_shift = norm_back(d_normed, own[0, :, 0].reshape(ROWS, D).astype(F32), gain[0])
    total = grad_rows + d_rows
    small = outs[-1]
    small[0:1] = g_gain
    small[1:2] = g_shift
    small[2:3] = jnp.sum(grad_rows, 0, keepdims=True)
    if last:
        keep, send = outs[0:2]
        keep[...] = jnp.where(sc[X] == 0, total[0:BLOCK], total[BLOCK:ROWS])
        send[...] = jnp.where(sc[X] == 0, total[BLOCK:ROWS], total[0:BLOCK]).astype(BF)
    else:
        outs[0][...] = total.astype(BF).reshape(2, BLOCK, D)


def attention_norm_back(scalars, layer, last, grad, part, part_rcv, own, own_spec, gain, deps=()):
    block = whole((2, BLOCK, D))
    if last:
        out_specs = [whole((BLOCK, D)), whole((BLOCK, D))]
        out_shape = [shape((BLOCK, D), F32), shape((BLOCK, D), BF)]
    else:
        out_specs, out_shape = [block], [shape((2, BLOCK, D), BF)]
    return call(
        partial(attn_norm_body, last),
        (1,),
        [block, block, block, own_spec, at_layer((1, 1, D), layer)],
        out_specs + [whole((3, D))],
        out_shape + [shape((3, D), F32)],
        [],
        (2e8, 5e6),
        deps,
    )(scalars, grad, part, part_rcv, own, gain)


BT = 768


def ffn_back_body(sc, grad, s2, gain, w_up, w_down, slope, dh, ds, small, bias, acc):
    t = pl.program_id(0)
    low = grad[0, :, 0].reshape(ROWS, D)
    d_act = dot_nt(low, w_down[0])
    d_hidden = d_act * slope[...].astype(F32)
    d_low = d_hidden.astype(BF)
    dh[...] = d_low
    bias[...] = jnp.sum(d_low.astype(F32), 0, keepdims=True)
    part = dot_nt(d_low, w_up[0])

    @pl.when(t == 0)
    def _():
        acc[...] = part

    @pl.when(t > 0)
    def _():
        acc[...] += part

    @pl.when(t == FF // BT - 1)
    def _():
        rows = low.astype(F32)
        d_rows, g_gain, g_shift = norm_back(acc[...], s2[...].astype(F32), gain[0])
        ds[...] = (rows + d_rows).astype(BF).reshape(2, BLOCK, D)
        small[0:1] = g_gain
        small[1:2] = g_shift
        small[2:3] = jnp.sum(rows, 0, keepdims=True)


def ffn_backward(scalars, layer, grad, grad_spec, s2, slope, weights, deps=()):
    gain, w_up, w_down = weights
    return call(
        ffn_back_body,
        (FF // BT,),
        [
            grad_spec,
            whole((ROWS, D)),
            at_layer((1, 1, D), layer),
            pl.BlockSpec((1, D, BT), lambda i, sc: (layer, 0, i)),
            pl.BlockSpec((1, BT, D), lambda i, sc: (layer, i, 0)),
            pl.BlockSpec((ROWS, BT), lambda i, sc: (0, i)),
        ],
        [
            pl.BlockSpec((ROWS, BT), lambda i, sc: (0, i)),
            whole((2, BLOCK, D)),
            whole((3, D)),
            pl.BlockSpec((1, BT), lambda i, sc: (0, i)),
        ],
        [shape((ROWS, FF), BF), shape((2, BLOCK, D), BF), shape((3, D), F32), shape((1, FF), F32)],
        [pltpu.VMEM((ROWS, D), F32)],
        (4.9e9, 18e6),
        deps,
    )(scalars, grad, s2, gain, w_up, w_down, slope)


def place(sc, piece):
    return (piece % 2) ^ sc[Y], (piece // 2) ^ sc[Z]


def ffn_weight_body(
    sc, grad, grad_o, s2, s2_o, gain, shift, act, dh, w_up, b_up, w_down, keep, send, n_t, n_o, n_t_o, g_t, g_t_o
):
    t = pl.program_id(0)
    core = sc[C]
    low, low_o = grad[0, :, 0].reshape(ROWS, D), grad_o[0, :, 0].reshape(ROWS, D)

    @pl.when(t == 0)
    def _():
        n_t[...] = norm_low(s2[...], gain[0], shift[0]).T
        other = norm_low(s2_o[...], gain[0], shift[0])
        n_o[...] = other
        n_t_o[...] = other.T
        x = sc[X]
        g_t[...] = jnp.where(x == 0, low[:, 0:HALF], low[:, HALF:D]).T
        g_t_o[...] = jnp.where(x == 0, low_o[:, 0:HALF], low_o[:, HALF:D]).T

    u = dot(n_o[...], w_up[0]) + b_up[0]
    active_o, slope_o = gelu_parts(u)

    @pl.when(t < 2)
    def _():
        dh_o = (dot_nt(low_o, w_down[0]) * slope_o).astype(BF)
        g_up = (dot(n_t[...], dh[...]) + dot(n_t_o[...], dh_o)).astype(BF)
        for ref, when in ((send, 0), (keep, 1)):

            @pl.when(t == when)
            def _():
                for piece in range(8):
                    py, pz = place(sc, piece)
                    for j in range(2):
                        ref[py, pz, j] = g_up[piece * PART : (piece + 1) * PART, j * HALF : (j + 1) * HALF]

    g_down = (dot(g_t[...], act[...]) + dot(g_t_o[...], active_o.astype(BF))).astype(BF).T
    tile = ffn_tile(t, sc)
    for half in range(2):
        py, pz = place(sc, 2 * tile + half)
        for j in range(2):
            first = g_down[half * HALF + j * PART : half * HALF + (j + 1) * PART]
            second = g_down[half * HALF + (j + 2) * PART : half * HALF + (j + 3) * PART]
            keep[py, pz, 2 + j] = jnp.where(core == 0, first, second)
            send[py, pz, 2 + j] = jnp.where(core == 0, second, first)


def ffn_tile(step, sc):
    mine = 2 * sc[X]
    rest = 2 - mine
    return jnp.where(step == 0, mine + 1 - sc[C], jnp.where(step == 1, mine + sc[C], rest + step - 2))


def ffn_weights(scalars, layer, grad, grad_spec, grad_o, grad_o_spec, s2, s2_o, act, dh, weights, deps=()):
    gain, shift, w_up, b_up, w_down = weights
    packed = (2, 4, 4, PART, HALF)
    return call(
        ffn_weight_body,
        (FF // BT,),
        [
            grad_spec,
            grad_o_spec,
            whole((ROWS, D)),
            whole((ROWS, D)),
            at_layer((1, 1, D), layer),
            at_layer((1, 1, D), layer),
            pl.BlockSpec((ROWS, BT), lambda i, sc: (0, ffn_tile(i, sc))),
            pl.BlockSpec((ROWS, BT), lambda i, sc: (0, ffn_tile(jnp.minimum(i, 1), sc))),
            pl.BlockSpec((1, D, BT), lambda i, sc: (layer, 0, ffn_tile(i, sc))),
            pl.BlockSpec((1, 1, BT), lambda i, sc: (layer, 0, ffn_tile(i, sc))),
            pl.BlockSpec((1, BT, D), lambda i, sc: (layer, ffn_tile(jnp.minimum(i, 1), sc), 0)),
        ],
        [whole(packed), whole(packed)],
        [shape(packed, BF), shape(packed, BF)],
        [
            pltpu.VMEM((D, ROWS), BF),
            pltpu.VMEM((ROWS, D), BF),
            pltpu.VMEM((D, ROWS), BF),
            pltpu.VMEM((HALF, ROWS), BF),
            pltpu.VMEM((HALF, ROWS), BF),
        ],
        (8.6e9, 22e6),
        deps,
    )(scalars, grad, grad_o, s2, s2_o, gain, shift, act, dh, w_up, b_up, w_down)


def attn_back_body(
    sc, gr_own, gr_rcv, qkv, ctx, lse, ep, w_out, wq, wk, wv, d_qkv, part_own, part_oth, bias, d_ctx, delta, d_k, d_v
):
    core = sc[C]
    for b in range(4):
        rows = slice(b * BLOCK, (b + 1) * BLOCK)
        d_ctx[rows] = dot_nt(in_order(gr_own, gr_rcv, b, core), w_out[0]).astype(BF)
    product = d_ctx[...].astype(F32) * ctx[...].astype(F32)
    high = product.astype(BF)
    rest = (product - high.astype(F32)).astype(BF)
    picks = (
        lax.broadcasted_iota(jnp.int32, (8, HALF), 0) == lax.broadcasted_iota(jnp.int32, (8, HALF), 1) // HEAD_DIM
    ).astype(BF)
    delta[...] = dot_nt(picks, high) + dot_nt(picks, rest)
    ep_row, ep_col = episode_columns(ep)
    for i in range(4):
        lo, hi = first_key(i), (i + 1) * BLOCK
        key_at = lo + lax.broadcasted_iota(jnp.int32, (hi - lo, BLOCK), 0)
        row_at = i * BLOCK + lax.broadcasted_iota(jnp.int32, (hi - lo, BLOCK), 1)
        same = ep_col[lo:hi, 0:1] == ep_row[0:1, i * BLOCK : hi]
        bias[i, 0 : hi - lo, :] = jnp.where((key_at <= row_at) & same, 0.0, MASKED)

    @pl.loop(0, 3)
    def _(p):
        at = pl.multiple_of(p * PAIR, PAIR)
        d_k[...] = jnp.zeros_like(d_k)
        d_v[...] = jnp.zeros_like(d_v)
        for i in range(4):
            lo, hi = first_key(i), (i + 1) * BLOCK
            rows = slice(i * BLOCK, hi)
            q = qkv[rows, pl.ds(at, PAIR)]
            k = qkv[lo:hi, pl.ds(HALF + at, PAIR)]
            v = qkv[lo:hi, pl.ds(2 * HALF + at, PAIR)]
            dc = d_ctx[rows, pl.ds(at, PAIR)]
            d_q = jnp.zeros((BLOCK, PAIR), F32)
            for h in range(2):

                def only(array):
                    lane = lax.broadcasted_iota(jnp.int32, array.shape, 1)
                    mine = (lane >= HEAD_DIM) if h else (lane < HEAD_DIM)
                    return jnp.where(mine, array, jnp.zeros_like(array))

                q_h, dc_h = only(q), only(dc)
                s = dot_nt(k, q_h) + bias[i, 0 : hi - lo, :]
                prob = jnp.exp(s - lse[pl.ds(2 * p + h, 1), rows])
                d_p = dot_nt(v, dc_h)
                d_s = (prob * (d_p - delta[pl.ds(2 * p + h, 1), rows])).astype(BF)
                d_v[lo:hi] += dot(prob.astype(BF), dc_h)
                d_k[lo:hi] += dot(d_s, q_h)
                d_q += dot_tn(d_s, only(k))
            d_qkv[rows, pl.ds(at, PAIR)] = (d_q * 0.125).astype(BF)
        d_qkv[:, pl.ds(HALF + at, PAIR)] = d_k[...].astype(BF)
        d_qkv[:, pl.ds(2 * HALF + at, PAIR)] = d_v[...].astype(BF)

    for b in range(4):
        rows = slice(b * BLOCK, (b + 1) * BLOCK)
        part = dot_nt(d_qkv[rows, 0:HALF], wq[0])
        part += dot_nt(d_qkv[rows, HALF : 2 * HALF], wk[0])
        part += dot_nt(d_qkv[rows, 2 * HALF : 3 * HALF], wv[0])

        @pl.when(core == b % 2)
        def _():
            part_own[b // 2] = part

        @pl.when(core != b % 2)
        def _():
            part_oth[b // 2] = part.astype(BF)


def attention_backward(scalars, layer, gr_own, gr_rcv, qkv, ctx, lse, episodes, ep_spec, w_out, w_qkv, deps=()):
    columns = [pl.BlockSpec((1, D, HALF), partial(lambda j, i, sc: (layer, 0, 2 * j + sc[C]), j)) for j in range(3)]
    block = whole((2, BLOCK, D))
    return call(
        attn_back_body,
        (1,),
        [
            block,
            block,
            whole((LENGTH, 3 * HALF)),
            whole((LENGTH, HALF)),
            whole((8, LENGTH)),
            ep_spec,
            pl.BlockSpec((1, HALF, D), lambda i, sc: (layer, sc[C], 0)),
        ]
        + columns,
        [whole((LENGTH, 3 * HALF)), block, block],
        [shape((LENGTH, 3 * HALF), BF), shape((2, BLOCK, D), F32), shape((2, BLOCK, D), BF)],
        [
            pltpu.VMEM((4, 3 * BLOCK, BLOCK), F32),
            pltpu.VMEM((LENGTH, HALF), BF),
            pltpu.VMEM((8, LENGTH), F32),
            pltpu.VMEM((LENGTH, PAIR), F32),
            pltpu.VMEM((LENGTH, PAIR), F32),
        ],
        (2.5e9 + 6e9, 12e6),
        deps,
    )(scalars, gr_own, gr_rcv, qkv, ctx, lse, episodes, w_out, w_qkv, w_qkv, w_qkv)


def attn_weight_body(
    sc, own, other, gain, shift, d_qkv, gr_own, gr_rcv, ctx_full, ctx_oth, ctx_rcv, keep, send, n_t, late
):
    core, x = sc[C], sc[X]
    own, other = own.at[0, :, 0], other.at[0, :, 0]
    for b in range(4):
        rows = slice(b * BLOCK, (b + 1) * BLOCK)
        n_t[:, rows] = norm_low(in_order(own, other, b, core), gain[0], shift[0]).T

    def columns(ref):
        rows = ref[...].reshape(ROWS, D)
        return jnp.where(core == 0, rows[:, 0:HALF], rows[:, HALF:D]).T

    a, b = ctx_oth[...].reshape(ROWS, HALF), ctx_rcv[...].reshape(ROWS, HALF)
    far = jnp.concatenate([jnp.where(core == 0, a, b), jnp.where(core == 0, b, a)], 1)
    g_out = (dot(columns(gr_own), ctx_full[...]) + dot(columns(gr_rcv), far)).astype(BF).T

    def grad(j):
        if j == 3:
            return g_out
        return dot(n_t[...], d_qkv[:, j * HALF : (j + 1) * HALF]).astype(BF)

    for j in range(2):
        first, second = grad(j), grad(j + 2)
        mine, yours = jnp.where(x == 0, first, second), jnp.where(x == 0, second, first)
        for piece in range(8):
            py, pz = place(sc, piece)
            keep[py, pz, j] = mine[piece * PART : (piece + 1) * PART]
            send[py, pz, j] = yours[piece * PART : (piece + 1) * PART]


def attention_weights(
    scalars, layer, own, own_spec, other, other_spec, gain, shift, d_qkv, gr_own, gr_rcv, ctx_full, ctx_oth, ctx_rcv, deps=()):
    packed = (2, 4, 2, PART, HALF)
    block = whole((2, BLOCK, D))
    return call(
        attn_weight_body,
        (1,),
        [
            own_spec,
            other_spec,
            at_layer((1, 1, D), layer),
            at_layer((1, 1, D), layer),
            whole((LENGTH, 3 * HALF)),
            block,
            block,
            whole((ROWS, D)),
            whole((2, BLOCK, HALF)),
            whole((2, BLOCK, HALF)),
        ],
        [whole(packed), whole(packed)],
        [shape(packed, BF), shape(packed, BF)],
        [pltpu.VMEM((D, LENGTH), BF), pltpu.VMEM((8, PAIR), F32)],
        (2.5e9, 12e6),
        deps,
    )(scalars, own, other, gain, shift, d_qkv, gr_own, gr_rcv, ctx_full, ctx_oth, ctx_rcv)


def to_core(value):
    return lax.ppermute(value, "section", [(0, 1), (1, 0), (2, 3), (3, 2)])


def to_chip(value):
    return lax.ppermute(value, "section", [(0, 2), (2, 0), (1, 3), (3, 1)])


def to_dp(value, distance):
    return lax.ppermute(value, "dp", [(i, i ^ distance) for i in range(8)])


def total(*terms):
    out = terms[0].astype(F32)
    for term in terms[1:]:
        out = out + term.astype(F32)
    return out.astype(BF)


def reduced_any(keep, send, first):
    both = total(keep, first(send))
    count = both.shape[2]
    return jnp.moveaxis(both, 0, 1).reshape(8, count, PART, HALF)


def gathered(share):
    far, near = to_chip(share), to_core(share)
    return share, far, near, to_core(far)


def unpack_body(sc, *refs):
    shares, (up, down, qkv, out) = refs[:16], refs[16:]
    for layer in range(2):
        for n in range(4):
            x, core = sc[X] ^ (n % 2), sc[C] ^ (n // 2)
            ffn, attn = shares[layer * 8 + n], shares[layer * 8 + 4 + n]
            for j in range(2):
                at = pl.multiple_of(x * 4 * HALF + core * 2 * HALF + j * HALF, PAIR)
                up[layer, :, pl.ds(at, HALF)] = ffn[j].astype(F32)
                rows = pl.ds(pl.multiple_of(core * 2 * PART + j * PART, 8), PART)
                down[layer, rows, pl.ds(pl.multiple_of(x * HALF, PAIR), HALF)] = ffn[2 + j].astype(F32)
            side = pl.multiple_of(core * HALF, PAIR)
            qkv[layer, :, pl.ds(pl.multiple_of(x * 2 * D + side, PAIR), HALF)] = attn[0].astype(F32)

            @pl.when(x == 0)
            def _():
                qkv[layer, :, pl.ds(pl.multiple_of(D + side, PAIR), HALF)] = attn[1].astype(F32)

            @pl.when(x == 1)
            def _():
                out[layer, :, pl.ds(side, HALF)] = attn[1].astype(F32)


def unpacked(scalars, shares):
    dims = ((2, PART, FF), (2, 4 * PART, D), (2, PART, 3 * D), (2, PART, D))
    return call(
        unpack_body,
        (1,),
        [whole(share.shape) for share in shares],
        [whole(d) for d in dims],
        [shape(d, F32) for d in dims],
        [],
        (1e6, 11e6),
    )(scalars, *shares)


def on_device(
    tokens,
    episodes,
    attn_gain,
    attn_shift,
    qkv_weight,
    out_weight,
    out_bias,
    ffn_gain,
    ffn_shift,
    up_weight,
    up_bias,
    down_weight,
    down_bias,
    cotangent,
):
    replicas = lax.axis_size("dp")
    section = lax.axis_index("section")
    replica = lax.axis_index("dp")
    chip, core = section // 2, section % 2
    direct = replicas == 8
    y, z = (replica % 2, replica // 2) if direct else (0, 0)
    scalars = jnp.stack([jnp.asarray(v, jnp.int32) for v in (chip, core, y, z)])

    stream = tokens.reshape(2, 2, 2, BLOCK, D)
    cot = cotangent.reshape(2, 2, 2, BLOCK, D)
    eps = episodes.reshape(2, 1, LENGTH)
    ep_spec = pl.BlockSpec((1, 1, LENGTH), lambda i, sc: (sc[X], 0, 0))

    def input_spec(micro, side):
        return pl.BlockSpec((1, 2, 1, BLOCK, D), lambda i, sc: (micro(sc[X]), 0, side(sc[C]), 0, 0))

    same, flip = (lambda v: v), (lambda v: 1 - v)
    own_in, other_in, far_in = input_spec(same, same), input_spec(same, flip), input_spec(flip, same)
    local = pl.BlockSpec((1, 2, 1, BLOCK, D), lambda i, sc: (0, 0, 0, 0, 0))

    def rows5(value):
        return value.reshape(1, 2, 1, BLOCK, D)

    def vec(array):
        return array.reshape(2, 1, -1)

    a_gain, a_shift, b_out = vec(attn_gain), vec(attn_shift), vec(out_bias)
    f_gain, f_shift, b_up, b_down = vec(ffn_gain), vec(ffn_shift), vec(up_bias), vec(down_bias)

    kept = []
    own, own_spec, other, other_spec = stream, own_in, stream, other_in
    for layer in range(2):
        qkv, ctx, ctx_own, ctx_oth, lse = attention_forward(
            scalars, layer, own, own_spec, other, other_spec, eps, ep_spec, a_gain, a_shift, qkv_weight
        )
        ctx_rcv = to_core(ctx_oth)
        ctx_far = to_core(ctx_own)
        s2, ctx_full, act, slope, *result = ffn_forward(
            scalars,
            layer,
            layer == 1,
            ctx_own,
            ctx_rcv,
            own,
            own_spec,
            (out_weight, b_out, f_gain, f_shift, up_weight, b_up, down_weight, b_down),
        )
        s2_o = to_chip(s2)
        kept.append((own, own_spec, other, other_spec, qkv, ctx, ctx_oth, ctx_far, ctx_full, lse, s2, s2_o, act, slope))
        if layer == 0:
            s3 = result[0]
            own, own_spec, other, other_spec = rows5(s3), local, rows5(to_core(s3)), local
    final_keep, final_send = result

    def ffn_back(layer, grad, grad_spec, deps=()):
        kept_now = kept[layer]
        s2, slope = kept_now[10], kept_now[13]
        return ffn_backward(scalars, layer, grad, grad_spec, s2, slope, (f_gain, up_weight, down_weight), deps)

    def ffn_grads(layer, grad, grad_spec, grad_o, grad_o_spec, dh, deps=()):
        s2, s2_o, act, slope = kept[layer][10:]
        weights = (f_gain, f_shift, up_weight, b_up, down_weight)
        return ffn_weights(
            scalars, layer, grad, grad_spec, grad_o, grad_o_spec, s2, s2_o, act, dh, weights, deps
        )

    def attn_back(layer, ds, ds_rcv, deps=()):
        own, own_spec, other, other_spec, qkv, ctx, ctx_oth, ctx_far, ctx_full, lse = kept[layer][:10]
        return attention_backward(
            scalars, layer, ds, ds_rcv, qkv, ctx, lse, eps, ep_spec, out_weight, qkv_weight, deps
        )

    def attn_grads(layer, ds, ds_rcv, d_qkv, deps=()):
        own, own_spec, other, other_spec, qkv, ctx, ctx_oth, ctx_far, ctx_full, lse = kept[layer][:10]
        return attention_weights(
            scalars, layer, own, own_spec, other, other_spec, a_gain, a_shift, d_qkv, ds, ds_rcv, ctx_full, ctx_oth,
            ctx_far, deps,
        )

    def attn_norm(layer, ds, part_own, part_rcv, deps=()):
        own, own_spec = kept[layer][:2]
        return attention_norm_back(
            scalars, layer, layer == 0, ds, part_own, part_rcv, own, own_spec, a_gain, deps
        )

    def y_sum(keep, got):
        return total(keep[1], got[1])

    def z_sums(keep, got, y_got):
        return [total(keep[0, k], got[0, k], y_got[k]) for k in (1, 2, 3)]

    def last_sum(keep, got, y_got, z_got):
        return total(keep[0, 0], got[0, 0], y_got[0], *z_got)

    def z_moved(sums):
        return [to_dp(value, 2 * k) for k, value in zip((1, 2, 3), sums)]

    def small_of(a_small, f_small, g_up_bias):
        return jnp.concatenate([a_small, f_small, g_up_bias.reshape(4, D)])

    if direct:
        dh1, ds1, fsmall1, ub1 = ffn_back(1, cot, own_in)
        ds1_rcv = to_core(ds1)
        fk1, fs1 = ffn_grads(1, cot, own_in, cot, far_in, dh1)
        fg1 = to_core(fs1)
        d_qkv1, part1, part1_oth = attn_back(1, ds1, ds1_rcv, [fk1])
        part1_rcv = to_core(part1_oth)
        fys1 = y_sum(fk1, fg1)
        fy1 = to_dp(fys1, 1)
        g0, asmall1 = attn_norm(1, ds1, part1, part1_rcv, [fys1])
        g0_o = to_chip(g0)
        ak1, as1 = attn_grads(1, ds1, ds1_rcv, d_qkv1, [g0])
        ag1 = to_chip(as1)
        dh0, ds0, fsmall0, ub0 = ffn_back(0, rows5(g0), local, [ak1])
        ds0_rcv = to_core(ds0)
        fzs1 = z_sums(fk1, fg1, fy1)
        fz1 = z_moved(fzs1)
        fk0, fs0 = ffn_grads(0, rows5(g0), local, rows5(g0_o), local, dh0, fzs1)
        fg0 = to_core(fs0)
        ays1 = y_sum(ak1, ag1)
        ay1 = to_dp(ays1, 1)
        d_qkv0, part0, part0_oth = attn_back(0, ds0, ds0_rcv, [fk0, ays1])
        part0_rcv = to_core(part0_oth)
        fys0 = y_sum(fk0, fg0)
        fy0 = to_dp(fys0, 1)
        azs1 = z_sums(ak1, ag1, ay1)
        az1 = z_moved(azs1)
        f1 = last_sum(fk1, fg1, fy1, fz1)
        f1_all = gathered(f1)
        ak0, as0 = attn_grads(0, ds0, ds0_rcv, d_qkv0, [fys0, f1] + azs1)
        ag0 = to_chip(as0)
        *result, asmall0 = attn_norm(0, ds0, part0, part0_rcv, [ak0])
        fz0 = z_moved(z_sums(fk0, fg0, fy0))
        a1_all = gathered(last_sum(ak1, ag1, ay1, az1))
        ay0 = to_dp(y_sum(ak0, ag0), 1)
        az0 = z_moved(z_sums(ak0, ag0, ay0))
        f0_all = gathered(last_sum(fk0, fg0, fy0, fz0))
        a0_all = gathered(last_sum(ak0, ag0, ay0, az0))
        ups, downs, qkvs, outs = unpacked(scalars, f0_all + a0_all + f1_all + a1_all)

        def small_pieces(a_small, f_small, g_up_bias):
            vectors = jnp.concatenate([a_small, f_small]).reshape(6, 8, PART).transpose(1, 0, 2)
            return jnp.concatenate([vectors, g_up_bias.reshape(8, 4, PART)], 1)

        small = jnp.concatenate([small_pieces(asmall0, fsmall0, ub0), small_pieces(asmall1, fsmall1, ub1)], 1)
        small = small + to_core(small)
        small = small + to_chip(small)

        def near(distance):
            return lax.dynamic_index_in_dim(small, replica ^ distance, 0, keepdims=False)

        halves = jnp.stack([near(2 * k + 1) for k in range(4)])
        y_got = to_dp(halves, 1)
        small = near(0) + y_got[0] + sum(to_dp(near(2 * k) + y_got[k], 2 * k) for k in (1, 2, 3))
        small = small.reshape(2, 10, PART)

        def piece(first):
            return small[:, first]

        up_bias_grad = small[:, 6:10].reshape(2, 4 * PART)
    else:
        grads = [None, None]
        smalls = [None, None]
        grad, grad_spec, grad_o, grad_o_spec = cot, own_in, cot, far_in
        for layer in (1, 0):
            dh, ds, f_small, g_up_bias = ffn_back(layer, grad, grad_spec)
            ds_rcv = to_core(ds)
            f_keep, f_send = ffn_grads(layer, grad, grad_spec, grad_o, grad_o_spec, dh)
            d_qkv, part_own, part_oth = attn_back(layer, ds, ds_rcv)
            a_keep, a_send = attn_grads(layer, ds, ds_rcv, d_qkv)
            *result, a_small = attn_norm(layer, ds, part_own, to_core(part_oth))
            if layer == 1:
                grad, grad_spec = rows5(result[0]), local
                grad_o, grad_o_spec = rows5(to_chip(result[0])), local
            smalls[layer] = small_of(a_small, f_small, g_up_bias)
            ordered = []
            for share in (reduced_any(f_keep, f_send, to_core), reduced_any(a_keep, a_send, to_chip)):
                mine, far, near, both = gathered(share)
                here = jnp.stack([jnp.where(chip == 0, mine, far), jnp.where(chip == 0, far, mine)])
                there = jnp.stack([jnp.where(chip == 0, near, both), jnp.where(chip == 0, both, near)])
                pair = jnp.stack([jnp.where(core == 0, here, there), jnp.where(core == 0, there, here)], 1)
                ordered.append(pair.astype(F32))
            f_all, a_all = ordered
            up = f_all[:, :, :, 0:2].transpose(2, 4, 0, 1, 3, 5).reshape(D, FF)
            down = f_all[:, :, :, 2:4].transpose(2, 1, 3, 4, 0, 5).reshape(FF, D)
            q_k = a_all[0].transpose(1, 3, 2, 0, 4).reshape(D, 2 * D)
            v = a_all[1, :, :, 0].transpose(1, 2, 0, 3).reshape(D, D)
            out = a_all[1, :, :, 1].transpose(1, 2, 0, 3).reshape(D, D)
            grads[layer] = [
                lax.psum_scatter(array, "dp", scatter_dimension=0, tiled=True)
                for array in (up, down, jnp.concatenate([q_k, v], 1), out)
            ]
        ups, downs, qkvs, outs = (jnp.stack(pair) for pair in zip(*grads))
        small = lax.psum(jnp.stack(smalls), ("section", "dp"))

        def mine_of(rows):
            width = rows.shape[-1] // replicas
            return lax.dynamic_slice_in_dim(rows, replica * width, width, 1)

        def piece(first):
            return mine_of(small[:, first])

        up_bias_grad = mine_of(small[:, 6:10].reshape(2, FF))
    input_keep, input_send = result

    def placed(keep, send):
        got = to_chip(send).astype(F32)
        return jnp.stack([jnp.where(chip == 0, keep, got), jnp.where(chip == 0, got, keep)])[:, None]

    final_out, input_out = placed(final_keep, final_send), placed(input_keep, input_send)
    return (
        final_out,
        input_out,
        piece(0),
        piece(1),
        qkvs,
        outs,
        piece(2),
        piece(3),
        piece(4),
        ups,
        up_bias_grad,
        downs,
        piece(5),
    )


def solution(mesh):
    split = P(None, "dp", None, None)
    placed = (split, P(None, "dp", None)) + (P(),) * 11 + (split,)
    rows = P(None, "dp", "section", None)
    vector, matrix = P(None, "dp"), P(None, "dp", None)
    return jax.shard_map(
        on_device,
        mesh=mesh,
        in_specs=placed,
        out_specs=(
            rows,
            rows,
            vector,
            vector,
            matrix,
            matrix,
            vector,
            vector,
            vector,
            matrix,
            vector,
            matrix,
            vector,
        ),
        check_vma=False,
    )
```

profile of v0, /device:TPU:0, one launch (start us, length us, event | category | flops | bytes accessed | tf_op | source)
XLA Modules:
  0.0 393.2 jit_solution(16509178563365538544)
XLA Ops:
  3.9 16.0 %shard_map.237 = (bf16[1024,1152]{1,0:T(8,128)(2,1)}, bf16[1024,384]{1,0:T(8,128)(2,1)}, bf16[2,256,384]{2,1,0:T(8,128)(2,1)}, bf16[2,256,384]{2,1,0:T(8,128)(2,1)}, f32[8,1024]{1,0:T(8,128)}) custom-call(s32[4]{0:T(128)} %pad_add_fusion.sc, bf16[2,2,2,256,768]{4,3,2,1,0:T(8,128)(2,1)} %bitcast.166, bf16[2,2,2,256,768]{4,3,2,1,0:T(8,128)(2,1)} %bitcast.167, ...), custom_call_target="tpu_custom_call" | custom-call | flops 4200000000 | bytes 8000000 | tf_op jit(solution)/shard_map/pallas_call | solution.py:71
  24.1 15.3 %shard_map.238 = (bf16[512,768]{1,0:T(8,128)(2,1)}, bf16[512,768]{1,0:T(8,128)(2,1)}, bf16[512,3072]{1,0:T(8,128)(2,1)}, bf16[512,3072]{1,0:T(8,128)(2,1)}, bf16[2,256,768]{2,1,0:T(8,128)(2,1)}) custom-call(s32[4]{0:T(128)} %pad_add_fusion.sc, bf16[2,256,384]{2,1,0:T(8,128)(2,1)} %get-tuple-element.65.refs_0_, bf16[2,256,384]{2,1,0:T(8,128)(2,1)} %copy-done.26, ...), custom_call_target="tpu_custom_call" | custom-call | flops 5400000000 | bytes 20000000 | tf_op jit(solution)/shard_map/pallas_call | solution.py:71
  42.9 15.6 %shard_map.239 = (bf16[1024,1152]{1,0:T(8,128)(2,1)}, bf16[1024,384]{1,0:T(8,128)(2,1)}, bf16[2,256,384]{2,1,0:T(8,128)(2,1)}, bf16[2,256,384]{2,1,0:T(8,128)(2,1)}, f32[8,1024]{1,0:T(8,128)}) custom-call(s32[4]{0:T(128)} %pad_add_fusion.sc, bf16[1,2,1,256,768]{4,3,2,1,0:T(8,128)(2,1)} %bitcast.175, bf16[1,2,1,256,768]{4,3,2,1,0:T(8,128)(2,1)} %bitcast.179, ...), custom_call_target="tpu_custom_call" | custom-call | flops 4200000000 | bytes 8000000 | tf_op jit(solution)/shard_map/pallas_call | solution.py:71
  61.1 15.5 %shard_map.240 = (bf16[512,768]{1,0:T(8,128)(2,1)}, bf16[512,768]{1,0:T(8,128)(2,1)}, bf16[512,3072]{1,0:T(8,128)(2,1)}, bf16[512,3072]{1,0:T(8,128)(2,1)}, f32[...) custom-call(s32[4]{0:T(128)} %pad_add_fusion.sc, bf16[2,256,384]{2,1,0:T(8,128)(2,1)} %get-tuple-element.68.refs_0_, ...), custom_call_target="tpu_custom_call" | custom-call | flops 5400000000 | bytes 20000000 | tf_op jit(solution)/shard_map/pallas_call | solution.py:71
  79.3 12.8 %shard_map.241 = (bf16[512,3072]{1,0:T(8,128)(2,1)}, bf16[2,256,768]{2,1,0:T(8,128)(2,1)}, f32[3,768]{1,0:T(4,128)}, f32[1,3072]{1,0:T(1,128)}) custom-call(s32[4]{0:T(128)} %pad_add_fusion.sc, bf16[2,2,2,256,768]{4,3,2,1,0:T(8,128)(2,1)} %bitcast.172, bf16[512,768]{1,0:T(8,128)(2,1)} %get-tuple-element.72.refs_1_.refs_2_, ...), custom_call_target="tpu_custom_call" | custom-call | flops 4899999744 | bytes 18000000 | tf_op jit(solution)/shard_map/pallas_call | solution.py:71
  92.1 5.5 %collective-permute-done.5.refs_3_ = bf16[512,768]{1,0:T(8,128)(2,1)S(1)} collective-permute-done((bf16[512,768]{1,0:T(8,128)(2,1)}, bf16[512,768]{1,0:T(8,128)(2,1)S(1)}, u32[]{:S(2)}, u32[]{:S(2)}) %collective-permute-start.5) | collective-permute-done | bytes 786464 | tf_op jit(solution)/shard_map/ppermute | solution.py:624
  98.5 21.9 %shard_map.242 = (bf16[2,4,4,96,384]{4,3,2,1,0:T(8,128)(2,1)}, bf16[2,4,4,96,384]{4,3,2,1,0:T(8,128)(2,1)}) custom-call(s32[4]{0:T(128)} %pad_add_fusion.sc, bf16[2,2,2,256,768]{4,3,2,1,0:T(8,128)(2,1)} %bitcast.173, bf16[2,2,2,256,768]{4,3,2,1,0:T(8,128)(2,1)} %bitcast.174, bf16[512,768]{1,0:T(8,128)(2,1)} %get-tuple-element.72.refs_1_.refs_2_, ...), custom_call_target="tpu_custom_call" | custom-call | flops 8600000512 | bytes 22000000 | tf_op jit(solution)/shard_map/pallas_call | solution.py:71
  120.9 4.8 %collective-permute-done.4.refs_1_.refs_6_ = bf16[2,256,768]{2,1,0:T(8,128)(2,1)S(1)} collective-permute-done((bf16[2,256,768]{2,1,0:T(8,128)(2,1)S(1)}, bf16[2,256,768]{2,1,0:T(8,128)(2,1)S(1)}, u32[]{:S(2)}, u32[]{:S(2)}) %collective-permute-start.4) | collective-permute-done | bytes 786464 | tf_op jit(solution)/shard_map/ppermute | solution.py:620
  126.6 23.9 %shard_map.243 = (bf16[1024,1152]{1,0:T(8,128)(2,1)}, f32[2,256,768]{2,1,0:T(8,128)}, bf16[2,256,768]{2,1,0:T(8,128)(2,1)}) custom-call(s32[4]{0:T(128)} %pad_add_fusion.sc, bf16[2,256,768]{2,1,0:T(8,128)(2,1)} %get-tuple-element.74.refs_0_.refs_5_, bf16[2,256,768]{2,1,0:T(8,128)(2,1)} %copy-done.48, bf16[1024,1152]{1,0:T(8,128)(2,1)} %get-tuple-element.75.refs_2_, ...), custom_call_target="tpu_custom_call" | custom-call | flops 8499999744 | bytes 12000000 | tf_op jit(solution)/shard_map/pallas_call | solution.py:71
  155.0 5.0 %shard_map.244 = (bf16[2,256,768]{2,1,0:T(8,128)(2,1)}, f32[3,768]{1,0:T(4,128)}) custom-call(s32[4]{0:T(128)} %pad_add_fusion.sc, bf16[2,256,768]{2,1,0:T(8,128)(2,1)} %get-tuple-element.74.refs_0_.refs_5_, f32[2,256,768]{2,1,0:T(8,128)} %get-tuple-element.81.refs_1_, bf16[2,256,768]{2,1,0:T(8,128)(2,1)} %collective-permute-done.6.refs_2_, ...), custom_call_target="tpu_custom_call" | custom-call | flops 200000000 | bytes 5000000 | tf_op jit(solution)/shard_map/pallas_call | solution.py:71
  161.5 9.1 %shard_map.245 = (bf16[2,4,2,96,384]{4,3,2,1,0:T(8,128)(2,1)}, bf16[2,4,2,96,384]{4,3,2,1,0:T(8,128)(2,1)}) custom-call(s32[4]{0:T(128)} %pad_add_fusion.sc, bf16[1,2,1,256,768]{4,3,2,1,0:T(8,128)(2,1)} %bitcast.178, bf16[1,2,1,256,768]{4,3,2,1,0:T(8,128)(2,1)} %bitcast.180, f32[2,1,768]{2,1,0:T(1,128)} %reshape.185.refs_3_.refs_4_.refs_2_, ...), custom_call_target="tpu_custom_call" | custom-call | flops 2500000000 | bytes 12000000 | tf_op jit(solution)/shard_map/pallas_call | solution.py:71
  171.1 13.6 %shard_map.246 = (bf16[512,3072]{1,0:T(8,128)(2,1)}, bf16[2,256,768]{2,1,0:T(8,128)(2,1)}, f32[3,768]{1,0:T(4,128)}, f32[1,3072]{1,0:T(1,128)}) custom-call(s32[4]{0:T(128)} %pad_add_fusion.sc, bf16[1,2,1,256,768]{4,3,2,1,0:T(8,128)(2,1)} %bitcast.181, bf16[512,768]{1,0:T(8,128)(2,1)} %get-tuple-element.85.refs_1_.refs_2_, ...), custom_call_target="tpu_custom_call" | custom-call | flops 4899999744 | bytes 18000000 | tf_op jit(solution)/shard_map/pallas_call | solution.py:71
  186.0 12.7 %collective-permute-done.10 = bf16[2,256,768]{2,1,0:T(8,128)(2,1)} collective-permute-done((bf16[2,256,768]{2,1,0:T(8,128)(2,1)}, bf16[2,256,768]{2,1,0:T(8,128)(2,1)}, u32[]{:S(2)}, u32[]{:S(2)}) %collective-permute-start.10) | collective-permute-done | bytes 786464 | tf_op jit(solution)/shard_map/ppermute | solution.py:624
  198.7 21.8 %shard_map.247 = (bf16[2,4,4,96,384]{4,3,2,1,0:T(8,128)(2,1)}, bf16[2,4,4,96,384]{4,3,2,1,0:T(8,128)(2,1)}) custom-call(s32[4]{0:T(128)} %pad_add_fusion.sc, bf16[1,2,1,256,768]{4,3,2,1,0:T(8,128)(2,1)} %bitcast.182, bf16[1,2,1,256,768]{4,3,2,1,0:T(8,128)(2,1)} %bitcast.14.refs_1_, bf16[512,768]{1,0:T(8,128)(2,1)} %get-tuple-element.85.refs_1_.refs_2_, ...), custom_call_target="tpu_custom_call" | custom-call | flops 8600000512 | bytes 22000000 | tf_op jit(solution)/shard_map/pallas_call | solution.py:71
  237.0 24.0 %shard_map.248 = (bf16[1024,1152]{1,0:T(8,128)(2,1)}, f32[2,256,768]{2,1,0:T(8,128)}, bf16[2,256,768]{2,1,0:T(8,128)(2,1)}) custom-call(s32[4]{0:T(128)} %pad_add_fusion.sc, bf16[2,256,768]{2,1,0:T(8,128)(2,1)} %get-tuple-element.90.refs_0_.refs_5_, bf16[2,256,768]{2,1,0:T(8,128)(2,1)} %collective-permute-done.9.refs_1_.refs_6_, ...), custom_call_target="tpu_custom_call" | custom-call | flops 8499999744 | bytes 12000000 | tf_op jit(solution)/shard_map/pallas_call | solution.py:71
  269.4 9.1 %shard_map.249 = (bf16[2,4,2,96,384]{4,3,2,1,0:T(8,128)(2,1)}, bf16[2,4,2,96,384]{4,3,2,1,0:T(8,128)(2,1)}) custom-call(s32[4]{0:T(128)} %pad_add_fusion.sc, bf16[2,2,2,256,768]{4,3,2,1,0:T(8,128)(2,1)} %bitcast.169, bf16[2,2,2,256,768]{4,3,2,1,0:T(8,128)(2,1)} %bitcast.170, f32[2,1,768]{2,1,0:T(1,128)} %reshape.185.refs_3_.refs_4_.refs_2_, ...), custom_call_target="tpu_custom_call" | custom-call | flops 2500000000 | bytes 12000000 | tf_op jit(solution)/shard_map/pallas_call | solution.py:71
  281.1 5.2 %shard_map.250 = (f32[256,768]{1,0:T(8,128)}, bf16[256,768]{1,0:T(8,128)(2,1)}, f32[3,768]{1,0:T(4,128)}) custom-call(s32[4]{0:T(128)} %pad_add_fusion.sc, bf16[2,256,768]{2,1,0:T(8,128)(2,1)} %get-tuple-element.90.refs_0_.refs_5_, f32[2,256,768]{2,1,0:T(8,128)} %get-tuple-element.98.refs_1_, bf16[2,256,768]{2,1,0:T(8,128)(2,1)} %copy-done.14, ...), custom_call_target="tpu_custom_call" | custom-call | flops 200000000 | bytes 5000000 | tf_op jit(solution)/shard_map/pallas_call | solution.py:71
  299.4 5.7 %collective-permute-done.47 = bf16[2,96,384]{2,1,0:T(8,128)(2,1)S(1)} collective-permute-done((bf16[2,96,384]{2,1,0:T(8,128)(2,1)S(1)}, bf16[2,96,384]{2,1,0:T(8,128)(2,1)S(1)}, u32[]{:S(2)}, u32[]{:S(2)}) %collective-permute-start.47) | collective-permute-done | bytes 147488 | tf_op jit(solution)/shard_map/ppermute | solution.py:628
  307.3 7.8 %collective-permute-done.23 = f32[8,20,96]{2,1,0:T(8,128)S(1)} collective-permute-done((f32[8,20,96]{2,1,0:T(8,128)S(1)}, f32[8,20,96]{2,1,0:T(8,128)S(1)}, u32[]{:S(2)}, u32[]{:S(2)}) %collective-permute-start.23) | collective-permute-done | bytes 61472 | tf_op jit(solution)/shard_map/ppermute | solution.py:624
  318.5 5.8 %collective-permute-done.24 = f32[4,20,96]{2,1,0:T(8,128)S(1)} collective-permute-done((f32[4,20,96]{2,1,0:T(8,128)S(1)}, f32[4,20,96]{2,1,0:T(8,128)S(1)}, u32[]{:S(2)}, u32[]{:S(2)}) %collective-permute-start.24) | collective-permute-done | bytes 30752 | tf_op jit(solution)/shard_map/ppermute | solution.py:628
  342.9 12.3 %collective-permute-done.30 = bf16[4,96,384]{2,1,0:T(8,128)(2,1)} collective-permute-done((bf16[4,96,384]{2,1,0:T(8,128)(2,1)}, bf16[4,96,384]{2,1,0:T(8,128)(2,1)}, u32[]{:S(2)}, u32[]{:S(2)}) %collective-permute-start.30) | collective-permute-done | bytes 294944 | tf_op jit(solution)/shard_map/ppermute | solution.py:628
  357.2 4.6 %collective-permute-start.38 = (bf16[2,96,384]{2,1,0:T(8,128)(2,1)}, bf16[2,96,384]{2,1,0:T(8,128)(2,1)S(1)}, u32[]{:S(2)}, u32[]{:S(2)}) collective-permute-start(bf16[2,96,384]{2,1,0:T(8,128)(2,1)} %get-tuple-element.151), channel_id=1, source_target_pairs={{0,4},{1,5},{2,6},{3,7},{4,0},{5,1},{6,2},{7,3},{8,12},{9,13},{10,... | collective-permute-start | bytes 442376 | tf_op jit(solution)/shard_map/ppermute | solution.py:628
  365.5 5.8 %collective-permute-done.38 = bf16[2,96,384]{2,1,0:T(8,128)(2,1)S(1)} collective-permute-done((bf16[2,96,384]{2,1,0:T(8,128)(2,1)}, bf16[2,96,384]{2,1,0:T(8,128)(2,1)S(1)}, u32[]{:S(2)}, u32[]{:S(2)}) %collective-permute-start.38) | collective-permute-done | bytes 147488 | tf_op jit(solution)/shard_map/ppermute | solution.py:628
  386.9 6.1 %shard_map.251 = (f32[2,96,3072]{2,1,0:T(8,128)}, f32[2,384,768]{2,1,0:T(8,128)}, f32[2,96,2304]{2,1,0:T(8,128)}, f32[2,96,768]{2,1,0:T(8,128)}) custom-call(s32[4]{0:T(128)} %pad_add_fusion.sc, bf16[4,96,384]{2,1,0:T(8,128)(2,1)} %copy-done.9, bf16[4,96,384]{2,1,0:T(8,128)(2,1)} %copy-done.28, bf16[4,96,384]{2,1,0:T(8,128)(2,1)} %copy-done.30, ...), custom_call_target="tpu_custom_call" | custom-call | flops 1000000 | bytes 11000000 | tf_op jit(solution)/shard_map/pallas_call | solution.py:71
  (238 shorter events, 112.2 us)
Async XLA Ops:
  76.6 21.0 %collective-permute-start.5 = (bf16[512,768]{1,0:T(8,128)(2,1)}, bf16[512,768]{1,0:T(8,128)(2,1)S(1)}, u32[]{:S(2)}, u32[]{:S(2)}) collective-permute-start(bf16[512,768]{1,0:T(8,128)(2,1)} %get-tuple-element.72.refs_1_.refs_2_), channel_id=1, source_target_pairs={{0,16},{16,0},{8,24},{24,8},{1,17},{17,1},{9,25},{25,9},{2,18},{18... | collective-permute-start | bytes 2359304 | tf_op jit(solution)/shard_map/ppermute | solution.py:624
  120.3 30.5 %collective-permute-start.7 = (bf16[2,4,4,96,384]{4,3,2,1,0:T(8,128)(2,1)}, bf16[2,4,4,96,384]{4,3,2,1,0:T(8,128)(2,1)S(1)}, u32[]{:S(2)}, u32[]{:S(2)}) collective-permute-start(bf16[2,4,4,96,384]{4,3,2,1,0:T(8,128)(2,1)} %get-tuple-element.83), channel_id=1, source_target_pairs={{0,8},{8,0},{16,24},{24,16},{1,9},{9,1},{17,25},{25,17},{2,10},{10... | collective-permute-start | bytes 7077896 | tf_op jit(solution)/shard_map/ppermute | solution.py:620
  151.1 33.6 %collective-permute-start.12 = (bf16[4,4,96,384]{3,2,1,0:T(8,128)(2,1)S(1)}, bf16[4,4,96,384]{3,2,1,0:T(8,128)(2,1)S(1)}, u32[]{:S(2)}, u32[]{:S(2)}) collective-permute-start(bf16[4,4,96,384]{3,2,1,0:T(8,128)(2,1)S(1)} %fusion.refs_5_), channel_id=1, source_target_pairs={{0,1},{1,0},{2,3},{3,2},{4,5},{5,4},{6,7},{7,6},{8,9},{9,8},{10,11... | collective-permute-start | bytes 3538952 | tf_op jit(solution)/shard_map/ppermute | solution.py:628
  153.0 33.0 %collective-permute-start.11 = (bf16[512,768]{1,0:T(8,128)(2,1)S(1)}, bf16[512,768]{1,0:T(8,128)(2,1)}, u32[]{:S(2)}, u32[]{:S(2)}) collective-permute-start(bf16[512,768]{1,0:T(8,128)(2,1)S(1)} %copy-done.10), channel_id=1, source_target_pairs={{0,16},{16,0},{8,24},{24,8},{1,17},{17,1},{9,25},{25,9},{2,18},{18... | collective-permute-start | bytes 2359304 | tf_op jit(solution)/shard_map/ppermute | solution.py:624
  154.5 67.9 %collective-permute-start.3 = (bf16[256,768]{1,0:T(8,128)(2,1)}, bf16[256,768]{1,0:T(8,128)(2,1)S(1)}, u32[]{:S(2)}, u32[]{:S(2)}) collective-permute-start(bf16[256,768]{1,0:T(8,128)(2,1)} %get-tuple-element.71), channel_id=1, source_target_pairs={{0,16},{16,0},{8,24},{24,8},{1,17},{17,1},{9,25},{25,9},{2,18},{18... | collective-permute-start | bytes 1179656 | tf_op jit(solution)/shard_map/ppermute | solution.py:624
  160.0 38.7 %collective-permute-start.10 = (bf16[2,256,768]{2,1,0:T(8,128)(2,1)}, bf16[2,256,768]{2,1,0:T(8,128)(2,1)}, u32[]{:S(2)}, u32[]{:S(2)}) collective-permute-start(bf16[2,256,768]{2,1,0:T(8,128)(2,1)} %get-tuple-element.84.refs_10_), channel_id=1, source_target_pairs={{0,16},{16,0},{8,24},{24,8},{1,17},{17,1},{9,25},{25,9},{2,18},{18... | collective-permute-start | bytes 2359304 | tf_op jit(solution)/shard_map/ppermute | solution.py:624
  170.5 64.2 %collective-permute-start.13 = (bf16[2,4,2,96,384]{4,3,2,1,0:T(8,128)(2,1)}, bf16[2,4,2,96,384]{4,3,2,1,0:T(8,128)(2,1)}, u32[]{:S(2)}, u32[]{:S(2)}) collective-permute-start(bf16[2,4,2,96,384]{4,3,2,1,0:T(8,128)(2,1)} %get-tuple-element.97), channel_id=1, source_target_pairs={{0,16},{16,0},{8,24},{24,8},{1,17},{17,1},{9,25},{25,9},{2,18},{18... | collective-permute-start | bytes 3538952 | tf_op jit(solution)/shard_map/ppermute | solution.py:624
  220.5 45.6 %collective-permute-start.16 = (bf16[2,4,4,96,384]{4,3,2,1,0:T(8,128)(2,1)}, bf16[2,4,4,96,384]{4,3,2,1,0:T(8,128)(2,1)}, u32[]{:S(2)}, u32[]{:S(2)}) collective-permute-start(bf16[2,4,4,96,384]{4,3,2,1,0:T(8,128)(2,1)} %get-tuple-element.102), channel_id=1, source_target_pairs={{0,8},{8,0},{16,24},{24,16},{1,9},{9,1},{17,25},{25,17},{2,10},{10... | collective-permute-start | bytes 7077896 | tf_op jit(solution)/shard_map/ppermute | solution.py:620
  220.6 15.6 %collective-permute-start.9 = (bf16[2,256,768]{2,1,0:T(8,128)(2,1)S(1)}, bf16[2,256,768]{2,1,0:T(8,128)(2,1)}, u32[]{:S(2)}, u32[]{:S(2)}) collective-permute-start(bf16[2,256,768]{2,1,0:T(8,128)(2,1)S(1)} %copy-done.4), channel_id=1, source_target_pairs={{0,8},{8,0},{16,24},{24,16},{1,9},{9,1},{17,25},{25,17},{2,10},{10... | collective-permute-start | bytes 2359304 | tf_op jit(solution)/shard_map/ppermute | solution.py:620
  230.6 30.4 %collective-permute-start.17 = (bf16[4,96,384]{2,1,0:T(8,128)(2,1)}, bf16[4,96,384]{2,1,0:T(8,128)(2,1)S(1)}, u32[]{:S(2)}, u32[]{:S(2)}) collective-permute-start(bf16[4,96,384]{2,1,0:T(8,128)(2,1)} %get-tuple-element.148.refs_11_), channel_id=1, source_target_pairs={{0,2},{1,3},{2,0},{3,1},{4,6},{5,7},{6,4},{7,5},{8,10},{9,11},{10,... | collective-permute-start | bytes 884744 | tf_op jit(solution)/shard_map/ppermute | solution.py:628
  232.1 28.9 %collective-permute-start.18 = (bf16[4,96,384]{2,1,0:T(8,128)(2,1)}, bf16[4,96,384]{2,1,0:T(8,128)(2,1)S(1)}, u32[]{:S(2)}, u32[]{:S(2)}) collective-permute-start(bf16[4,96,384]{2,1,0:T(8,128)(2,1)} %get-tuple-element.147.refs_12_), channel_id=1, source_target_pairs={{0,4},{1,5},{2,6},{3,7},{4,0},{5,1},{6,2},{7,3},{8,12},{9,13},{10,... | collective-permute-start | bytes 884744 | tf_op jit(solution)/shard_map/ppermute | solution.py:628
  234.7 26.8 %collective-permute-start.19 = (bf16[4,96,384]{2,1,0:T(8,128)(2,1)}, bf16[4,96,384]{2,1,0:T(8,128)(2,1)S(1)}, u32[]{:S(2)}, u32[]{:S(2)}) collective-permute-start(bf16[4,96,384]{2,1,0:T(8,128)(2,1)} %get-tuple-element.146.refs_13_), channel_id=1, source_target_pairs={{0,6},{1,7},{2,4},{3,5},{4,2},{5,3},{6,0},{7,1},{8,14},{9,15},{10,... | collective-permute-start | bytes 884744 | tf_op jit(solution)/shard_map/ppermute | solution.py:628
  236.2 27.7 %collective-permute-start.20 = (bf16[4,2,96,384]{3,2,1,0:T(8,128)(2,1)S(1)}, bf16[4,2,96,384]{3,2,1,0:T(8,128)(2,1)S(1)}, u32[]{:S(2)}, u32[]{:S(2)}) collective-permute-start(bf16[4,2,96,384]{3,2,1,0:T(8,128)(2,1)S(1)} %fusion.6.refs_11_), channel_id=1, source_target_pairs={{0,1},{1,0},{2,3},{3,2},{4,5},{5,4},{6,7},{7,6},{8,9},{9,8},{10,11... | collective-permute-start | bytes 1769480 | tf_op jit(solution)/shard_map/ppermute | solution.py:628
  261.1 19.1 %collective-permute-start.14 = (bf16[2,256,768]{2,1,0:T(8,128)(2,1)}, bf16[2,256,768]{2,1,0:T(8,128)(2,1)S(1)}, u32[]{:S(2)}, u32[]{:S(2)}) collective-permute-start(bf16[2,256,768]{2,1,0:T(8,128)(2,1)} %get-tuple-element.99), channel_id=1, source_target_pairs={{0,8},{8,0},{16,24},{24,16},{1,9},{9,1},{17,25},{25,17},{2,10},{10... | collective-permute-start | bytes 2359304 | tf_op jit(solution)/shard_map/ppermute | solution.py:620
  278.5 38.0 %collective-permute-start.35 = (bf16[2,4,2,96,384]{4,3,2,1,0:T(8,128)(2,1)}, bf16[2,4,2,96,384]{4,3,2,1,0:T(8,128)(2,1)}, u32[]{:S(2)}, u32[]{:S(2)}) collective-permute-start(bf16[2,4,2,96,384]{4,3,2,1,0:T(8,128)(2,1)} %get-tuple-element.112), channel_id=1, source_target_pairs={{0,16},{16,0},{8,24},{24,8},{1,17},{17,1},{9,25},{25,9},{2,18},{18... | collective-permute-start | bytes 3538952 | tf_op jit(solution)/shard_map/ppermute | solution.py:624
  290.7 14.5 %collective-permute-start.47 = (bf16[2,96,384]{2,1,0:T(8,128)(2,1)S(1)}, bf16[2,96,384]{2,1,0:T(8,128)(2,1)S(1)}, u32[]{:S(2)}, u32[]{:S(2)}) collective-permute-start(bf16[2,96,384]{2,1,0:T(8,128)(2,1)S(1)} %copy-done.21), channel_id=1, source_target_pairs={{0,4},{1,5},{2,6},{3,7},{4,0},{5,1},{6,2},{7,3},{8,12},{9,13},{10,... | collective-permute-start | bytes 442376 | tf_op jit(solution)/shard_map/ppermute | solution.py:628
  294.4 34.2 %collective-permute-start.28 = (bf16[4,4,96,384]{3,2,1,0:T(8,128)(2,1)S(1)}, bf16[4,4,96,384]{3,2,1,0:T(8,128)(2,1)S(1)}, u32[]{:S(2)}, u32[]{:S(2)}) collective-permute-start(bf16[4,4,96,384]{3,2,1,0:T(8,128)(2,1)S(1)} %copy-done.2), channel_id=1, source_target_pairs={{0,1},{1,0},{2,3},{3,2},{4,5},{5,4},{6,7},{7,6},{8,9},{9,8},{10,11... | collective-permute-start | bytes 3538952 | tf_op jit(solution)/shard_map/ppermute | solution.py:628
  299.0 58.2 %collective-permute-start.43 = (bf16[4,96,384]{2,1,0:T(8,128)(2,1)}, bf16[4,96,384]{2,1,0:T(8,128)(2,1)}, u32[]{:S(2)}, u32[]{:S(2)}) collective-permute-start(bf16[4,96,384]{2,1,0:T(8,128)(2,1)} %fusion.18.refs_11_.refs_8_), channel_id=1, source_target_pairs={{0,16},{16,0},{8,24},{24,8},{1,17},{17,1},{9,25},{25,9},{2,18},{18... | collective-permute-start | bytes 884744 | tf_op jit(solution)/shard_map/ppermute | solution.py:624
  317.7 18.6 %collective-permute-start.36 = (bf16[4,2,96,384]{3,2,1,0:T(8,128)(2,1)S(1)}, bf16[4,2,96,384]{3,2,1,0:T(8,128)(2,1)S(1)}, u32[]{:S(2)}, u32[]{:S(2)}) collective-permute-start(bf16[4,2,96,384]{3,2,1,0:T(8,128)(2,1)S(1)} %fusion.7), channel_id=1, source_target_pairs={{0,1},{1,0},{2,3},{3,2},{4,5},{5,4},{6,7},{7,6},{8,9},{9,8},{10,11... | collective-permute-start | bytes 1769480 | tf_op jit(solution)/shard_map/ppermute | solution.py:628
  331.7 23.5 %collective-permute-start.30 = (bf16[4,96,384]{2,1,0:T(8,128)(2,1)}, bf16[4,96,384]{2,1,0:T(8,128)(2,1)}, u32[]{:S(2)}, u32[]{:S(2)}) collective-permute-start(bf16[4,96,384]{2,1,0:T(8,128)(2,1)} %get-tuple-element.145), channel_id=1, source_target_pairs={{0,4},{1,5},{2,6},{3,7},{4,0},{5,1},{6,2},{7,3},{8,12},{9,13},{10,... | collective-permute-start | bytes 884744 | tf_op jit(solution)/shard_map/ppermute | solution.py:628
  335.5 19.7 %collective-permute-start.31 = (bf16[4,96,384]{2,1,0:T(8,128)(2,1)}, bf16[4,96,384]{2,1,0:T(8,128)(2,1)}, u32[]{:S(2)}, u32[]{:S(2)}) collective-permute-start(bf16[4,96,384]{2,1,0:T(8,128)(2,1)} %get-tuple-element.144), channel_id=1, source_target_pairs={{0,6},{1,7},{2,4},{3,5},{4,2},{5,3},{6,0},{7,1},{8,14},{9,15},{10,... | collective-permute-start | bytes 884744 | tf_op jit(solution)/shard_map/ppermute | solution.py:628
  336.3 37.7 %collective-permute-start.44 = (bf16[4,96,384]{2,1,0:T(8,128)(2,1)}, bf16[4,96,384]{2,1,0:T(8,128)(2,1)}, u32[]{:S(2)}, u32[]{:S(2)}) collective-permute-start(bf16[4,96,384]{2,1,0:T(8,128)(2,1)} %fusion.18.refs_11_.refs_8_), channel_id=1, source_target_pairs={{0,8},{8,0},{16,24},{24,16},{1,9},{9,1},{17,25},{25,17},{2,10},{10... | collective-permute-start | bytes 884744 | tf_op jit(solution)/shard_map/ppermute | solution.py:620
  342.5 35.7 %collective-permute-start.21 = (bf16[256,768]{1,0:T(8,128)(2,1)}, bf16[256,768]{1,0:T(8,128)(2,1)}, u32[]{:S(2)}, u32[]{:S(2)}) collective-permute-start(bf16[256,768]{1,0:T(8,128)(2,1)} %get-tuple-element.105), channel_id=1, source_target_pairs={{0,16},{16,0},{8,24},{24,8},{1,17},{17,1},{9,25},{25,9},{2,18},{18... | collective-permute-start | bytes 1179656 | tf_op jit(solution)/shard_map/ppermute | solution.py:624
  356.8 21.0 %collective-permute-start.32 = (bf16[4,96,384]{2,1,0:T(8,128)(2,1)S(1)}, bf16[4,96,384]{2,1,0:T(8,128)(2,1)S(1)}, u32[]{:S(2)}, u32[]{:S(2)}) collective-permute-start(bf16[4,96,384]{2,1,0:T(8,128)(2,1)S(1)} %fusion.14.refs_0_), channel_id=1, source_target_pairs={{0,16},{16,0},{8,24},{24,8},{1,17},{17,1},{9,25},{25,9},{2,18},{18... | collective-permute-start | bytes 884744 | tf_op jit(solution)/shard_map/ppermute | solution.py:624
  (77 other events, 659.6 us)
where the time goes:
time: 399 us; the launch traced here: 393 us
  Pallas kernels  215 us (54%)
  waiting for transfers between devices  77.3 us (19%)
  starting transfers between devices  47.1 us (12%)
  other arithmetic  31.1 us (8%)
  local copies, waits for them, and re-layouts  21.7 us (5%)
    pallas_call x15, Pallas kernels, call(): return lambda *args: kernel(*args, *deps)  215 us
    ppermute x20, waiting for transfers between devices, to_dp(): return lax.ppermute(value, 'dp', [(i, i ^ distance) for i in range(8)])  36.5 us
    ppermute x12, waiting for transfers between devices, to_chip(): return lax.ppermute(value, 'section', [(0, 2), (2, 0), (1, 3), (3, 1)])  31.7 us
    ppermute x20, starting transfers between devices, to_dp(): return lax.ppermute(value, 'dp', [(i, i ^ distance) for i in range(8)])  29.7 us
    convert_element_type x12, other arithmetic, total(): return out.astype(BF)  20 us
    ppermute x12, starting transfers between devices, to_chip(): return lax.ppermute(value, 'section', [(0, 2), (2, 0), (1, 3), (3, 1)])  13.2 us
    unnamed x98, local copies, waits for them, and re-layouts  10 us
    ppermute x20, waiting for transfers between devices, to_core(): return lax.ppermute(value, 'section', [(0, 1), (1, 0), (2, 3), (3, 2)])  9.07 us
  transfers between devices with their start and end apart: 52, of which 14 were waited for; matrix products, arithmetic and copies ran while one was open for 10% of the time, Pallas kernels for 32%

commit v1 on v0

--- a/solution.py
+++ b/solution.py
@@ -47,7 +47,7 @@
     return (unit * gain + shift).astype(BF)
 
 
-def call(body, grid, in_specs, out_specs, out_shape, scratch, cost=None, deps=()):
+def call(body, grid, in_specs, out_specs, out_shape, scratch, cost, deps=()):
     count = len(in_specs)
 
     def with_deps(sc, *refs):
@@ -63,16 +63,22 @@
             scratch_shapes=scratch,
         ),
         out_shape=out_shape,
-        compiler_params=pltpu.CompilerParams(vmem_limit_bytes=56 * 1024 * 1024),
-        cost_estimate=None
-        if cost is None
-        else pl.CostEstimate(flops=int(cost[0]), bytes_accessed=int(cost[1]), transcendentals=0),
+        compiler_params=pltpu.CompilerParams(vmem_limit_bytes=32 * 1024 * 1024),
+        cost_estimate=pl.CostEstimate(flops=int(5 * cost[0]), bytes_accessed=int(5 * cost[1]), transcendentals=0),
     )
     return lambda *args: kernel(*args, *deps)
 
 
 def shape(dims, dtype):
     return jax.ShapeDtypeStruct(dims, dtype)
+
+
+def stored(dims, dtype):
+    return pltpu.MemorySpace.HBM(dims, dtype)
+
+
+def from_hbm(array):
+    return pltpu.with_memory_space_constraint(array, pltpu.MemorySpace.HBM)
 
 
 def whole(dims):
@@ -168,8 +174,8 @@
             whole((8, LENGTH)),
         ],
         [
-            shape((LENGTH, 3 * HALF), BF),
-            shape((LENGTH, HALF), BF),
+            stored((LENGTH, 3 * HALF), BF),
+            stored((LENGTH, HALF), BF),
             shape((2, BLOCK, HALF), BF),
             shape((2, BLOCK, HALF), BF),
             shape((8, LENGTH), F32),
@@ -180,7 +186,7 @@
             pltpu.VMEM((LENGTH, PAIR), F32),
         ],
         (1.8e9 + 2.4e9, 8e6),
-    )(scalars, own, other, episodes, gain, shift, w_qkv, w_qkv, w_qkv)
+    )(scalars, own, other, episodes, gain, shift, *[from_hbm(w_qkv)] * 3)
 
 
 def gelu_parts(u):
@@ -231,7 +237,7 @@
             s3[...] = acc[...].reshape(2, BLOCK, D).astype(BF)
 
 
-def ffn_forward(scalars, layer, last, ctx_own, ctx_rcv, own, own_spec, weights):
+def ffn_forward(scalars, layer, last, ctx_own, ctx_rcv, own, own_spec, weights, dep):
     w_out, b_out, gain, shift, w_up, b_up, w_down, b_down = weights
     vector = at_layer((1, 1, D), layer)
     out_specs = [
@@ -240,7 +246,7 @@
         pl.BlockSpec((ROWS, FT), lambda i, sc: (0, i)),
         pl.BlockSpec((ROWS, FT), lambda i, sc: (0, i)),
     ]
-    out_shape = [shape((ROWS, D), BF), shape((ROWS, D), BF), shape((ROWS, FF), BF), shape((ROWS, FF), BF)]
+    out_shape = [shape((ROWS, D), BF), shape((ROWS, D), BF), stored((ROWS, FF), BF), stored((ROWS, FF), BF)]
     if last:
         out_specs += [whole((BLOCK, D)), whole((BLOCK, D))]
         out_shape += [shape((BLOCK, D), F32), shape((BLOCK, D), BF)]
@@ -267,7 +273,8 @@
         out_shape,
         [pltpu.VMEM((ROWS, D), BF), pltpu.VMEM((ROWS, D), F32)],
         (5.4e9, 20e6),
-    )(scalars, ctx_own, ctx_rcv, own, w_out, b_out, gain, shift, w_up, b_up, w_down, b_down)
+        () if dep is None else (dep,),
+    )(scalars, ctx_own, ctx_rcv, own, from_hbm(w_out), b_out, gain, shift, from_hbm(w_up), b_up, from_hbm(w_down), b_down)
 
 
 def norm_back(d_normed, rows, gain):
@@ -279,15 +286,20 @@
     return d_rows, jnp.sum(d_normed * unit, 0, keepdims=True), jnp.sum(d_normed, 0, keepdims=True)
 
 
-def attn_norm_body(last, sc, grad, part, part_rcv, own, gain, *outs):
+def small_rows(*vectors):
+    return jnp.concatenate(vectors + (jnp.zeros((8 - len(vectors), D), F32),))
+
+
+def attn_norm_body(last, sc, grad, part, part_rcv, own, gain, *rest):
+    before, outs = rest[:3] if last else (), rest[3:] if last else rest
     grad_rows = grad[...].reshape(ROWS, D).astype(F32)
     d_normed = part[...].reshape(ROWS, D) + part_rcv[...].reshape(ROWS, D).astype(F32)
     d_rows, g_gain, g_shift = norm_back(d_normed, own[0, :, 0].reshape(ROWS, D).astype(F32), gain[0])
     total = grad_rows + d_rows
     small = outs[-1]
-    small[0:1] = g_gain
-    small[1:2] = g_shift
-    small[2:3] = jnp.sum(grad_rows, 0, keepdims=True)
+    small[0:8] = small_rows(g_gain, g_shift, jnp.sum(grad_rows, 0, keepdims=True))
+    for j, ref in enumerate(before):
+        small[8 * (j + 1) : 8 * (j + 2)] = ref[...]
     if last:
         keep, send = outs[0:2]
         keep[...] = jnp.where(sc[X] == 0, total[0:BLOCK], total[BLOCK:ROWS])
@@ -296,36 +308,38 @@
         outs[0][...] = total.astype(BF).reshape(2, BLOCK, D)
 
 
-def attention_norm_back(scalars, layer, last, grad, part, part_rcv, own, own_spec, gain, deps=()):
+def attention_norm_back(scalars, layer, grad, part, part_rcv, own, own_spec, gain, smalls=(), deps=()):
     block = whole((2, BLOCK, D))
+    last = bool(smalls)
     if last:
         out_specs = [whole((BLOCK, D)), whole((BLOCK, D))]
         out_shape = [shape((BLOCK, D), F32), shape((BLOCK, D), BF)]
     else:
         out_specs, out_shape = [block], [shape((2, BLOCK, D), BF)]
+    rows = 8 * (1 + len(smalls))
     return call(
         partial(attn_norm_body, last),
         (1,),
-        [block, block, block, own_spec, at_layer((1, 1, D), layer)],
-        out_specs + [whole((3, D))],
-        out_shape + [shape((3, D), F32)],
+        [block, block, block, own_spec, at_layer((1, 1, D), layer)] + [whole((8, D))] * len(smalls),
+        out_specs + [whole((rows, D))],
+        out_shape + [shape((rows, D), F32)],
         [],
         (2e8, 5e6),
         deps,
-    )(scalars, grad, part, part_rcv, own, gain)
+    )(scalars, grad, part, part_rcv, own, gain, *smalls)
 
 
 BT = 768
 
 
-def ffn_back_body(sc, grad, s2, gain, w_up, w_down, slope, dh, ds, small, bias, acc):
+def ffn_back_body(sc, grad, s2, gain, w_up, w_down, slope, dh, ds, small, acc):
     t = pl.program_id(0)
     low = grad[0, :, 0].reshape(ROWS, D)
     d_act = dot_nt(low, w_down[0])
     d_hidden = d_act * slope[...].astype(F32)
     d_low = d_hidden.astype(BF)
     dh[...] = d_low
-    bias[...] = jnp.sum(d_low.astype(F32), 0, keepdims=True)
+    small[pl.ds(4 + t, 1)] = jnp.sum(d_low.astype(F32), 0, keepdims=True)
     part = dot_nt(d_low, w_up[0])
 
     @pl.when(t == 0)
@@ -341,9 +355,7 @@
         rows = low.astype(F32)
         d_rows, g_gain, g_shift = norm_back(acc[...], s2[...].astype(F32), gain[0])
         ds[...] = (rows + d_rows).astype(BF).reshape(2, BLOCK, D)
-        small[0:1] = g_gain
-        small[1:2] = g_shift
-        small[2:3] = jnp.sum(rows, 0, keepdims=True)
+        small[0:4] = small_rows(g_gain, g_shift, jnp.sum(rows, 0, keepdims=True))[0:4]
 
 
 def ffn_backward(scalars, layer, grad, grad_spec, s2, slope, weights, deps=()):
@@ -362,14 +374,13 @@
         [
             pl.BlockSpec((ROWS, BT), lambda i, sc: (0, i)),
             whole((2, BLOCK, D)),
-            whole((3, D)),
-            pl.BlockSpec((1, BT), lambda i, sc: (0, i)),
+            whole((8, D)),
         ],
-        [shape((ROWS, FF), BF), shape((2, BLOCK, D), BF), shape((3, D), F32), shape((1, FF), F32)],
+        [stored((ROWS, FF), BF), shape((2, BLOCK, D), BF), shape((8, D), F32)],
         [pltpu.VMEM((ROWS, D), F32)],
         (4.9e9, 18e6),
         deps,
-    )(scalars, grad, s2, gain, w_up, w_down, slope)
+    )(scalars, grad, s2, gain, from_hbm(w_up), from_hbm(w_down), from_hbm(slope))
 
 
 def place(sc, piece):
@@ -446,7 +457,7 @@
             pl.BlockSpec((1, BT, D), lambda i, sc: (layer, ffn_tile(jnp.minimum(i, 1), sc), 0)),
         ],
         [whole(packed), whole(packed)],
-        [shape(packed, BF), shape(packed, BF)],
+        [stored(packed, BF), shape(packed, BF)],
         [
             pltpu.VMEM((D, ROWS), BF),
             pltpu.VMEM((ROWS, D), BF),
@@ -456,7 +467,7 @@
         ],
         (8.6e9, 22e6),
         deps,
-    )(scalars, grad, grad_o, s2, s2_o, gain, shift, act, dh, w_up, b_up, w_down)
+    )(scalars, grad, grad_o, s2, s2_o, gain, shift, from_hbm(act), from_hbm(dh), from_hbm(w_up), b_up, from_hbm(w_down))
 
 
 def attn_back_body(
@@ -555,11 +566,11 @@
         ],
         (2.5e9 + 6e9, 12e6),
         deps,
-    )(scalars, gr_own, gr_rcv, qkv, ctx, lse, episodes, w_out, w_qkv, w_qkv, w_qkv)
+    )(scalars, gr_own, gr_rcv, from_hbm(qkv), from_hbm(ctx), lse, episodes, from_hbm(w_out), *[from_hbm(w_qkv)] * 3)
 
 
 def attn_weight_body(
-    sc, own, other, gain, shift, d_qkv, gr_own, gr_rcv, ctx_full, ctx_oth, ctx_rcv, keep, send, n_t, late
+    z_first, sc, own, other, gain, shift, d_qkv, gr_own, gr_rcv, ctx_full, ctx_oth, ctx_rcv, keep, send, z_keep, z_send, n_t
 ):
     core, x = sc[C], sc[X]
     own, other = own.at[0, :, 0], other.at[0, :, 0]
@@ -571,30 +582,49 @@
         rows = ref[...].reshape(ROWS, D)
         return jnp.where(core == 0, rows[:, 0:HALF], rows[:, HALF:D]).T
 
+    def grad(j):
+        return dot(n_t[...], d_qkv[:, j * HALF : (j + 1) * HALF]).astype(BF)
+
+    first, second = grad(0), grad(2)
+    mine, yours = jnp.where(x == 0, first, second), jnp.where(x == 0, second, first)
+    for piece in range(8):
+        py, pz = place(sc, piece)
+        keep[py, pz] = mine[piece * PART : (piece + 1) * PART]
+        send[py, pz] = yours[piece * PART : (piece + 1) * PART]
+
     a, b = ctx_oth[...].reshape(ROWS, HALF), ctx_rcv[...].reshape(ROWS, HALF)
     far = jnp.concatenate([jnp.where(core == 0, a, b), jnp.where(core == 0, b, a)], 1)
     g_out = (dot(columns(gr_own), ctx_full[...]) + dot(columns(gr_rcv), far)).astype(BF).T
-
-    def grad(j):
-        if j == 3:
-            return g_out
-        return dot(n_t[...], d_qkv[:, j * HALF : (j + 1) * HALF]).astype(BF)
-
-    for j in range(2):
-        first, second = grad(j), grad(j + 2)
-        mine, yours = jnp.where(x == 0, first, second), jnp.where(x == 0, second, first)
+    for j, rows in enumerate((grad(1), g_out)):
         for piece in range(8):
             py, pz = place(sc, piece)
-            keep[py, pz, j] = mine[piece * PART : (piece + 1) * PART]
-            send[py, pz, j] = yours[piece * PART : (piece + 1) * PART]
+            value = rows[piece * PART : (piece + 1) * PART]
+
+            far = pz % 2 if z_first else py
+
+            @pl.when(far == 0)
+            def _():
+                if z_first:
+                    z_keep[pz // 2, py, j] = value
+                else:
+                    z_keep[pz, j] = value
+
+            @pl.when(far == 1)
+            def _():
+                if z_first:
+                    z_send[pz // 2, py, j] = value
+                else:
+                    z_send[pz, j] = value
 
 
 def attention_weights(
-    scalars, layer, own, own_spec, other, other_spec, gain, shift, d_qkv, gr_own, gr_rcv, ctx_full, ctx_oth, ctx_rcv, deps=()):
-    packed = (2, 4, 2, PART, HALF)
+    scalars, layer, own, own_spec, other, other_spec, gain, shift, d_qkv, gr_own, gr_rcv, ctx_full, ctx_oth, ctx_rcv, deps=()
+):
+    z_first = layer == 1
+    packed, z_packed = (2, 4, PART, HALF), ((2, 2) if z_first else (4,)) + (2, PART, HALF)
     block = whole((2, BLOCK, D))
     return call(
-        attn_weight_body,
+        partial(attn_weight_body, z_first),
         (1,),
         [
             own_spec,
@@ -608,9 +638,9 @@
             whole((2, BLOCK, HALF)),
             whole((2, BLOCK, HALF)),
         ],
-        [whole(packed), whole(packed)],
-        [shape(packed, BF), shape(packed, BF)],
-        [pltpu.VMEM((D, LENGTH), BF), pltpu.VMEM((8, PAIR), F32)],
+        [whole(packed), whole(packed), whole(z_packed), whole(z_packed)],
+        [stored(packed, BF), shape(packed, BF), stored(z_packed, BF), shape(z_packed, BF)],
+        [pltpu.VMEM((D, LENGTH), BF)],
         (2.5e9, 12e6),
         deps,
     )(scalars, own, other, gain, shift, d_qkv, gr_own, gr_rcv, ctx_full, ctx_oth, ctx_rcv)
@@ -635,10 +665,46 @@
     return out.astype(BF)
 
 
-def reduced_any(keep, send, first):
-    both = total(keep, first(send))
-    count = both.shape[2]
-    return jnp.moveaxis(both, 0, 1).reshape(8, count, PART, HALF)
+def combined(scalars, outputs, deps=(), pinned=()):
+    terms, dims, dtypes = [], [], []
+    for pieces in outputs:
+        first = pieces[0][0]
+        rest = first[0].shape[len(first) - 1 :]
+        dims.append(((len(pieces),) if len(pieces) > 1 else ()) + rest)
+        dtypes.append(first[0].dtype)
+        terms += [term for piece in pieces for term in piece]
+
+    def spec(term):
+        array, *index = term
+        rest = array.shape[len(index) :]
+        return pl.BlockSpec((None,) * len(index) + rest, lambda i, sc: (*index, *(0 for _ in rest)))
+
+    def body(sc, *refs):
+        given = iter(refs[: len(terms)])
+        for out, pieces in zip(refs[len(terms) :], outputs):
+            for n, piece in enumerate(pieces):
+                value = next(given)[...].astype(F32)
+                for _ in piece[1:]:
+                    value = value + next(given)[...].astype(F32)
+                if len(pieces) > 1:
+                    out[n] = value.astype(out.dtype)
+                else:
+                    out[...] = value.astype(out.dtype)
+
+    return call(
+        body,
+        (1,),
+        [spec(term) for term in terms],
+        [whole(d) for d in dims],
+        [shape(d, t) for d, t in zip(dims, dtypes)],
+        [],
+        (1e10, 1e7),
+        deps,
+    )(scalars, *[from_hbm(term[0]) if any(term[0] is a for a in pinned) else term[0] for term in terms])
+
+
+def in_dp_order(both):
+    return jnp.moveaxis(both, 0, 1).reshape((8,) + both.shape[2:])
 
 
 def gathered(share):
@@ -647,39 +713,53 @@
 
 
 def unpack_body(sc, *refs):
-    shares, (up, down, qkv, out) = refs[:16], refs[16:]
+    (final_keep, final_got, input_keep, input_got, small), shares, outs = refs[:5], refs[5:25], refs[25:]
+    final, inputs, up, down, qkv, out, a_gain, a_shift, b_out, f_gain, f_shift, b_down, b_up = outs
+    x = sc[X]
+    for ref, mine, got in ((final, final_keep, final_got), (inputs, input_keep, input_got)):
+        ref[x, 0] = mine[...]
+        ref[1 - x, 0] = got[...].astype(F32)
     for layer in range(2):
+        ffn, qv, ko = shares[10 * layer : 10 * layer + 4], shares[10 * layer + 4 : 10 * layer + 8], shares[10 * layer + 8 : 10 * layer + 10]
         for n in range(4):
             x, core = sc[X] ^ (n % 2), sc[C] ^ (n // 2)
-            ffn, attn = shares[layer * 8 + n], shares[layer * 8 + 4 + n]
             for j in range(2):
                 at = pl.multiple_of(x * 4 * HALF + core * 2 * HALF + j * HALF, PAIR)
-                up[layer, :, pl.ds(at, HALF)] = ffn[j].astype(F32)
+                up[layer, :, pl.ds(at, HALF)] = ffn[n][j].astype(F32)
                 rows = pl.ds(pl.multiple_of(core * 2 * PART + j * PART, 8), PART)
-                down[layer, rows, pl.ds(pl.multiple_of(x * HALF, PAIR), HALF)] = ffn[2 + j].astype(F32)
-            side = pl.multiple_of(core * HALF, PAIR)
-            qkv[layer, :, pl.ds(pl.multiple_of(x * 2 * D + side, PAIR), HALF)] = attn[0].astype(F32)
-
-            @pl.when(x == 0)
-            def _():
-                qkv[layer, :, pl.ds(pl.multiple_of(D + side, PAIR), HALF)] = attn[1].astype(F32)
-
-            @pl.when(x == 1)
-            def _():
-                out[layer, :, pl.ds(side, HALF)] = attn[1].astype(F32)
-
-
-def unpacked(scalars, shares):
-    dims = ((2, PART, FF), (2, 4 * PART, D), (2, PART, 3 * D), (2, PART, D))
+                down[layer, rows, pl.ds(pl.multiple_of(x * HALF, PAIR), HALF)] = ffn[n][2 + j].astype(F32)
+            qkv[layer, :, pl.ds(pl.multiple_of(x * 2 * D + core * HALF, PAIR), HALF)] = qv[n][...].astype(F32)
+        for n in range(2):
+            side = pl.multiple_of((sc[C] ^ n) * HALF, PAIR)
+            qkv[layer, :, pl.ds(pl.multiple_of(D + side, PAIR), HALF)] = ko[n][0].astype(F32)
+            out[layer, :, pl.ds(side, HALF)] = ko[n][1].astype(F32)
+    piece = 2 * sc[Z] + sc[Y]
+    mine = jnp.zeros((32, PART), F32)
+    for d in range(8):
+        mine = jnp.where(piece == d, small[:, d * PART : (d + 1) * PART], mine)
+    for layer in range(2):
+        for j, (a_ref, f_ref) in enumerate(((a_gain, f_gain), (a_shift, f_shift), (b_out, b_down))):
+            a_ref[layer : layer + 1] = mine[8 * layer + j : 8 * layer + j + 1]
+            f_ref[layer : layer + 1] = mine[16 + 8 * layer + j : 16 + 8 * layer + j + 1]
+        row = jnp.zeros((1, 4 * PART), F32)
+        for d in range(8):
+            at = 16 + 8 * layer + 4 + d // 2
+            row = jnp.where(piece == d, small[at : at + 1, (d % 2) * HALF : (d % 2 + 1) * HALF], row)
+        b_up[layer : layer + 1] = row
+
+
+def unpacked(scalars, rows, small, shares):
+    moved = ((2, 1, BLOCK, D),) * 2
+    dims = ((2, PART, FF), (2, 4 * PART, D), (2, PART, 3 * D), (2, PART, D)) + ((2, PART),) * 6 + ((2, 4 * PART),)
     return call(
         unpack_body,
         (1,),
-        [whole(share.shape) for share in shares],
-        [whole(d) for d in dims],
-        [shape(d, F32) for d in dims],
+        [whole((BLOCK, D))] * 4 + [whole((32, D))] + [whole(share.shape) for share in shares],
+        [whole(d) for d in moved + dims],
+        [shape(d, F32) for d in moved + dims],
         [],
         (1e6, 11e6),
-    )(scalars, *shares)
+    )(scalars, *rows, small, *shares)
 
 
 def on_device(
@@ -744,6 +824,7 @@
             own,
             own_spec,
             (out_weight, b_out, f_gain, f_shift, up_weight, b_up, down_weight, b_down),
+            None if layer == 0 else kept[0][7],
         )
         s2_o = to_chip(s2)
         kept.append((own, own_spec, other, other_spec, qkv, ctx, ctx_oth, ctx_far, ctx_full, lse, s2, s2_o, act, slope))
@@ -777,151 +858,189 @@
             ctx_far, deps,
         )
 
-    def attn_norm(layer, ds, part_own, part_rcv, deps=()):
+    def attn_norm(layer, ds, part_own, part_rcv, smalls=(), deps=()):
         own, own_spec = kept[layer][:2]
-        return attention_norm_back(
-            scalars, layer, layer == 0, ds, part_own, part_rcv, own, own_spec, a_gain, deps
-        )
-
-    def y_sum(keep, got):
-        return total(keep[1], got[1])
-
-    def z_sums(keep, got, y_got):
-        return [total(keep[0, k], got[0, k], y_got[k]) for k in (1, 2, 3)]
-
-    def last_sum(keep, got, y_got, z_got):
-        return total(keep[0, 0], got[0, 0], y_got[0], *z_got)
-
-    def z_moved(sums):
-        return [to_dp(value, 2 * k) for k, value in zip((1, 2, 3), sums)]
-
-    def small_of(a_small, f_small, g_up_bias):
-        return jnp.concatenate([a_small, f_small, g_up_bias.reshape(4, D)])
+        return attention_norm_back(scalars, layer, ds, part_own, part_rcv, own, own_spec, a_gain, smalls, deps)
 
     if direct:
-        dh1, ds1, fsmall1, ub1 = ffn_back(1, cot, own_in)
+        pinned = []
+
+        def summed(*outputs, deps=()):
+            return combined(scalars, outputs, deps, pinned)
+
+        def y_sum(keep, got):
+            return [[(keep, 1), (got, 1)]]
+
+        def z_sum(keep, got, y_got):
+            return [[(keep, 0, k), (got, 0, k), (y_got, k)] for k in (1, 3)]
+
+        def far_sum(keep, got, y_got, z_got):
+            return [[(keep, 0, 2), (got, 0, 2), (y_got, 2), (z_got, 1)]]
+
+        def share(keep, got, y_got, z_got, far_got):
+            return [[(keep, 0, 0), (got, 0, 0), (y_got, 0), (z_got, 0), (far_got,)]]
+
+        dh1, ds1, f_small1 = ffn_back(1, cot, own_in, [kept[0][11], kept[1][7]])
         ds1_rcv = to_core(ds1)
-        fk1, fs1 = ffn_grads(1, cot, own_in, cot, far_in, dh1)
-        fg1 = to_core(fs1)
+        fk1, send = ffn_grads(1, cot, own_in, cot, far_in, dh1)
+        pinned.append(fk1)
+        fg1 = to_core(send)
         d_qkv1, part1, part1_oth = attn_back(1, ds1, ds1_rcv, [fk1])
         part1_rcv = to_core(part1_oth)
-        fys1 = y_sum(fk1, fg1)
-        fy1 = to_dp(fys1, 1)
-        g0, asmall1 = attn_norm(1, ds1, part1, part1_rcv, [fys1])
+        value, final_low = summed(y_sum(fk1, fg1), [[(final_send,)]], deps=[part1])
+        fy1 = to_dp(value, 1)
+        g0, a_small1 = attn_norm(1, ds1, part1, part1_rcv, deps=[value])
         g0_o = to_chip(g0)
-        ak1, as1 = attn_grads(1, ds1, ds1_rcv, d_qkv1, [g0])
-        ag1 = to_chip(as1)
-        dh0, ds0, fsmall0, ub0 = ffn_back(0, rows5(g0), local, [ak1])
+        dh0, ds0, f_small0 = ffn_back(0, rows5(g0), local)
         ds0_rcv = to_core(ds0)
-        fzs1 = z_sums(fk1, fg1, fy1)
-        fz1 = z_moved(fzs1)
-        fk0, fs0 = ffn_grads(0, rows5(g0), local, rows5(g0_o), local, dh0, fzs1)
-        fg0 = to_core(fs0)
-        ays1 = y_sum(ak1, ag1)
-        ay1 = to_dp(ays1, 1)
-        d_qkv0, part0, part0_oth = attn_back(0, ds0, ds0_rcv, [fk0, ays1])
+        fk0, send = ffn_grads(0, rows5(g0), local, rows5(g0_o), local, dh0)
+        pinned.append(fk0)
+        (fz1,) = summed(z_sum(fk1, fg1, fy1), deps=[fk0])
+        fg0 = to_core(send)
+        qk1, send, ok1, z_send = attn_grads(1, ds1, ds1_rcv, d_qkv1, [fz1])
+        pinned += [qk1, ok1]
+        qg1, og1 = to_chip(send), to_dp(z_send, 2)
+        fy0, final_low = summed(y_sum(fk0, fg0), [[(final_low,)]], deps=[qk1])
+        d_qkv0, part0, part0_oth = attn_back(0, ds0, ds0_rcv, [fy0])
+        final_got = to_chip(final_low)
+        fz1, fy0 = to_dp(fz1, 2), to_dp(fy0, 1)
         part0_rcv = to_core(part0_oth)
-        fys0 = y_sum(fk0, fg0)
-        fy0 = to_dp(fys0, 1)
-        azs1 = z_sums(ak1, ag1, ay1)
-        az1 = z_moved(azs1)
-        f1 = last_sum(fk1, fg1, fy1, fz1)
+        far1, oy1, qy1 = summed(
+            far_sum(fk1, fg1, fy1, fz1),
+            [[(ok1, 0, 1), (og1, 0, 1)], [(ok1, 1, 1), (og1, 1, 1)]],
+            y_sum(qk1, qg1),
+            deps=[part0],
+        )
+        input_keep, input_send, small = attn_norm(
+            0, ds0, part0, part0_rcv, (a_small1, f_small0, f_small1), [far1, final_got]
+        )
+        far1, oy1, qy1 = to_dp(far1, 4), to_dp(oy1, 1), to_dp(qy1, 1)
+        small_got = to_core(small)
+        input_got = to_chip(input_send)
+        fz0, small = summed(z_sum(fk0, fg0, fy0), [[(small,), (small_got,)]], deps=[input_keep])
+        qk0, send, ok0, y_send = attn_grads(0, ds0, ds0_rcv, d_qkv0, [fz0])
+        fz0, small_got = to_dp(fz0, 2), to_dp(small, 1)
+        pinned += [qk0, ok0]
+        qg0, oy0 = to_chip(send), to_dp(y_send, 1)
+
+        of1, qz1, far0, f1, small = summed(
+            [[(ok1, 1, 0), (og1, 1, 0), (oy1, 1)]],
+            z_sum(qk1, qg1, qy1),
+            far_sum(fk0, fg0, fy0, fz0),
+            share(fk1, fg1, fy1, fz1, far1),
+            [[(small,), (small_got,)]],
+            deps=[qk0],
+        )
+        of1, qz1, far0, small_got = to_dp(of1, 4), to_dp(qz1, 2), to_dp(far0, 4), to_dp(small, 2)
         f1_all = gathered(f1)
-        ak0, as0 = attn_grads(0, ds0, ds0_rcv, d_qkv0, [fys0, f1] + azs1)
-        ag0 = to_chip(as0)
-        *result, asmall0 = attn_norm(0, ds0, part0, part0_rcv, [ak0])
-        fz0 = z_moved(z_sums(fk0, fg0, fy0))
-        a1_all = gathered(last_sum(ak1, ag1, ay1, az1))
-        ay0 = to_dp(y_sum(ak0, ag0), 1)
-        az0 = z_moved(z_sums(ak0, ag0, ay0))
-        f0_all = gathered(last_sum(fk0, fg0, fy0, fz0))
-        a0_all = gathered(last_sum(ak0, ag0, ay0, az0))
-        ups, downs, qkvs, outs = unpacked(scalars, f0_all + a0_all + f1_all + a1_all)
-
-        def small_pieces(a_small, f_small, g_up_bias):
-            vectors = jnp.concatenate([a_small, f_small]).reshape(6, 8, PART).transpose(1, 0, 2)
-            return jnp.concatenate([vectors, g_up_bias.reshape(8, 4, PART)], 1)
-
-        small = jnp.concatenate([small_pieces(asmall0, fsmall0, ub0), small_pieces(asmall1, fsmall1, ub1)], 1)
-        small = small + to_core(small)
-        small = small + to_chip(small)
-
-        def near(distance):
-            return lax.dynamic_index_in_dim(small, replica ^ distance, 0, keepdims=False)
-
-        halves = jnp.stack([near(2 * k + 1) for k in range(4)])
-        y_got = to_dp(halves, 1)
-        small = near(0) + y_got[0] + sum(to_dp(near(2 * k) + y_got[k], 2 * k) for k in (1, 2, 3))
-        small = small.reshape(2, 10, PART)
-
-        def piece(first):
-            return small[:, first]
-
-        up_bias_grad = small[:, 6:10].reshape(2, 4 * PART)
+
+        qy0, oz_1, oz_2, oz_3, ox1, qf1, small = summed(
+            y_sum(qk0, qg0),
+            *[[[(ok0, k), (oy0, k)]] for k in (1, 2, 3)],
+            [[(ok1, 0, 0), (og1, 0, 0), (oy1, 0), (of1,)]],
+            far_sum(qk1, qg1, qy1, qz1),
+            [[(small,), (small_got,)]],
+            deps=[input_got],
+        )
+        qy0, ox1_got, qf1, small_got = to_dp(qy0, 1), to_chip(ox1), to_dp(qf1, 4), to_dp(small, 4)
+        oz0 = [to_dp(value, 2 * k) for k, value in ((1, oz_1), (2, oz_2), (3, oz_3))]
+
+        qz_1, qz_2, qz_3, ox0, f0, q1, o1, small = summed(
+            *[[[(qk0, 0, k), (qg0, 0, k), (qy0, k)]] for k in (1, 2, 3)],
+            [[(ok0, 0), (oy0, 0)] + [(got,) for got in oz0]],
+            share(fk0, fg0, fy0, fz0, far0),
+            share(qk1, qg1, qy1, qz1, qf1),
+            [[(ox1,), (ox1_got,)]],
+            [[(small,), (small_got,)]],
+            deps=f1_all[1:],
+        )
+        ox0_got, small_got = to_chip(ox0), to_chip(small)
+        qz0 = [to_dp(value, 2 * k) for k, value in ((1, qz_1), (2, qz_2), (3, qz_3))]
+        f0_all, a1_all = gathered(f0), gathered(q1) + (o1, to_core(o1))
+
+        q0, o0, small = summed(
+            [[(qk0, 0, 0), (qg0, 0, 0), (qy0, 0)] + [(got,) for got in qz0]],
+            [[(ox0,), (ox0_got,)]],
+            [[(small,), (small_got,)]],
+        )
+        a0_all = gathered(q0) + (o0, to_core(o0))
+        (final_out, input_out, ups, downs, qkvs, outs, *vectors) = unpacked(
+            scalars,
+            (final_keep, final_got, input_keep, input_got),
+            small,
+            f0_all + a0_all + f1_all + a1_all,
+        )
+        g_a_gain, g_a_shift, g_b_out, g_f_gain, g_f_shift, g_b_down, g_b_up = vectors
     else:
+        final_got = to_chip(final_send)
         grads = [None, None]
-        smalls = [None, None]
         grad, grad_spec, grad_o, grad_o_spec = cot, own_in, cot, far_in
         for layer in (1, 0):
-            dh, ds, f_small, g_up_bias = ffn_back(layer, grad, grad_spec)
+            dh, ds, f_small = ffn_back(layer, grad, grad_spec)
             ds_rcv = to_core(ds)
             f_keep, f_send = ffn_grads(layer, grad, grad_spec, grad_o, grad_o_spec, dh)
             d_qkv, part_own, part_oth = attn_back(layer, ds, ds_rcv)
-            a_keep, a_send = attn_grads(layer, ds, ds_rcv, d_qkv)
-            *result, a_small = attn_norm(layer, ds, part_own, to_core(part_oth))
+            keep, send, z_keep, z_send = attn_grads(layer, ds, ds_rcv, d_qkv)
             if layer == 1:
-                grad, grad_spec = rows5(result[0]), local
-                grad_o, grad_o_spec = rows5(to_chip(result[0])), local
-            smalls[layer] = small_of(a_small, f_small, g_up_bias)
+                g0, a_small1 = attn_norm(1, ds, part_own, to_core(part_oth))
+                grad, grad_spec, grad_o, grad_o_spec = rows5(g0), local, rows5(to_chip(g0)), local
+                f_small1 = f_small
+            else:
+                input_keep, input_send, small = attn_norm(
+                    0, ds, part_own, to_core(part_oth), (a_small1, f_small, f_small1)
+                )
+            ffn = in_dp_order(total(f_keep, to_core(f_send)))
+            qv = in_dp_order(total(keep, to_chip(send)))
+            ko = jnp.stack([z_keep, z_send], 1).reshape(8, 2, PART, HALF)
+            ko = total(ko, to_chip(ko))
             ordered = []
-            for share in (reduced_any(f_keep, f_send, to_core), reduced_any(a_keep, a_send, to_chip)):
-                mine, far, near, both = gathered(share)
+            for mine, far, near, both in (gathered(ffn), gathered(qv)):
                 here = jnp.stack([jnp.where(chip == 0, mine, far), jnp.where(chip == 0, far, mine)])
                 there = jnp.stack([jnp.where(chip == 0, near, both), jnp.where(chip == 0, both, near)])
                 pair = jnp.stack([jnp.where(core == 0, here, there), jnp.where(core == 0, there, here)], 1)
                 ordered.append(pair.astype(F32))
-            f_all, a_all = ordered
+            ko_other = to_core(ko)
+            ko_all = jnp.stack([jnp.where(core == 0, ko, ko_other), jnp.where(core == 0, ko_other, ko)]).astype(F32)
+            f_all, qv_all = ordered
             up = f_all[:, :, :, 0:2].transpose(2, 4, 0, 1, 3, 5).reshape(D, FF)
             down = f_all[:, :, :, 2:4].transpose(2, 1, 3, 4, 0, 5).reshape(FF, D)
-            q_k = a_all[0].transpose(1, 3, 2, 0, 4).reshape(D, 2 * D)
-            v = a_all[1, :, :, 0].transpose(1, 2, 0, 3).reshape(D, D)
-            out = a_all[1, :, :, 1].transpose(1, 2, 0, 3).reshape(D, D)
+            q, v = (qv_all[n].transpose(1, 2, 0, 3).reshape(D, D) for n in range(2))
+            k, out = (ko_all[:, :, n].transpose(1, 2, 0, 3).reshape(D, D) for n in range(2))
             grads[layer] = [
                 lax.psum_scatter(array, "dp", scatter_dimension=0, tiled=True)
-                for array in (up, down, jnp.concatenate([q_k, v], 1), out)
+                for array in (up, down, jnp.concatenate([q, k, v], 1), out)
             ]
         ups, downs, qkvs, outs = (jnp.stack(pair) for pair in zip(*grads))
-        small = lax.psum(jnp.stack(smalls), ("section", "dp"))
+        small = lax.psum(small, ("section", "dp")).reshape(4, 8, D)
 
         def mine_of(rows):
             width = rows.shape[-1] // replicas
             return lax.dynamic_slice_in_dim(rows, replica * width, width, 1)
 
-        def piece(first):
-            return mine_of(small[:, first])
-
-        up_bias_grad = mine_of(small[:, 6:10].reshape(2, FF))
-    input_keep, input_send = result
-
-    def placed(keep, send):
-        got = to_chip(send).astype(F32)
-        return jnp.stack([jnp.where(chip == 0, keep, got), jnp.where(chip == 0, got, keep)])[:, None]
-
-    final_out, input_out = placed(final_keep, final_send), placed(input_keep, input_send)
+        g_a_gain, g_a_shift, g_b_out = (mine_of(small[0:2, n]) for n in range(3))
+        g_f_gain, g_f_shift, g_b_down = (mine_of(small[2:4, n]) for n in range(3))
+        g_b_up = mine_of(small[2:4, 4:8].reshape(2, FF))
+
+        def placed(keep, got):
+            got = got.astype(F32)
+            return jnp.stack([jnp.where(chip == 0, keep, got), jnp.where(chip == 0, got, keep)])[:, None]
+
+        final_out, input_out = placed(final_keep, final_got), placed(input_keep, to_chip(input_send))
+
     return (
         final_out,
         input_out,
-        piece(0),
-        piece(1),
+        g_a_gain,
+        g_a_shift,
         qkvs,
         outs,
-        piece(2),
-        piece(3),
-        piece(4),
+        g_b_out,
+        g_f_gain,
+        g_f_shift,
         ups,
-        up_bias_grad,
+        g_b_up,
         downs,
-        piece(5),
+        g_b_down,
     )
 
 

time: 399 us -> 343 us (0.86)
  other arithmetic: 31.1 us -> 0.08 us
  waiting for transfers between devices: 77.3 us -> 66.1 us
  local copies, waits for them, and re-layouts: 21.7 us -> 10.6 us
  Pallas kernels: 215 us -> 207 us
  starting transfers between devices: 47.1 us -> 51.8 us
    convert_element_type x12 -> x0, other arithmetic: 20 us -> none  [total(): return out.astype(BF)]
    pallas_call x15 -> x24, Pallas kernels: 215 us -> 207 us  [call(): return lambda *args: kernel(*args, *deps)]
    ppermute x12 -> x14, starting transfers between devices: 13.2 us -> 18.4 us  [to_chip(): return lax.ppermute(value, 'section', [(0, 2), (2, 0), (1, 3), (3, 1)])]
    ppermute x20 -> x22, waiting for transfers between devices: 9.07 us -> 4.3 us  [to_core(): return lax.ppermute(value, 'section', [(0, 1), (1, 0), (2, 3), (3, 2)])]
    reshape x6 -> x0, local copies, waits for them, and re-layouts: 4.23 us -> none  [the longest x2 1.5 us: small_pieces(): jnp.concatenate([a_small, f_small]).reshape(6, 8, PART).transpose(1, 0, 2)]
    reshape x7, local copies, waits for them, and re-layouts: 5.59 us -> 1.44 us  [vec(): return array.reshape(2, 1, -1)]
    ppermute x20 -> x23, waiting for transfers between devices: 36.5 us -> 32.7 us  [to_dp(): return lax.ppermute(value, 'dp', [(i, i ^ distance) for i in range(8)])]
    ppermute x12 -> x14, waiting for transfers between devices: 31.7 us -> 29.1 us  [to_chip(): return lax.ppermute(value, 'section', [(0, 2), (2, 0), (1, 3), (3, 1)])]
  transfers between devices with their start and end apart: 52 -> 59, of which waited for: 14 -> 17; matrix products, arithmetic and copies ran while one was open for 10% -> 0% of each run, Pallas kernels for 32% -> 51%
where the time goes in v1:
time: 343 us; the launch traced here: 337 us
  Pallas kernels  207 us (60%)
  waiting for transfers between devices  66.1 us (19%)
  starting transfers between devices  51.8 us (15%)
  local copies, waits for them, and re-layouts  10.6 us (3%)
    pallas_call x24, Pallas kernels, call(): return lambda *args: kernel(*args, *deps)  207 us
    ppermute x23, waiting for transfers between devices, to_dp(): return lax.ppermute(value, 'dp', [(i, i ^ distance) for i in range(8)])  32.7 us
    ppermute x14, waiting for transfers between devices, to_chip(): return lax.ppermute(value, 'section', [(0, 2), (2, 0), (1, 3), (3, 1)])  29.1 us
    ppermute x23, starting transfers between devices, to_dp(): return lax.ppermute(value, 'dp', [(i, i ^ distance) for i in range(8)])  29 us
    ppermute x14, starting transfers between devices, to_chip(): return lax.ppermute(value, 'section', [(0, 2), (2, 0), (1, 3), (3, 1)])  18.4 us
    unnamed x74, local copies, waits for them, and re-layouts  9.19 us
  transfers between devices with their start and end apart: 59, of which 17 were waited for; matrix products, arithmetic and copies ran while one was open for 0% of the time, Pallas kernels for 51%

profile of v1, /device:TPU:0, one launch (start us, length us, event | category | flops | bytes accessed | tf_op | source)
XLA Modules:
  0.0 337.5 jit_solution(13386963271844028562)
XLA Ops:
  4.8 14.8 %shard_map.237 = (bf16[1024,1152]{1,0:T(8,128)(2,1)}, bf16[1024,384]{1,0:T(8,128)(2,1)}, bf16[2,256,384]{2,1,0:T(8,128)(2,1)S(1)}, bf16[2,256,384]{2,1,0:T(8,128)(2,1)S(1)}, f32[8,1024]{1,0:T(8,128)S(1)}) custom-call(s32[4]{0:T(128)S(1)} %pad_add_fusion.sc, bf16[2,2,2,256,768]{4,3,2,1,0:T(8,128)(2,1)S(1)} %bitcast.10, ...), custom_call_target="tpu_custom_call" | custom-call | flops 20999999488 | bytes 40000000 | tf_op jit(solution)/shard_map/pallas_call | solution.py:69
  21.4 14.0 %shard_map.238 = (bf16[512,768]{1,0:T(8,128)(2,1)S(1)}, bf16[512,768]{1,0:T(8,128)(2,1)S(1)}, bf16[512,3072]{1,0:T(8,128)(2,1)}, bf16[512,3072]{1,0:T(8,128)(2,1)}, bf16[2,256,768]{2,1,0:T(8,128)(2,1)S(1)}) custom-call(s32[4]{0:T(128)S(1)} %pad_add_fusion.sc, bf16[2,256,384]{2,1,0:T(8,128)(2,1)S(1)} %get-tuple-element.108.refs_0_, ...), custom_call_target="tpu_custom_call" | custom-call | flops 27000000512 | bytes 100000000 | tf_op jit(solution)/shard_map/pallas_call | solution.py:69
  37.8 14.9 %shard_map.239 = (bf16[1024,1152]{1,0:T(8,128)(2,1)}, bf16[1024,384]{1,0:T(8,128)(2,1)}, bf16[2,256,384]{2,1,0:T(8,128)(2,1)S(1)}, bf16[2,256,384]{2,1,0:T(8,128)(2,1)S(1)}, f32[8,1024]{1,0:T(8,128)S(1)}) custom-call(s32[4]{0:T(128)S(1)} %pad_add_fusion.sc, bf16[1,2,1,256,768]{4,3,2,1,0:T(8,128)(2,1)S(1)} %bitcast.16, ...), custom_call_target="tpu_custom_call" | custom-call | flops 20999999488 | bytes 40000000 | tf_op jit(solution)/shard_map/pallas_call | solution.py:69
  56.6 14.4 %shard_map.240 = (bf16[512,768]{1,0:T(8,128)(2,1)S(1)}, bf16[512,768]{1,0:T(8,128)(2,1)S(1)}, bf16[512,3072]{1,0:T(8,128)(2,1)}, bf16[512,3072]{1,0:T(8,128)(2,1...) custom-call(s32[4]{0:T(128)S(1)} %pad_add_fusion.sc, bf16[2,256,384]{2,1,0:T(8,128)(2,1)S(1)} %get-tuple-element.111.refs_0_, ...), custom_call_target="tpu_custom_call" | custom-call | flops 27000000512 | bytes 100000000 | tf_op jit(solution)/shard_map/pallas_call | solution.py:69
  71.3 3.6 %collective-permute-done.4.refs_6_.refs_3_ = bf16[512,768]{1,0:T(8,128)(2,1)S(1)} collective-permute-done((bf16[512,768]{1,0:T(8,128)(2,1)S(1)}, bf16[512,768]{1,0:T(8,128)(2,1)S(1)}, u32[]{:S(2)}, u32[]{:S(2)}) %collective-permute-start.4) | collective-permute-done | bytes 786464 | tf_op jit(solution)/shard_map/ppermute | solution.py:654
  74.9 11.9 %shard_map.241 = (bf16[512,3072]{1,0:T(8,128)(2,1)}, bf16[2,256,768]{2,1,0:T(8,128)(2,1)S(1)}, f32[8,768]{1,0:T(8,128)S(1)}) custom-call(s32[4]{0:T(128)S(1)} %pad_add_fusion.sc, bf16[2,2,2,256,768]{4,3,2,1,0:T(8,128)(2,1)S(1)} %bitcast.20, bf16[512,768]{1,0:T(8,128)(2,1)S(1)} %get-tuple-element.114.refs_1_.refs_2_, ...), custom_call_target="tpu_custom_call" | custom-call | flops 24500000768 | bytes 90000000 | tf_op jit(solution)/shard_map/pallas_call | solution.py:69
  86.9 4.5 %collective-permute-done.7.refs_3_ = bf16[512,768]{1,0:T(8,128)(2,1)S(1)} collective-permute-done((bf16[512,768]{1,0:T(8,128)(2,1)S(1)}, bf16[512,768]{1,0:T(8,128)(2,1)S(1)}, u32[]{:S(2)}, u32[]{:S(2)}) %collective-permute-start.7) | collective-permute-done | bytes 786464 | tf_op jit(solution)/shard_map/ppermute | solution.py:654
  91.4 20.1 %shard_map.242 = (bf16[2,4,4,96,384]{4,3,2,1,0:T(8,128)(2,1)}, bf16[2,4,4,96,384]{4,3,2,1,0:T(8,128)(2,1)S(1)}) custom-call(s32[4]{0:T(128)S(1)} %pad_add_fusion.sc, bf16[2,2,2,256,768]{4,3,2,1,0:T(8,128)(2,1)S(1)} %bitcast.21, bf16[2,2,2,256,768]{4,3,2,1,0:T(8,128)(2,1)S(1)} %bitcast.22, bf16[512,768]{1,0:T(8,128)(2,1)S(1)} %get-tuple-element.114.refs_1_.refs_2_, ...), custom_call_target="tpu_custom_call" | custom-call | flops 43000000512 | bytes 110000000 | tf_op jit(solution)/shard_map/pallas_call | solution.py:69
  113.6 21.0 %shard_map.243 = (bf16[1024,1152]{1,0:T(8,128)(2,1)S(1)}, f32[2,256,768]{2,1,0:T(8,128)S(1)}, bf16[2,256,768]{2,1,0:T(8,128)(2,1)S(1)}) custom-call(s32[4]{0:T(128)S(1)} %pad_add_fusion.sc, bf16[2,256,768]{2,1,0:T(8,128)(2,1)S(1)} %get-tuple-element.117.refs_0_.refs_5_, bf16[2,256,768]{2,1,0:T(8,128)(2,1)S(1)} %collective-permute-done.6.refs_1_.refs_6_, ...), custom_call_target="tpu_custom_call" | custom-call | flops 42500001792 | bytes 60000000 | tf_op jit(solution)/shard_map/pallas_call | solution.py:69
  142.5 12.3 %shard_map.246 = (bf16[512,3072]{1,0:T(8,128)(2,1)}, bf16[2,256,768]{2,1,0:T(8,128)(2,1)}, f32[8,768]{1,0:T(8,128)S(1)}) custom-call(s32[4]{0:T(128)S(1)} %pad_add_fusion.sc, bf16[1,2,1,256,768]{4,3,2,1,0:T(8,128)(2,1)S(1)} %bitcast.25, bf16[512,768]{1,0:T(8,128)(2,1)S(1)} %copy-done.12, f32[2,1,768]{2,1,0:T(1,128)S(1)} %reshape.70.refs_5_.refs_2_.refs_4_, ...), custom_call_target="tpu_custom_call" | custom-call | flops 24500000768 | bytes 90000000 | tf_op jit(solution)/shard_map/pallas_call | solution.py:69
  154.8 5.4 %collective-permute-done.10 = bf16[2,256,768]{2,1,0:T(8,128)(2,1)S(1)} collective-permute-done((bf16[2,256,768]{2,1,0:T(8,128)(2,1)S(1)}, bf16[2,256,768]{2,1,0:T(8,128)(2,1)S(1)}, u32[]{:S(2)}, u32[]{:S(2)}) %collective-permute-start.10) | collective-permute-done | bytes 786464 | tf_op jit(solution)/shard_map/ppermute | solution.py:654
  160.3 19.7 %shard_map.247 = (bf16[2,4,4,96,384]{4,3,2,1,0:T(8,128)(2,1)}, bf16[2,4,4,96,384]{4,3,2,1,0:T(8,128)(2,1)S(1)}) custom-call(s32[4]{0:T(128)S(1)} %pad_add_fusion.sc, bf16[1,2,1,256,768]{4,3,2,1,0:T(8,128)(2,1)S(1)} %bitcast.26, bf16[1,2,1,256,768]{4,3,2,1,0:T(8,128)(2,1)S(1)} %bitcast.27, bf16[512,768]{1,0:T(8,128)(2,1)S(1)} %copy-done.12, ...), custom_call_target="tpu_custom_call" | custom-call | flops 43000000512 | bytes 110000000 | tf_op jit(solution)/shard_map/pallas_call | solution.py:69
  185.3 6.2 %shard_map.249 = (bf16[2,4,96,384]{3,2,1,0:T(8,128)(2,1)}, bf16[2,4,96,384]{3,2,1,0:T(8,128)(2,1)S(1)}, bf16[2,2,2,96,384]{4,3,2,1,0:T(8,128)(2,1)}, bf16[2,2,2,96,384]{4,3,2,1,0:T(8,128)(2,1)S(1)}) custom-call(s32[4]{0:T(128)S(1)} %pad_add_fusion.sc, bf16[1,2,1,256,768]{4,3,2,1,0:T(8,128)(2,1)S(1)} %bitcast.19, bf16[1,2,1,256,768]{4,3,2,1,0:T(8,128)(2,1)S(1)} %bitcast.24, ...), custom_call_target="tpu_custom_call" | custom-call | flops 12499999744 | bytes 60000000 | tf_op jit(solution)/shard_map/pallas_call | solution.py:69
  197.6 21.6 %shard_map.251 = (bf16[1024,1152]{1,0:T(8,128)(2,1)S(1)}, f32[2,256,768]{2,1,0:T(8,128)S(1)}, bf16[2,256,768]{2,1,0:T(8,128)(2,1)S(1)}) custom-call(s32[4]{0:T(128)S(1)} %pad_add_fusion.sc, bf16[2,256,768]{2,1,0:T(8,128)(2,1)} %get-tuple-element.140.refs_0_.refs_5_, bf16[2,256,768]{2,1,0:T(8,128)(2,1)} %collective-permute-done.14.refs_1_.refs_6_, ...), custom_call_target="tpu_custom_call" | custom-call | flops 42500001792 | bytes 60000000 | tf_op jit(solution)/shard_map/pallas_call | solution.py:69
  235.1 7.8 %shard_map.255 = (bf16[2,4,96,384]{3,2,1,0:T(8,128)(2,1)}, bf16[2,4,96,384]{3,2,1,0:T(8,128)(2,1)S(1)}, bf16[4,2,96,384]{3,2,1,0:T(8,128)(2,1)}, bf16[4,2,96,384]{3,2,1,0:T(8,128)(2,1)S(1)}) custom-call(s32[4]{0:T(128)S(1)} %pad_add_fusion.sc, bf16[2,2,2,256,768]{4,3,2,1,0:T(8,128)(2,1)S(1)} %bitcast.14, bf16[2,2,2,256,768]{4,3,2,1,0:T(8,128)(2,1)S(1)} %bitcast.15, ...), custom_call_target="tpu_custom_call" | custom-call | flops 12499999744 | bytes 60000000 | tf_op jit(solution)/shard_map/pallas_call | solution.py:69
  247.3 5.6 %collective-permute-done.26.refs_12_.refs_17_ = bf16[2,4,96,384]{3,2,1,0:T(8,128)(2,1)S(1)} collective-permute-done((bf16[2,4,96,384]{3,2,1,0:T(8,128)(2,1)S(1)}, bf16[2,4,96,384]{3,2,1,0:T(8,128)(2,1)S(1)}, u32[]{:S(2)}, u32[]{:S(2)}) %collective-permute-start.26) | collective-permute-done | bytes 589856 | tf_op jit(solution)/shard_map/ppermute | solution.py:658
  259.3 6.0 %collective-permute-done.22.refs_1_.refs_4_.refs_7_ = bf16[2,4,96,384]{3,2,1,0:T(8,128)(2,1)S(1)} collective-permute-done((bf16[2,4,96,384]{3,2,1,0:T(8,128)(2,1)S(1)}, bf16[2,4,96,384]{3,2,1,0:T(8,128)(2,1)S(1)}, u32[]{:S(2)}, u32[]{:S(2)}) %collective-permute-start.22) | collective-permute-done | bytes 589856 | tf_op jit(solution)/shard_map/ppermute | solution.py:654
  274.0 10.2 %collective-permute-done.37.refs_23_ = bf16[96,384]{1,0:T(8,128)(2,1)S(1)} collective-permute-done((bf16[96,384]{1,0:T(8,128)(2,1)S(1)}, bf16[96,384]{1,0:T(8,128)(2,1)S(1)}, u32[]{:S(2)}, u32[]{:S(2)}) %collective-permute-start.37) | collective-permute-done | bytes 73760 | tf_op jit(solution)/shard_map/ppermute | solution.py:658
  286.9 5.9 %collective-permute-done.35.refs_13_ = bf16[2,96,384]{2,1,0:T(8,128)(2,1)S(1)} collective-permute-done((bf16[2,96,384]{2,1,0:T(8,128)(2,1)S(1)}, bf16[2,96,384]{2,1,0:T(8,128)(2,1)S(1)}, u32[]{:S(2)}, u32[]{:S(2)}) %collective-permute-start.35) | collective-permute-done | bytes 147488 | tf_op jit(solution)/shard_map/ppermute | solution.py:658
  294.3 3.6 %collective-permute-done.38.refs_25_ = bf16[2,96,384]{2,1,0:T(8,128)(2,1)S(1)} collective-permute-done((bf16[2,96,384]{2,1,0:T(8,128)(2,1)S(1)}, bf16[2,96,384]{2,1,0:T(8,128)(2,1)S(1)}, u32[]{:S(2)}, u32[]{:S(2)}) %collective-permute-start.38) | collective-permute-done | bytes 147488 | tf_op jit(solution)/shard_map/ppermute | solution.py:654
  297.9 7.3 %collective-permute-done.36.refs_18_ = bf16[4,96,384]{2,1,0:T(8,128)(2,1)S(1)} collective-permute-done((bf16[4,96,384]{2,1,0:T(8,128)(2,1)S(1)}, bf16[4,96,384]{2,1,0:T(8,128)(2,1)S(1)}, u32[]{:S(2)}, u32[]{:S(2)}) %collective-permute-start.36) | collective-permute-done | bytes 294944 | tf_op jit(solution)/shard_map/ppermute | solution.py:658
  316.6 3.5 %collective-permute-done.45.refs_5_ = bf16[96,384]{1,0:T(8,128)(2,1)S(1)} collective-permute-done((bf16[96,384]{1,0:T(8,128)(2,1)S(1)}, bf16[96,384]{1,0:T(8,128)(2,1)S(1)}, u32[]{:S(2)}, u32[]{:S(2)}) %collective-permute-start.45) | collective-permute-done | bytes 73760 | tf_op jit(solution)/shard_map/ppermute | solution.py:658
  320.0 3.2 collective-permute-done.55.refs_20_
  331.9 5.1 %shard_map.260 = (f32[2,1,256,768]{3,2,1,0:T(8,128)}, f32[2,1,256,768]{3,2,1,0:T(8,128)}, f32[2,96,3072]{2,1,0:T(8,128)}, f32[2,384,768]{2,1,0:T(8,128)}, f32[2,...) custom-call(s32[4]{0:T(128)S(1)} %pad_add_fusion.sc, ...), custom_call_target="tpu_custom_call" | custom-call | flops 5000000 | bytes 55000000 | tf_op jit(solution)/shard_map/pallas_call | solution.py:69
  (200 shorter events, 93.4 us)
Async XLA Ops:
  35.9 20.6 %collective-permute-start.3 = (bf16[2,256,384]{2,1,0:T(8,128)(2,1)S(1)}, bf16[2,256,384]{2,1,0:T(8,128)(2,1)S(1)}, u32[]{:S(2)}, u32[]{:S(2)}) collective-permute-start(bf16[2,256,384]{2,1,0:T(8,128)(2,1)S(1)} %get-tuple-element.108.refs_0_), channel_id=1, source_target_pairs={{0,8},{8,0},{16,24},{24,16},{1,9},{9,1},{17,25},{25,17},{2,10},{10... | collective-permute-start | bytes 1179656 | tf_op jit(solution)/shard_map/ppermute | solution.py:650
  53.8 21.0 %collective-permute-start.4 = (bf16[512,768]{1,0:T(8,128)(2,1)S(1)}, bf16[512,768]{1,0:T(8,128)(2,1)S(1)}, u32[]{:S(2)}, u32[]{:S(2)}) collective-permute-start(bf16[512,768]{1,0:T(8,128)(2,1)S(1)} %get-tuple-element.116.refs_1_.refs_2_), channel_id=1, source_target_pairs={{0,16},{16,0},{8,24},{24,8},{1,17},{17,1},{9,25},{25,9},{2,18},{18... | collective-permute-start | bytes 2359304 | tf_op jit(solution)/shard_map/ppermute | solution.py:654
  56.5 18.4 %collective-permute-start.5 = (bf16[2,256,384]{2,1,0:T(8,128)(2,1)S(1)}, bf16[2,256,384]{2,1,0:T(8,128)(2,1)S(1)}, u32[]{:S(2)}, u32[]{:S(2)}) collective-permute-start(bf16[2,256,384]{2,1,0:T(8,128)(2,1)S(1)} %get-tuple-element.111.refs_0_), channel_id=1, source_target_pairs={{0,8},{8,0},{16,24},{24,16},{1,9},{9,1},{17,25},{25,17},{2,10},{10... | collective-permute-start | bytes 1179656 | tf_op jit(solution)/shard_map/ppermute | solution.py:650
  71.0 20.4 %collective-permute-start.7 = (bf16[512,768]{1,0:T(8,128)(2,1)S(1)}, bf16[512,768]{1,0:T(8,128)(2,1)S(1)}, u32[]{:S(2)}, u32[]{:S(2)}) collective-permute-start(bf16[512,768]{1,0:T(8,128)(2,1)S(1)} %get-tuple-element.114.refs_1_.refs_2_), channel_id=1, source_target_pairs={{0,16},{16,0},{8,24},{24,8},{1,17},{17,1},{9,25},{25,9},{2,18},{18... | collective-permute-start | bytes 2359304 | tf_op jit(solution)/shard_map/ppermute | solution.py:654
  86.8 24.8 %collective-permute-start.6 = (bf16[2,256,768]{2,1,0:T(8,128)(2,1)S(1)}, bf16[2,256,768]{2,1,0:T(8,128)(2,1)S(1)}, u32[]{:S(2)}, u32[]{:S(2)}) collective-permute-start(bf16[2,256,768]{2,1,0:T(8,128)(2,1)S(1)} %get-tuple-element.117.refs_0_.refs_5_), channel_id=1, source_target_pairs={{0,8},{8,0},{16,24},{24,16},{1,9},{9,1},{17,25},{25,17},{2,10},{10... | collective-permute-start | bytes 2359304 | tf_op jit(solution)/shard_map/ppermute | solution.py:650
  111.5 23.6 %collective-permute-start.9 = (bf16[2,4,4,96,384]{4,3,2,1,0:T(8,128)(2,1)S(1)}, bf16[2,4,4,96,384]{4,3,2,1,0:T(8,128)(2,1)S(1)}, u32[]{:S(2)}, u32[]{:S(2)}) collective-permute-start(bf16[2,4,4,96,384]{4,3,2,1,0:T(8,128)(2,1)S(1)} %get-tuple-element.126), channel_id=1, source_target_pairs={{0,8},{8,0},{16,24},{24,16},{1,9},{9,1},{17,25},{25,17},{2,10},{10... | collective-permute-start | bytes 7077896 | tf_op jit(solution)/shard_map/ppermute | solution.py:650
  137.2 42.8 %collective-permute-start.12 = (bf16[4,4,96,384]{3,2,1,0:T(8,128)(2,1)S(1)}, bf16[4,4,96,384]{3,2,1,0:T(8,128)(2,1)S(1)}, u32[]{:S(2)}, u32[]{:S(2)}) collective-permute-start(bf16[4,4,96,384]{3,2,1,0:T(8,128)(2,1)S(1)} %get-tuple-element.128.refs_5_), channel_id=1, source_target_pairs={{0,1},{1,0},{2,3},{3,2},{4,5},{5,4},{6,7},{7,6},{8,9},{9,8},{10,11... | collective-permute-start | bytes 3538952 | tf_op jit(solution)/shard_map/ppermute | solution.py:658
  141.0 19.3 %collective-permute-start.10 = (bf16[2,256,768]{2,1,0:T(8,128)(2,1)S(1)}, bf16[2,256,768]{2,1,0:T(8,128)(2,1)S(1)}, u32[]{:S(2)}, u32[]{:S(2)}) collective-permute-start(bf16[2,256,768]{2,1,0:T(8,128)(2,1)S(1)} %get-tuple-element.129), channel_id=1, source_target_pairs={{0,16},{16,0},{8,24},{24,8},{1,17},{17,1},{9,25},{25,9},{2,18},{18... | collective-permute-start | bytes 2359304 | tf_op jit(solution)/shard_map/ppermute | solution.py:654
  154.8 42.4 %collective-permute-start.14 = (bf16[2,256,768]{2,1,0:T(8,128)(2,1)}, bf16[2,256,768]{2,1,0:T(8,128)(2,1)}, u32[]{:S(2)}, u32[]{:S(2)}) collective-permute-start(bf16[2,256,768]{2,1,0:T(8,128)(2,1)} %get-tuple-element.140.refs_0_.refs_5_), channel_id=1, source_target_pairs={{0,8},{8,0},{16,24},{24,16},{1,9},{9,1},{17,25},{25,17},{2,10},{10... | collective-permute-start | bytes 2359304 | tf_op jit(solution)/shard_map/ppermute | solution.py:650
  183.7 35.7 %collective-permute-start.16 = (bf16[2,4,96,384]{3,2,1,0:T(8,128)(2,1)S(1)}, bf16[2,4,96,384]{3,2,1,0:T(8,128)(2,1)S(1)}, u32[]{:S(2)}, u32[]{:S(2)}) collective-permute-start(bf16[2,4,96,384]{3,2,1,0:T(8,128)(2,1)S(1)} %shard_map.248.refs_10_), channel_id=1, source_target_pairs={{0,2},{1,3},{2,0},{3,1},{4,6},{5,7},{6,4},{7,5},{8,10},{9,11},{10,... | collective-permute-start | bytes 1769480 | tf_op jit(solution)/shard_map/ppermute | solution.py:658
  191.5 27.7 %collective-permute-start.17 = (bf16[2,2,2,96,384]{4,3,2,1,0:T(8,128)(2,1)S(1)}, bf16[2,2,2,96,384]{4,3,2,1,0:T(8,128)(2,1)S(1)}, u32[]{:S(2)}, u32[]{:S(2)}) collective-permute-start(bf16[2,2,2,96,384]{4,3,2,1,0:T(8,128)(2,1)S(1)} %get-tuple-element.151), channel_id=1, source_target_pairs={{0,2},{1,3},{2,0},{3,1},{4,6},{5,7},{6,4},{7,5},{8,10},{9,11},{10,... | collective-permute-start | bytes 1769480 | tf_op jit(solution)/shard_map/ppermute | solution.py:658
  192.0 27.3 %collective-permute-start.18 = (bf16[2,4,96,384]{3,2,1,0:T(8,128)(2,1)S(1)}, bf16[2,4,96,384]{3,2,1,0:T(8,128)(2,1)S(1)}, u32[]{:S(2)}, u32[]{:S(2)}) collective-permute-start(bf16[2,4,96,384]{3,2,1,0:T(8,128)(2,1)S(1)} %get-tuple-element.152), channel_id=1, source_target_pairs={{0,16},{16,0},{8,24},{24,8},{1,17},{17,1},{9,25},{25,9},{2,18},{18... | collective-permute-start | bytes 1769480 | tf_op jit(solution)/shard_map/ppermute | solution.py:654
  196.8 24.9 %collective-permute-start.13 = (bf16[256,768]{1,0:T(8,128)(2,1)S(1)}, bf16[256,768]{1,0:T(8,128)(2,1)S(1)}, u32[]{:S(2)}, u32[]{:S(2)}) collective-permute-start(bf16[256,768]{1,0:T(8,128)(2,1)S(1)} %get-tuple-element.139), channel_id=1, source_target_pairs={{0,16},{16,0},{8,24},{24,8},{1,17},{17,1},{9,25},{25,9},{2,18},{18... | collective-permute-start | bytes 1179656 | tf_op jit(solution)/shard_map/ppermute | solution.py:654
  197.2 32.9 %collective-permute-start.20 = (bf16[4,4,96,384]{3,2,1,0:T(8,128)(2,1)S(1)}, bf16[4,4,96,384]{3,2,1,0:T(8,128)(2,1)S(1)}, u32[]{:S(2)}, u32[]{:S(2)}) collective-permute-start(bf16[4,4,96,384]{3,2,1,0:T(8,128)(2,1)S(1)} %get-tuple-element.144.refs_10_), channel_id=1, source_target_pairs={{0,1},{1,0},{2,3},{3,2},{4,5},{5,4},{6,7},{7,6},{8,9},{9,8},{10,11... | collective-permute-start | bytes 3538952 | tf_op jit(solution)/shard_map/ppermute | solution.py:658
  225.3 20.5 %collective-permute-start.27 = (bf16[4,96,384]{2,1,0:T(8,128)(2,1)S(1)}, bf16[4,96,384]{2,1,0:T(8,128)(2,1)S(1)}, u32[]{:S(2)}, u32[]{:S(2)}) collective-permute-start(bf16[4,96,384]{2,1,0:T(8,128)(2,1)S(1)} %get-tuple-element.153.refs_8_), channel_id=1, source_target_pairs={{0,4},{1,5},{2,6},{3,7},{4,0},{5,1},{6,2},{7,3},{8,12},{9,13},{10,... | collective-permute-start | bytes 884744 | tf_op jit(solution)/shard_map/ppermute | solution.py:658
  233.5 19.3 %collective-permute-start.26 = (bf16[2,4,96,384]{3,2,1,0:T(8,128)(2,1)S(1)}, bf16[2,4,96,384]{3,2,1,0:T(8,128)(2,1)S(1)}, u32[]{:S(2)}, u32[]{:S(2)}) collective-permute-start(bf16[2,4,96,384]{3,2,1,0:T(8,128)(2,1)S(1)} %get-tuple-element.159.refs_10_), channel_id=1, source_target_pairs={{0,2},{1,3},{2,0},{3,1},{4,6},{5,7},{6,4},{7,5},{8,10},{9,11},{10,... | collective-permute-start | bytes 1769480 | tf_op jit(solution)/shard_map/ppermute | solution.py:658
  244.5 20.7 %collective-permute-start.22 = (bf16[2,4,96,384]{3,2,1,0:T(8,128)(2,1)S(1)}, bf16[2,4,96,384]{3,2,1,0:T(8,128)(2,1)S(1)}, u32[]{:S(2)}, u32[]{:S(2)}) collective-permute-start(bf16[2,4,96,384]{3,2,1,0:T(8,128)(2,1)S(1)} %get-tuple-element.161), channel_id=1, source_target_pairs={{0,16},{16,0},{8,24},{24,8},{1,17},{17,1},{9,25},{25,9},{2,18},{18... | collective-permute-start | bytes 1769480 | tf_op jit(solution)/shard_map/ppermute | solution.py:654
  245.8 21.1 %collective-permute-start.23 = (bf16[4,2,96,384]{3,2,1,0:T(8,128)(2,1)S(1)}, bf16[4,2,96,384]{3,2,1,0:T(8,128)(2,1)S(1)}, u32[]{:S(2)}, u32[]{:S(2)}) collective-permute-start(bf16[4,2,96,384]{3,2,1,0:T(8,128)(2,1)S(1)} %get-tuple-element.163), channel_id=1, source_target_pairs={{0,1},{1,0},{2,3},{3,2},{4,5},{5,4},{6,7},{7,6},{8,9},{9,8},{10,11... | collective-permute-start | bytes 1769480 | tf_op jit(solution)/shard_map/ppermute | solution.py:658
  265.2 21.3 %collective-permute-start.40 = (bf16[4,96,384]{2,1,0:T(8,128)(2,1)S(1)}, bf16[4,96,384]{2,1,0:T(8,128)(2,1)S(1)}, u32[]{:S(2)}, u32[]{:S(2)}) collective-permute-start(bf16[4,96,384]{2,1,0:T(8,128)(2,1)S(1)} %get-tuple-element.178.refs_15_), channel_id=1, source_target_pairs={{0,16},{16,0},{8,24},{24,8},{1,17},{17,1},{9,25},{25,9},{2,18},{18... | collective-permute-start | bytes 884744 | tf_op jit(solution)/shard_map/ppermute | solution.py:654
  269.0 17.5 %collective-permute-start.33 = (bf16[2,96,384]{2,1,0:T(8,128)(2,1)S(1)}, bf16[2,96,384]{2,1,0:T(8,128)(2,1)S(1)}, u32[]{:S(2)}, u32[]{:S(2)}) collective-permute-start(bf16[2,96,384]{2,1,0:T(8,128)(2,1)S(1)} %get-tuple-element.171), channel_id=1, source_target_pairs={{0,2},{1,3},{2,0},{3,1},{4,6},{5,7},{6,4},{7,5},{8,10},{9,11},{10,... | collective-permute-start | bytes 442376 | tf_op jit(solution)/shard_map/ppermute | solution.py:658
  284.2 21.0 %collective-permute-start.41 = (bf16[4,96,384]{2,1,0:T(8,128)(2,1)S(1)}, bf16[4,96,384]{2,1,0:T(8,128)(2,1)S(1)}, u32[]{:S(2)}, u32[]{:S(2)}) collective-permute-start(bf16[4,96,384]{2,1,0:T(8,128)(2,1)S(1)} %get-tuple-element.178.refs_15_), channel_id=1, source_target_pairs={{0,8},{8,0},{16,24},{24,16},{1,9},{9,1},{17,25},{25,17},{2,10},{10... | collective-permute-start | bytes 884744 | tf_op jit(solution)/shard_map/ppermute | solution.py:650
  286.5 18.7 %collective-permute-start.36 = (bf16[4,96,384]{2,1,0:T(8,128)(2,1)S(1)}, bf16[4,96,384]{2,1,0:T(8,128)(2,1)S(1)}, u32[]{:S(2)}, u32[]{:S(2)}) collective-permute-start(bf16[4,96,384]{2,1,0:T(8,128)(2,1)S(1)} %get-tuple-element.174), channel_id=1, source_target_pairs={{0,4},{1,5},{2,6},{3,7},{4,0},{5,1},{6,2},{7,3},{8,12},{9,13},{10,... | collective-permute-start | bytes 884744 | tf_op jit(solution)/shard_map/ppermute | solution.py:658
  286.5 18.7 %collective-permute-start.32 = (bf16[4,96,384]{2,1,0:T(8,128)(2,1)S(1)}, bf16[4,96,384]{2,1,0:T(8,128)(2,1)S(1)}, u32[]{:S(2)}, u32[]{:S(2)}) collective-permute-start(bf16[4,96,384]{2,1,0:T(8,128)(2,1)S(1)} %get-tuple-element.170), channel_id=1, source_target_pairs={{0,1},{1,0},{2,3},{3,2},{4,5},{5,4},{6,7},{7,6},{8,9},{9,8},{10,11... | collective-permute-start | bytes 884744 | tf_op jit(solution)/shard_map/ppermute | solution.py:658
  286.6 18.6 %collective-permute-start.42 = (bf16[4,96,384]{2,1,0:T(8,128)(2,1)S(1)}, bf16[4,96,384]{2,1,0:T(8,128)(2,1)S(1)}, u32[]{:S(2)}, u32[]{:S(2)}) collective-permute-start(bf16[4,96,384]{2,1,0:T(8,128)(2,1)S(1)} %collective-permute-done.40.refs_28_.refs_16_), channel_id=1, source_target_pairs={{0,8},{8,0},{16,24},{24,16},{1,9},{9,1},{17,25},{25,17},{2,10},{10... | collective-permute-start | bytes 884744 | tf_op jit(solution)/shard_map/ppermute | solution.py:650
  (72 other events, 621.8 us)

commit v2 on v1

--- a/solution.py
+++ b/solution.py
@@ -96,6 +96,17 @@
 
 def in_order(own, other, block, core):
     return jnp.where(core == block % 2, own[block // 2], other[block // 2])
+
+
+def weight_copies(layer, core, weights, sides, sems):
+    return [
+        pltpu.make_async_copy(
+            weights.at[layer, :, pl.ds(pl.multiple_of(j * D + core * HALF, PAIR), HALF)],
+            sides.at[:, j * HALF : (j + 1) * HALF],
+            sems.at[j],
+        )
+        for j in range(3)
+    ]
 
 
 def episode_columns(ep_ref):
@@ -198,25 +209,30 @@
     return active, slope
 
 
-FT = 512
-
-
-def ffn_fwd_body(last, sc, ctx_own, ctx_rcv, own, w_out, b_out, gain, shift, w_up, b_up, w_down, b_down, *rest):
+FT = 1024
+
+
+def project_body(sc, ctx_own, ctx_rcv, own, w_out, b_out, s2, ctx_full):
+    core = sc[C]
+    a, b = ctx_own[...].reshape(ROWS, HALF), ctx_rcv[...].reshape(ROWS, HALF)
+    both = jnp.concatenate([jnp.where(core == 0, a, b), jnp.where(core == 0, b, a)], 1)
+    ctx_full[...] = both
+    stream = own[0, :, 0].reshape(ROWS, D).astype(F32) + dot(both, w_out[0]) + b_out[0]
+    s2[...] = stream.astype(BF)
+
+
+def ffn_fwd_body(last, sc, *refs):
     if last:
-        s2, ctx_full, act, slope, keep, send, normed, acc = rest
+        s2, gain, shift, w_up, b_up, w_down, b_down, act, slope, keep, send, normed, acc = refs
     else:
-        s2, ctx_full, act, slope, s3, normed, acc = rest
+        gain, shift, w_up, b_up, w_down, b_down, s2, ctx_full, act, slope, s3, normed, acc = refs[5:]
     t = pl.program_id(0)
-    core = sc[C]
 
     @pl.when(t == 0)
     def _():
-        a, b = ctx_own[...].reshape(ROWS, HALF), ctx_rcv[...].reshape(ROWS, HALF)
-        both = jnp.concatenate([jnp.where(core == 0, a, b), jnp.where(core == 0, b, a)], 1)
-        ctx_full[...] = both
-        stream = own[0, :, 0].reshape(ROWS, D).astype(F32) + dot(both, w_out[0]) + b_out[0]
-        low = stream.astype(BF)
-        s2[...] = low
+        if not last:
+            project_body(sc, *refs[:5], s2, ctx_full)
+        low = s2[...]
         normed[...] = norm_low(low, gain[0], shift[0])
         acc[...] = low.astype(F32) + b_down[0]
 
@@ -237,44 +253,66 @@
             s3[...] = acc[...].reshape(2, BLOCK, D).astype(BF)
 
 
-def ffn_forward(scalars, layer, last, ctx_own, ctx_rcv, own, own_spec, weights, dep):
+def ffn_forward(scalars, layer, ctx_own, ctx_rcv, own, own_spec, weights, deps):
+    specs, ffn_weight_specs, hidden = projection_specs(layer, own_spec), ffn_specs(layer), hidden_specs()
     w_out, b_out, gain, shift, w_up, b_up, w_down, b_down = weights
-    vector = at_layer((1, 1, D), layer)
-    out_specs = [
-        whole((ROWS, D)),
-        whole((ROWS, D)),
-        pl.BlockSpec((ROWS, FT), lambda i, sc: (0, i)),
-        pl.BlockSpec((ROWS, FT), lambda i, sc: (0, i)),
-    ]
-    out_shape = [shape((ROWS, D), BF), shape((ROWS, D), BF), stored((ROWS, FF), BF), stored((ROWS, FF), BF)]
-    if last:
-        out_specs += [whole((BLOCK, D)), whole((BLOCK, D))]
-        out_shape += [shape((BLOCK, D), F32), shape((BLOCK, D), BF)]
-    else:
-        out_specs += [whole((2, BLOCK, D))]
-        out_shape += [shape((2, BLOCK, D), BF)]
     return call(
-        partial(ffn_fwd_body, last),
+        partial(ffn_fwd_body, False),
         (FF // FT,),
-        [
-            whole((2, BLOCK, HALF)),
-            whole((2, BLOCK, HALF)),
-            own_spec,
-            at_layer((1, D, D), layer),
-            vector,
-            vector,
-            vector,
-            pl.BlockSpec((1, D, FT), lambda i, sc: (layer, 0, i)),
-            pl.BlockSpec((1, 1, FT), lambda i, sc: (layer, 0, i)),
-            pl.BlockSpec((1, FT, D), lambda i, sc: (layer, i, 0)),
-            vector,
-        ],
-        out_specs,
-        out_shape,
+        specs + ffn_weight_specs,
+        [whole((ROWS, D)), whole((ROWS, D))] + hidden + [whole((2, BLOCK, D))],
+        [shape((ROWS, D), BF)] * 2 + [stored((ROWS, FF), BF)] * 2 + [shape((2, BLOCK, D), BF)],
         [pltpu.VMEM((ROWS, D), BF), pltpu.VMEM((ROWS, D), F32)],
         (5.4e9, 20e6),
-        () if dep is None else (dep,),
+        deps,
     )(scalars, ctx_own, ctx_rcv, own, from_hbm(w_out), b_out, gain, shift, from_hbm(w_up), b_up, from_hbm(w_down), b_down)
+
+
+def projected(scalars, layer, ctx_own, ctx_rcv, own, own_spec, w_out, b_out, deps):
+    return call(
+        project_body,
+        (1,),
+        projection_specs(layer, own_spec),
+        [whole((ROWS, D)), whole((ROWS, D))],
+        [shape((ROWS, D), BF)] * 2,
+        [],
+        (6e8, 5e6),
+        deps,
+    )(scalars, ctx_own, ctx_rcv, own, from_hbm(w_out), b_out)
+
+
+def last_ffn_forward(scalars, layer, s2, weights):
+    gain, shift, w_up, b_up, w_down, b_down = weights
+    return call(
+        partial(ffn_fwd_body, True),
+        (FF // FT,),
+        [whole((ROWS, D))] + ffn_specs(layer),
+        hidden_specs() + [whole((BLOCK, D)), whole((BLOCK, D))],
+        [shape((ROWS, FF), BF)] * 2 + [shape((BLOCK, D), F32), shape((BLOCK, D), BF)],
+        [pltpu.VMEM((ROWS, D), BF), pltpu.VMEM((ROWS, D), F32)],
+        (4.8e9, 18e6),
+    )(scalars, s2, gain, shift, from_hbm(w_up), b_up, from_hbm(w_down), b_down)
+
+
+def projection_specs(layer, own_spec):
+    part = whole((2, BLOCK, HALF))
+    return [part, part, own_spec, at_layer((1, D, D), layer), at_layer((1, 1, D), layer)]
+
+
+def ffn_specs(layer):
+    vector = at_layer((1, 1, D), layer)
+    return [
+        vector,
+        vector,
+        pl.BlockSpec((1, D, FT), lambda i, sc: (layer, 0, i)),
+        pl.BlockSpec((1, 1, FT), lambda i, sc: (layer, 0, i)),
+        pl.BlockSpec((1, FT, D), lambda i, sc: (layer, i, 0)),
+        vector,
+    ]
+
+
+def hidden_specs():
+    return [pl.BlockSpec((ROWS, FT), lambda i, sc: (0, i))] * 2
 
 
 def norm_back(d_normed, rows, gain):
@@ -330,6 +368,7 @@
 
 
 BT = 768
+AT = 1536
 
 
 def ffn_back_body(sc, grad, s2, gain, w_up, w_down, slope, dh, ds, small, acc):
@@ -339,7 +378,9 @@
     d_hidden = d_act * slope[...].astype(F32)
     d_low = d_hidden.astype(BF)
     dh[...] = d_low
-    small[pl.ds(4 + t, 1)] = jnp.sum(d_low.astype(F32), 0, keepdims=True)
+    sums = jnp.sum(d_low.astype(F32), 0, keepdims=True)
+    for j in range(2):
+        small[pl.ds(4 + 2 * t + j, 1)] = sums[:, j * D : (j + 1) * D]
     part = dot_nt(d_low, w_up[0])
 
     @pl.when(t == 0)
@@ -350,7 +391,7 @@
     def _():
         acc[...] += part
 
-    @pl.when(t == FF // BT - 1)
+    @pl.when(t == FF // AT - 1)
     def _():
         rows = low.astype(F32)
         d_rows, g_gain, g_shift = norm_back(acc[...], s2[...].astype(F32), gain[0])
@@ -362,25 +403,25 @@
     gain, w_up, w_down = weights
     return call(
         ffn_back_body,
-        (FF // BT,),
+        (FF // AT,),
         [
             grad_spec,
             whole((ROWS, D)),
             at_layer((1, 1, D), layer),
-            pl.BlockSpec((1, D, BT), lambda i, sc: (layer, 0, i)),
-            pl.BlockSpec((1, BT, D), lambda i, sc: (layer, i, 0)),
-            pl.BlockSpec((ROWS, BT), lambda i, sc: (0, i)),
+            pl.BlockSpec((1, D, AT), lambda i, sc: (layer, 0, i)),
+            pl.BlockSpec((1, AT, D), lambda i, sc: (layer, i, 0)),
+            pl.BlockSpec((ROWS, AT), lambda i, sc: (0, i)),
         ],
         [
-            pl.BlockSpec((ROWS, BT), lambda i, sc: (0, i)),
+            pl.BlockSpec((ROWS, AT), lambda i, sc: (0, i)),
             whole((2, BLOCK, D)),
             whole((8, D)),
         ],
-        [stored((ROWS, FF), BF), shape((2, BLOCK, D), BF), shape((8, D), F32)],
+        [shape((ROWS, FF), BF), shape((2, BLOCK, D), BF), shape((8, D), F32)],
         [pltpu.VMEM((ROWS, D), F32)],
         (4.9e9, 18e6),
         deps,
-    )(scalars, grad, s2, gain, from_hbm(w_up), from_hbm(w_down), from_hbm(slope))
+    )(scalars, grad, s2, gain, from_hbm(w_up), from_hbm(w_down), (slope if layer == 1 else from_hbm(slope)))
 
 
 def place(sc, piece):
@@ -467,13 +508,17 @@
         ],
         (8.6e9, 22e6),
         deps,
-    )(scalars, grad, grad_o, s2, s2_o, gain, shift, from_hbm(act), from_hbm(dh), from_hbm(w_up), b_up, from_hbm(w_down))
+    )(scalars, grad, grad_o, s2, s2_o, gain, shift, (act if layer == 1 else from_hbm(act)), dh, from_hbm(w_up), b_up, from_hbm(w_down))
 
 
 def attn_back_body(
-    sc, gr_own, gr_rcv, qkv, ctx, lse, ep, w_out, wq, wk, wv, d_qkv, part_own, part_oth, bias, d_ctx, delta, d_k, d_v
+    layer, sc, gr_own, gr_rcv, qkv, ctx, lse, ep, w_out, weights, d_qkv, part_own, part_oth, bias, d_ctx, delta, d_k, d_v,
+    sides, sems
 ):
     core = sc[C]
+    copies = weight_copies(layer, core, weights, sides, sems)
+    for copy in copies:
+        copy.start()
     for b in range(4):
         rows = slice(b * BLOCK, (b + 1) * BLOCK)
         d_ctx[rows] = dot_nt(in_order(gr_own, gr_rcv, b, core), w_out[0]).astype(BF)
@@ -524,11 +569,11 @@
         d_qkv[:, pl.ds(HALF + at, PAIR)] = d_k[...].astype(BF)
         d_qkv[:, pl.ds(2 * HALF + at, PAIR)] = d_v[...].astype(BF)
 
+    for copy in copies:
+        copy.wait()
     for b in range(4):
         rows = slice(b * BLOCK, (b + 1) * BLOCK)
-        part = dot_nt(d_qkv[rows, 0:HALF], wq[0])
-        part += dot_nt(d_qkv[rows, HALF : 2 * HALF], wk[0])
-        part += dot_nt(d_qkv[rows, 2 * HALF : 3 * HALF], wv[0])
+        part = dot_nt(d_qkv[rows], sides[...])
 
         @pl.when(core == b % 2)
         def _():
@@ -540,10 +585,9 @@
 
 
 def attention_backward(scalars, layer, gr_own, gr_rcv, qkv, ctx, lse, episodes, ep_spec, w_out, w_qkv, deps=()):
-    columns = [pl.BlockSpec((1, D, HALF), partial(lambda j, i, sc: (layer, 0, 2 * j + sc[C]), j)) for j in range(3)]
     block = whole((2, BLOCK, D))
     return call(
-        attn_back_body,
+        partial(attn_back_body, layer),
         (1,),
         [
             block,
@@ -553,8 +597,8 @@
             whole((8, LENGTH)),
             ep_spec,
             pl.BlockSpec((1, HALF, D), lambda i, sc: (layer, sc[C], 0)),
-        ]
-        + columns,
+            pl.BlockSpec(memory_space=pl.ANY),
+        ],
         [whole((LENGTH, 3 * HALF)), block, block],
         [shape((LENGTH, 3 * HALF), BF), shape((2, BLOCK, D), F32), shape((2, BLOCK, D), BF)],
         [
@@ -563,10 +607,12 @@
             pltpu.VMEM((8, LENGTH), F32),
             pltpu.VMEM((LENGTH, PAIR), F32),
             pltpu.VMEM((LENGTH, PAIR), F32),
+            pltpu.VMEM((D, 3 * HALF), BF),
+            pltpu.SemaphoreType.DMA((3,)),
         ],
         (2.5e9 + 6e9, 12e6),
         deps,
-    )(scalars, gr_own, gr_rcv, from_hbm(qkv), from_hbm(ctx), lse, episodes, from_hbm(w_out), *[from_hbm(w_qkv)] * 3)
+    )(scalars, gr_own, gr_rcv, from_hbm(qkv), from_hbm(ctx), lse, episodes, from_hbm(w_out), from_hbm(w_qkv))
 
 
 def attn_weight_body(
@@ -665,31 +711,61 @@
     return out.astype(BF)
 
 
+class Flat(list):
+    pass
+
+
 def combined(scalars, outputs, deps=(), pinned=()):
     terms, dims, dtypes = [], [], []
+
+    def block_of(term):
+        array, *index = term
+        if index and isinstance(index[0], slice):
+            count = index[0].stop - index[0].start
+            return (count,) + array.shape[1:], (index[0].start // count,) + (0,) * (array.ndim - 1)
+        rest = array.shape[len(index) :]
+        return (None,) * len(index) + rest, tuple(index) + (0,) * len(rest)
+
+    def dims_of(term):
+        return tuple(d for d in block_of(term)[0] if d is not None)
+
+    def rows_of(piece):
+        found = dims_of(piece[0])
+        return found[0] if len(found) == 3 else 1
+
     for pieces in outputs:
-        first = pieces[0][0]
-        rest = first[0].shape[len(first) - 1 :]
-        dims.append(((len(pieces),) if len(pieces) > 1 else ()) + rest)
-        dtypes.append(first[0].dtype)
+        rest = dims_of(pieces[0][0])
+        if isinstance(pieces, Flat):
+            dims.append((sum(rows_of(piece) for piece in pieces),) + rest[-2:])
+        else:
+            dims.append(((len(pieces),) if len(pieces) > 1 else ()) + rest)
+        dtypes.append(pieces[0][0][0].dtype)
         terms += [term for piece in pieces for term in piece]
 
     def spec(term):
-        array, *index = term
-        rest = array.shape[len(index) :]
-        return pl.BlockSpec((None,) * len(index) + rest, lambda i, sc: (*index, *(0 for _ in rest)))
+        block, index = block_of(term)
+        return pl.BlockSpec(block, lambda i, sc: index)
 
     def body(sc, *refs):
         given = iter(refs[: len(terms)])
         for out, pieces in zip(refs[len(terms) :], outputs):
+            at = 0
             for n, piece in enumerate(pieces):
                 value = next(given)[...].astype(F32)
                 for _ in piece[1:]:
                     value = value + next(given)[...].astype(F32)
-                if len(pieces) > 1:
-                    out[n] = value.astype(out.dtype)
+                value = value.astype(out.dtype)
+                if isinstance(pieces, Flat):
+                    rows = rows_of(piece)
+                    if len(value.shape) == 3:
+                        out[at : at + rows] = value
+                    else:
+                        out[at] = value
+                    at += rows
+                elif len(pieces) > 1:
+                    out[n] = value
                 else:
-                    out[...] = value.astype(out.dtype)
+                    out[...] = value
 
     return call(
         body,
@@ -712,27 +788,29 @@
     return share, far, near, to_core(far)
 
 
-def unpack_body(sc, *refs):
-    (final_keep, final_got, input_keep, input_got, small), shares, outs = refs[:5], refs[5:25], refs[25:]
-    final, inputs, up, down, qkv, out, a_gain, a_shift, b_out, f_gain, f_shift, b_down, b_up = outs
+def unpack_body(shares, sc, *refs):
+    (final_keep, final_got, input_keep, input_got, small), refs = refs[:5], refs[5:]
+    final, inputs, up, down, qkv, out, a_gain, a_shift, b_out, f_gain, f_shift, b_down, b_up = refs[-13:]
     x = sc[X]
     for ref, mine, got in ((final, final_keep, final_got), (inputs, input_keep, input_got)):
         ref[x, 0] = mine[...]
         ref[1 - x, 0] = got[...].astype(F32)
     for layer in range(2):
-        ffn, qv, ko = shares[10 * layer : 10 * layer + 4], shares[10 * layer + 4 : 10 * layer + 8], shares[10 * layer + 8 : 10 * layer + 10]
+        ffn, qv, ko = shares[layer]
         for n in range(4):
             x, core = sc[X] ^ (n % 2), sc[C] ^ (n // 2)
             for j in range(2):
                 at = pl.multiple_of(x * 4 * HALF + core * 2 * HALF + j * HALF, PAIR)
-                up[layer, :, pl.ds(at, HALF)] = ffn[n][j].astype(F32)
+                up[layer, :, pl.ds(at, HALF)] = refs[ffn[n]][j].astype(F32)
                 rows = pl.ds(pl.multiple_of(core * 2 * PART + j * PART, 8), PART)
-                down[layer, rows, pl.ds(pl.multiple_of(x * HALF, PAIR), HALF)] = ffn[n][2 + j].astype(F32)
-            qkv[layer, :, pl.ds(pl.multiple_of(x * 2 * D + core * HALF, PAIR), HALF)] = qv[n][...].astype(F32)
+                down[layer, rows, pl.ds(pl.multiple_of(x * HALF, PAIR), HALF)] = refs[ffn[n]][2 + j].astype(F32)
+            index, at = qv[n]
+            value = refs[index][...] if at is None else refs[index][at]
+            qkv[layer, :, pl.ds(pl.multiple_of(x * 2 * D + core * HALF, PAIR), HALF)] = value.astype(F32)
         for n in range(2):
             side = pl.multiple_of((sc[C] ^ n) * HALF, PAIR)
-            qkv[layer, :, pl.ds(pl.multiple_of(D + side, PAIR), HALF)] = ko[n][0].astype(F32)
-            out[layer, :, pl.ds(side, HALF)] = ko[n][1].astype(F32)
+            qkv[layer, :, pl.ds(pl.multiple_of(D + side, PAIR), HALF)] = refs[ko[n]][0].astype(F32)
+            out[layer, :, pl.ds(side, HALF)] = refs[ko[n]][1].astype(F32)
     piece = 2 * sc[Z] + sc[Y]
     mine = jnp.zeros((32, PART), F32)
     for d in range(8):
@@ -748,18 +826,18 @@
         b_up[layer : layer + 1] = row
 
 
-def unpacked(scalars, rows, small, shares):
+def unpacked(scalars, rows, small, arrays, shares):
     moved = ((2, 1, BLOCK, D),) * 2
     dims = ((2, PART, FF), (2, 4 * PART, D), (2, PART, 3 * D), (2, PART, D)) + ((2, PART),) * 6 + ((2, 4 * PART),)
     return call(
-        unpack_body,
+        partial(unpack_body, shares),
         (1,),
-        [whole((BLOCK, D))] * 4 + [whole((32, D))] + [whole(share.shape) for share in shares],
+        [whole((BLOCK, D))] * 4 + [whole((32, D))] + [whole(array.shape) for array in arrays],
         [whole(d) for d in moved + dims],
         [shape(d, F32) for d in moved + dims],
         [],
         (1e6, 11e6),
-    )(scalars, *rows, small, *shares)
+    )(scalars, *rows, small, *arrays)
 
 
 def on_device(
@@ -815,18 +893,18 @@
         )
         ctx_rcv = to_core(ctx_oth)
         ctx_far = to_core(ctx_own)
-        s2, ctx_full, act, slope, *result = ffn_forward(
-            scalars,
-            layer,
-            layer == 1,
-            ctx_own,
-            ctx_rcv,
-            own,
-            own_spec,
-            (out_weight, b_out, f_gain, f_shift, up_weight, b_up, down_weight, b_down),
-            None if layer == 0 else kept[0][7],
-        )
-        s2_o = to_chip(s2)
+        ffn = (f_gain, f_shift, up_weight, b_up, down_weight, b_down)
+        if layer == 0:
+            s2, ctx_full, act, slope, *result = ffn_forward(
+                scalars, layer, ctx_own, ctx_rcv, own, own_spec, (out_weight, b_out) + ffn, ()
+            )
+            s2_o = to_chip(s2)
+        else:
+            s2, ctx_full = projected(
+                scalars, layer, ctx_own, ctx_rcv, own, own_spec, out_weight, b_out, (kept[0][7], kept[0][11])
+            )
+            s2_o = to_chip(s2)
+            act, slope, *result = last_ffn_forward(scalars, layer, s2, ffn)
         kept.append((own, own_spec, other, other_spec, qkv, ctx, ctx_oth, ctx_far, ctx_full, lse, s2, s2_o, act, slope))
         if layer == 0:
             s3 = result[0]
@@ -880,12 +958,12 @@
         def share(keep, got, y_got, z_got, far_got):
             return [[(keep, 0, 0), (got, 0, 0), (y_got, 0), (z_got, 0), (far_got,)]]
 
-        dh1, ds1, f_small1 = ffn_back(1, cot, own_in, [kept[0][11], kept[1][7]])
+        dh1, ds1, f_small1 = ffn_back(1, cot, own_in, [kept[1][7]])
         ds1_rcv = to_core(ds1)
         fk1, send = ffn_grads(1, cot, own_in, cot, far_in, dh1)
         pinned.append(fk1)
         fg1 = to_core(send)
-        d_qkv1, part1, part1_oth = attn_back(1, ds1, ds1_rcv, [fk1])
+        d_qkv1, part1, part1_oth = attn_back(1, ds1, ds1_rcv, [from_hbm(fk1)])
         part1_rcv = to_core(part1_oth)
         value, final_low = summed(y_sum(fk1, fg1), [[(final_send,)]], deps=[part1])
         fy1 = to_dp(value, 1)
@@ -895,80 +973,83 @@
         ds0_rcv = to_core(ds0)
         fk0, send = ffn_grads(0, rows5(g0), local, rows5(g0_o), local, dh0)
         pinned.append(fk0)
-        (fz1,) = summed(z_sum(fk1, fg1, fy1), deps=[fk0])
+        (fz1,) = summed(z_sum(fk1, fg1, fy1), deps=[from_hbm(fk0)])
         fg0 = to_core(send)
         qk1, send, ok1, z_send = attn_grads(1, ds1, ds1_rcv, d_qkv1, [fz1])
         pinned += [qk1, ok1]
         qg1, og1 = to_chip(send), to_dp(z_send, 2)
-        fy0, final_low = summed(y_sum(fk0, fg0), [[(final_low,)]], deps=[qk1])
+        fy0, final_low = summed(y_sum(fk0, fg0), [[(final_low,)]], deps=[from_hbm(qk1)])
         d_qkv0, part0, part0_oth = attn_back(0, ds0, ds0_rcv, [fy0])
         final_got = to_chip(final_low)
         fz1, fy0 = to_dp(fz1, 2), to_dp(fy0, 1)
         part0_rcv = to_core(part0_oth)
-        far1, oy1, qy1 = summed(
+        far1, y1 = summed(
             far_sum(fk1, fg1, fy1, fz1),
-            [[(ok1, 0, 1), (og1, 0, 1)], [(ok1, 1, 1), (og1, 1, 1)]],
-            y_sum(qk1, qg1),
+            Flat([[(ok1, 0, 1), (og1, 0, 1)], [(ok1, 1, 1), (og1, 1, 1)]] + y_sum(qk1, qg1)),
             deps=[part0],
         )
         input_keep, input_send, small = attn_norm(
             0, ds0, part0, part0_rcv, (a_small1, f_small0, f_small1), [far1, final_got]
         )
-        far1, oy1, qy1 = to_dp(far1, 4), to_dp(oy1, 1), to_dp(qy1, 1)
+        far1, y1 = to_dp(far1, 4), to_dp(y1, 1)
         small_got = to_core(small)
         input_got = to_chip(input_send)
         fz0, small = summed(z_sum(fk0, fg0, fy0), [[(small,), (small_got,)]], deps=[input_keep])
         qk0, send, ok0, y_send = attn_grads(0, ds0, ds0_rcv, d_qkv0, [fz0])
-        fz0, small_got = to_dp(fz0, 2), to_dp(small, 1)
+        fz0, small_got = to_dp(fz0, 2), to_dp(small, 4)
         pinned += [qk0, ok0]
         qg0, oy0 = to_chip(send), to_dp(y_send, 1)
 
-        of1, qz1, far0, f1, small = summed(
-            [[(ok1, 1, 0), (og1, 1, 0), (oy1, 1)]],
-            z_sum(qk1, qg1, qy1),
-            far_sum(fk0, fg0, fy0, fz0),
+        far, qz1, f1, small = summed(
+            Flat(far_sum(fk0, fg0, fy0, fz0) + [[(ok1, 1, 0), (og1, 1, 0), (y1, slice(2, 4))]]),
+            [[(qk1, 0, k), (qg1, 0, k), (y1, 4 + k)] for k in (1, 3)],
             share(fk1, fg1, fy1, fz1, far1),
             [[(small,), (small_got,)]],
-            deps=[qk0],
-        )
-        of1, qz1, far0, small_got = to_dp(of1, 4), to_dp(qz1, 2), to_dp(far0, 4), to_dp(small, 2)
+            deps=[from_hbm(qk0)],
+        )
+        far, qz1, small_got = to_dp(far, 4), to_dp(qz1, 2), to_dp(small, 1)
         f1_all = gathered(f1)
 
-        qy0, oz_1, oz_2, oz_3, ox1, qf1, small = summed(
+        qy0, oz0, qf1, small = summed(
             y_sum(qk0, qg0),
-            *[[[(ok0, k), (oy0, k)]] for k in (1, 2, 3)],
-            [[(ok1, 0, 0), (og1, 0, 0), (oy1, 0), (of1,)]],
-            far_sum(qk1, qg1, qy1, qz1),
+            [[(ok0, k), (oy0, k)] for k in (1, 3)],
+            [[(qk1, 0, 2), (qg1, 0, 2), (y1, 6), (qz1, 1)]],
             [[(small,), (small_got,)]],
             deps=[input_got],
         )
-        qy0, ox1_got, qf1, small_got = to_dp(qy0, 1), to_chip(ox1), to_dp(qf1, 4), to_dp(small, 4)
-        oz0 = [to_dp(value, 2 * k) for k, value in ((1, oz_1), (2, oz_2), (3, oz_3))]
-
-        qz_1, qz_2, qz_3, ox0, f0, q1, o1, small = summed(
-            *[[[(qk0, 0, k), (qg0, 0, k), (qy0, k)]] for k in (1, 2, 3)],
-            [[(ok0, 0), (oy0, 0)] + [(got,) for got in oz0]],
-            share(fk0, fg0, fy0, fz0, far0),
-            share(qk1, qg1, qy1, qz1, qf1),
+        qy0, oz0, qf1, small_got = to_dp(qy0, 1), to_dp(oz0, 2), to_dp(qf1, 4), to_chip(small)
+
+        of0, qz0, f0, ox1, small = summed(
+            [[(ok0, 2), (oy0, 2), (oz0, 1)]],
+            z_sum(qk0, qg0, qy0),
+            [[(fk0, 0, 0), (fg0, 0, 0), (fy0, 0), (fz0, 0), (far, slice(0, 4))]],
+            [[(ok1, 0, 0), (og1, 0, 0), (y1, slice(0, 2)), (far, slice(4, 6))]],
+            [[(small,), (small_got,)]],
+            deps=f1_all[1:],
+        )
+        of0, qz0, ox1_got, small_got = to_dp(of0, 4), to_dp(qz0, 2), to_chip(ox1), to_dp(small, 2)
+        f0_all = gathered(f0)
+
+        qf0, ox0, o1, small = summed(
+            far_sum(qk0, qg0, qy0, qz0),
+            [[(ok0, 0), (oy0, 0), (oz0, 0), (of0,)]],
             [[(ox1,), (ox1_got,)]],
             [[(small,), (small_got,)]],
-            deps=f1_all[1:],
-        )
-        ox0_got, small_got = to_chip(ox0), to_chip(small)
-        qz0 = [to_dp(value, 2 * k) for k, value in ((1, qz_1), (2, qz_2), (3, qz_3))]
-        f0_all, a1_all = gathered(f0), gathered(q1) + (o1, to_core(o1))
-
-        q0, o0, small = summed(
-            [[(qk0, 0, 0), (qg0, 0, 0), (qy0, 0)] + [(got,) for got in qz0]],
+        )
+        qf0, ox0_got = to_dp(qf0, 4), to_chip(ox0)
+
+        both, o0 = summed(
+            share(qk0, qg0, qy0, qz0, qf0) + [[(qk1, 0, 0), (qg1, 0, 0), (y1, 4), (qz1, 0), (qf1,)]],
             [[(ox0,), (ox0_got,)]],
-            [[(small,), (small_got,)]],
-        )
-        a0_all = gathered(q0) + (o0, to_core(o0))
+            deps=f0_all[1:],
+        )
+        arrays = f0_all + f1_all + gathered(both) + (o0, to_core(o0), o1, to_core(o1))
+        shares = (
+            ((0, 1, 2, 3), tuple((n, 0) for n in range(8, 12)), (12, 13)),
+            ((4, 5, 6, 7), tuple((n, 1) for n in range(8, 12)), (14, 15)),
+        )
         (final_out, input_out, ups, downs, qkvs, outs, *vectors) = unpacked(
-            scalars,
-            (final_keep, final_got, input_keep, input_got),
-            small,
-            f0_all + a0_all + f1_all + a1_all,
+            scalars, (final_keep, final_got, input_keep, input_got), small, arrays, shares
         )
         g_a_gain, g_a_shift, g_b_out, g_f_gain, g_f_shift, g_b_down, g_b_up = vectors
     else:

time: 343 us -> 310 us (0.904)
  waiting for transfers between devices: 66.1 us -> 52.6 us
  Pallas kernels: 207 us -> 199 us
  local copies, waits for them, and re-layouts: 10.6 us -> 4.89 us
  starting transfers between devices: 51.8 us -> 46.6 us
    ppermute x14 -> x13, waiting for transfers between devices: 29.1 us -> 16.1 us  [to_chip(): return lax.ppermute(value, 'section', [(0, 2), (2, 0), (1, 3), (3, 1)])]
    pallas_call x24 -> x26, Pallas kernels: 207 us -> 199 us  [call(): return lambda *args: kernel(*args, *deps)]
    unnamed x74 -> x66, local copies, waits for them, and re-layouts: 9.19 us -> 3.46 us
    ppermute x14 -> x13, starting transfers between devices: 18.4 us -> 14.5 us  [to_chip(): return lax.ppermute(value, 'section', [(0, 2), (2, 0), (1, 3), (3, 1)])]
    ppermute x23 -> x19, waiting for transfers between devices: 32.7 us -> 34.5 us  [to_dp(): return lax.ppermute(value, 'dp', [(i, i ^ distance) for i in range(8)])]
    ppermute x23 -> x19, starting transfers between devices: 29 us -> 28.2 us  [to_dp(): return lax.ppermute(value, 'dp', [(i, i ^ distance) for i in range(8)])]
  transfers between devices with their start and end apart: 59 -> 52, of which waited for: 17 -> 13; matrix products, arithmetic and copies ran while one was open for 0% -> 0% of each run, Pallas kernels for 51% -> 53%
where the time goes in v2:
time: 310 us; the launch traced here: 304 us
  Pallas kernels  199 us (64%)
  waiting for transfers between devices  52.6 us (17%)
  starting transfers between devices  46.6 us (15%)
  local copies, waits for them, and re-layouts  4.89 us (2%)
    pallas_call x26, Pallas kernels, call(): return lambda *args: kernel(*args, *deps)  199 us
    ppermute x19, waiting for transfers between devices, to_dp(): return lax.ppermute(value, 'dp', [(i, i ^ distance) for i in range(8)])  34.5 us
    ppermute x19, starting transfers between devices, to_dp(): return lax.ppermute(value, 'dp', [(i, i ^ distance) for i in range(8)])  28.2 us
    ppermute x13, waiting for transfers between devices, to_chip(): return lax.ppermute(value, 'section', [(0, 2), (2, 0), (1, 3), (3, 1)])  16.1 us
    ppermute x13, starting transfers between devices, to_chip(): return lax.ppermute(value, 'section', [(0, 2), (2, 0), (1, 3), (3, 1)])  14.5 us
  transfers between devices with their start and end apart: 52, of which 13 were waited for; matrix products, arithmetic and copies ran while one was open for 0% of the time, Pallas kernels for 53%

profile of v2, /device:TPU:0, one launch (start us, length us, event | category | flops | bytes accessed | tf_op | source)
XLA Modules:
  0.0 304.5 jit_solution(5566131045705605294)
XLA Ops:
  4.8 14.8 %shard_map.237 = (bf16[1024,1152]{1,0:T(8,128)(2,1)}, bf16[1024,384]{1,0:T(8,128)(2,1)}, bf16[2,256,384]{2,1,0:T(8,128)(2,1)S(1)}, bf16[2,256,384]{2,1,0:T(8,128)(2,1)S(1)}, f32[8,1024]{1,0:T(8,128)S(1)}) custom-call(s32[4]{0:T(128)S(1)} %pad_add_fusion.sc, bf16[2,2,2,256,768]{4,3,2,1,0:T(8,128)(2,1)S(1)} %bitcast.10, ...), custom_call_target="tpu_custom_call" | custom-call | flops 20999999488 | bytes 40000000 | tf_op jit(solution)/shard_map/pallas_call | solution.py:69
  21.4 13.2 %shard_map.238 = (bf16[512,768]{1,0:T(8,128)(2,1)S(1)}, bf16[512,768]{1,0:T(8,128)(2,1)S(1)}, bf16[512,3072]{1,0:T(8,128)(2,1)}, bf16[512,3072]{1,0:T(8,128)(2,1)}, bf16[2,256,768]{2,1,0:T(8,128)(2,1)S(1)}) custom-call(s32[4]{0:T(128)S(1)} %pad_add_fusion.sc, bf16[2,256,384]{2,1,0:T(8,128)(2,1)S(1)} %get-tuple-element.103.refs_0_, ...), custom_call_target="tpu_custom_call" | custom-call | flops 27000000512 | bytes 100000000 | tf_op jit(solution)/shard_map/pallas_call | solution.py:69
  38.1 14.9 %shard_map.239 = (bf16[1024,1152]{1,0:T(8,128)(2,1)}, bf16[1024,384]{1,0:T(8,128)(2,1)}, bf16[2,256,384]{2,1,0:T(8,128)(2,1)S(1)}, bf16[2,256,384]{2,1,0:T(8,128)(2,1)S(1)}, f32[8,1024]{1,0:T(8,128)S(1)}) custom-call(s32[4]{0:T(128)S(1)} %pad_add_fusion.sc, bf16[1,2,1,256,768]{4,3,2,1,0:T(8,128)(2,1)S(1)} %bitcast.16, ...), custom_call_target="tpu_custom_call" | custom-call | flops 20999999488 | bytes 40000000 | tf_op jit(solution)/shard_map/pallas_call | solution.py:69
  60.5 10.9 %shard_map.241 = (bf16[512,3072]{1,0:T(8,128)(2,1)S(1)}, bf16[512,3072]{1,0:T(8,128)(2,1)S(1)}, f32[256,768]{1,0:T(8,128)S(1)}, bf16[256,768]{1,0:T(8,128)(2,1)S(1)}) custom-call(s32[4]{0:T(128)S(1)} %pad_add_fusion.sc, bf16[512,768]{1,0:T(8,128)(2,1)S(1)} %get-tuple-element.109.refs_0_.refs_1_.refs_2_, ...), custom_call_target="tpu_custom_call" | custom-call | flops 24000000000 | bytes 90000000 | tf_op jit(solution)/shard_map/pallas_call | solution.py:69
  71.4 10.2 %shard_map.242 = (bf16[512,3072]{1,0:T(8,128)(2,1)S(1)}, bf16[2,256,768]{2,1,0:T(8,128)(2,1)S(1)}, f32[8,768]{1,0:T(8,128)S(1)}) custom-call(s32[4]{0:T(128)S(1)} %pad_add_fusion.sc, bf16[2,2,2,256,768]{4,3,2,1,0:T(8,128)(2,1)S(1)} %bitcast.20, bf16[512,768]{1,0:T(8,128)(2,1)S(1)} %get-tuple-element.109.refs_0_.refs_1_.refs_2_, ...), custom_call_target="tpu_custom_call" | custom-call | flops 24500000768 | bytes 90000000 | tf_op jit(solution)/shard_map/pallas_call | solution.py:69
  81.7 19.8 %shard_map.243 = (bf16[2,4,4,96,384]{4,3,2,1,0:T(8,128)(2,1)}, bf16[2,4,4,96,384]{4,3,2,1,0:T(8,128)(2,1)S(1)}) custom-call(s32[4]{0:T(128)S(1)} %pad_add_fusion.sc, bf16[2,2,2,256,768]{4,3,2,1,0:T(8,128)(2,1)S(1)} %bitcast.21, bf16[2,2,2,256,768]{4,3,2,1,0:T(8,128)(2,1)S(1)} %bitcast.22, bf16[512,768]{1,0:T(8,128)(2,1)S(1)} %get-tuple-element.109.refs_0_.refs_1_.refs_2_, ...), custom_call_target="tpu_custom_call" | custom-call | flops 43000000512 | bytes 110000000 | tf_op jit(solution)/shard_map/pallas_call | solution.py:69
  102.0 18.7 %shard_map.244 = (bf16[1024,1152]{1,0:T(8,128)(2,1)S(1)}, f32[2,256,768]{2,1,0:T(8,128)S(1)}, bf16[2,256,768]{2,1,0:T(8,128)(2,1)S(1)}) custom-call(s32[4]{0:T(128)S(1)} %pad_add_fusion.sc, bf16[2,256,768]{2,1,0:T(8,128)(2,1)S(1)} %get-tuple-element.112.refs_0_.refs_5_, bf16[2,256,768]{2,1,0:T(8,128)(2,1)S(1)} %collective-permute-done.6.refs_1_.refs_6_, ...), custom_call_target="tpu_custom_call" | custom-call | flops 42500001792 | bytes 60000000 | tf_op jit(solution)/shard_map/pallas_call | solution.py:69
  127.0 11.5 %shard_map.247 = (bf16[512,3072]{1,0:T(8,128)(2,1)S(1)}, bf16[2,256,768]{2,1,0:T(8,128)(2,1)}, f32[8,768]{1,0:T(8,128)S(1)}) custom-call(s32[4]{0:T(128)S(1)} %pad_add_fusion.sc, bf16[1,2,1,256,768]{4,3,2,1,0:T(8,128)(2,1)S(1)} %bitcast.25, bf16[512,768]{1,0:T(8,128)(2,1)S(1)} %copy-done.12, f32[2,1,768]{2,1,0:T(1,128)S(1)} %reshape.70.refs_5_.refs_1_.refs_2_.refs_4_, ...), custom_call_target="tpu_custom_call" | custom-call | flops 24500000768 | bytes 90000000 | tf_op jit(solution)/shard_map/pallas_call | solution.py:69
  138.5 7.6 %collective-permute-done.10 = bf16[2,256,768]{2,1,0:T(8,128)(2,1)S(1)} collective-permute-done((bf16[2,256,768]{2,1,0:T(8,128)(2,1)S(1)}, bf16[2,256,768]{2,1,0:T(8,128)(2,1)S(1)}, u32[]{:S(2)}, u32[]{:S(2)}) %collective-permute-start.10) | collective-permute-done | bytes 786464 | tf_op jit(solution)/shard_map/ppermute | solution.py:700
  146.1 19.5 %shard_map.248 = (bf16[2,4,4,96,384]{4,3,2,1,0:T(8,128)(2,1)}, bf16[2,4,4,96,384]{4,3,2,1,0:T(8,128)(2,1)S(1)}) custom-call(s32[4]{0:T(128)S(1)} %pad_add_fusion.sc, bf16[1,2,1,256,768]{4,3,2,1,0:T(8,128)(2,1)S(1)} %bitcast.26, bf16[1,2,1,256,768]{4,3,2,1,0:T(8,128)(2,1)S(1)} %bitcast.27, bf16[512,768]{1,0:T(8,128)(2,1)S(1)} %copy-done.12, ...), custom_call_target="tpu_custom_call" | custom-call | flops 43000000512 | bytes 110000000 | tf_op jit(solution)/shard_map/pallas_call | solution.py:69
  169.3 6.2 %shard_map.250 = (bf16[2,4,96,384]{3,2,1,0:T(8,128)(2,1)}, bf16[2,4,96,384]{3,2,1,0:T(8,128)(2,1)S(1)}, bf16[2,2,2,96,384]{4,3,2,1,0:T(8,128)(2,1)}, bf16[2,2,2,96,384]{4,3,2,1,0:T(8,128)(2,1)S(1)}) custom-call(s32[4]{0:T(128)S(1)} %pad_add_fusion.sc, bf16[1,2,1,256,768]{4,3,2,1,0:T(8,128)(2,1)S(1)} %bitcast.19, bf16[1,2,1,256,768]{4,3,2,1,0:T(8,128)(2,1)S(1)} %bitcast.24, ...), custom_call_target="tpu_custom_call" | custom-call | flops 12499999744 | bytes 60000000 | tf_op jit(solution)/shard_map/pallas_call | solution.py:69
  180.7 19.2 %shard_map.252 = (bf16[1024,1152]{1,0:T(8,128)(2,1)S(1)}, f32[2,256,768]{2,1,0:T(8,128)S(1)}, bf16[2,256,768]{2,1,0:T(8,128)(2,1)S(1)}) custom-call(s32[4]{0:T(128)S(1)} %pad_add_fusion.sc, bf16[2,256,768]{2,1,0:T(8,128)(2,1)} %get-tuple-element.135.refs_0_.refs_5_, bf16[2,256,768]{2,1,0:T(8,128)(2,1)} %collective-permute-done.14.refs_1_.refs_6_, ...), custom_call_target="tpu_custom_call" | custom-call | flops 42500001792 | bytes 60000000 | tf_op jit(solution)/shard_map/pallas_call | solution.py:69
  202.3 3.0 %shard_map.254 = (f32[256,768]{1,0:T(8,128)S(1)}, bf16[256,768]{1,0:T(8,128)(2,1)S(1)}, f32[32,768]{1,0:T(8,128)S(1)}) custom-call(s32[4]{0:T(128)S(1)} %pad_add_fusion.sc, bf16[2,256,768]{2,1,0:T(8,128)(2,1)} %get-tuple-element.135.refs_0_.refs_5_, f32[2,256,768]{2,1,0:T(8,128)S(1)} %get-tuple-element.140.refs_10_.refs_1_, ...), custom_call_target="tpu_custom_call" | custom-call | flops 1000000000 | bytes 25000000 | tf_op jit(solution)/shard_map/pallas_call | solution.py:69
  214.4 7.5 %shard_map.256 = (bf16[2,4,96,384]{3,2,1,0:T(8,128)(2,1)}, bf16[2,4,96,384]{3,2,1,0:T(8,128)(2,1)S(1)}, bf16[4,2,96,384]{3,2,1,0:T(8,128)(2,1)}, bf16[4,2,96,384]{3,2,1,0:T(8,128)(2,1)S(1)}) custom-call(s32[4]{0:T(128)S(1)} %pad_add_fusion.sc, bf16[2,2,2,256,768]{4,3,2,1,0:T(8,128)(2,1)S(1)} %bitcast.14, bf16[2,2,2,256,768]{4,3,2,1,0:T(8,128)(2,1)S(1)} %bitcast.15, ...), custom_call_target="tpu_custom_call" | custom-call | flops 12499999744 | bytes 60000000 | tf_op jit(solution)/shard_map/pallas_call | solution.py:69
  221.9 3.3 %collective-permute-done.26.refs_17_ = bf16[4,96,384]{2,1,0:T(8,128)(2,1)S(1)} collective-permute-done((bf16[4,96,384]{2,1,0:T(8,128)(2,1)S(1)}, bf16[4,96,384]{2,1,0:T(8,128)(2,1)S(1)}, u32[]{:S(2)}, u32[]{:S(2)}) %collective-permute-start.26) | collective-permute-done | bytes 294944 | tf_op jit(solution)/shard_map/ppermute | solution.py:704
  227.3 7.1 %collective-permute-done.25.refs_3_.refs_12_ = bf16[2,4,96,384]{3,2,1,0:T(8,128)(2,1)S(1)} collective-permute-done((bf16[2,4,96,384]{3,2,1,0:T(8,128)(2,1)S(1)}, bf16[2,4,96,384]{3,2,1,0:T(8,128)(2,1)S(1)}, u32[]{:S(2)}, u32[]{:S(2)}) %collective-permute-start.25) | collective-permute-done | bytes 589856 | tf_op jit(solution)/shard_map/ppermute | solution.py:704
  238.7 5.1 %collective-permute-start.32 = (bf16[6,96,384]{2,1,0:T(8,128)(2,1)S(1)}, bf16[6,96,384]{2,1,0:T(8,128)(2,1)S(1)}, u32[]{:S(2)}, u32[]{:S(2)}) collective-permute-start(bf16[6,96,384]{2,1,0:T(8,128)(2,1)S(1)} %get-tuple-element.165), channel_id=1, source_target_pairs={{0,4},{1,5},{2,6},{3,7},{4,0},{5,1},{6,2},{7,3},{8,12},{9,13},{10,... | collective-permute-start | bytes 1327112 | tf_op jit(solution)/shard_map/ppermute | solution.py:704
  251.0 4.7 %collective-permute-done.30.refs_5_.refs_8_.refs_2_ = bf16[4,96,384]{2,1,0:T(8,128)(2,1)S(1)} collective-permute-done((bf16[4,96,384]{2,1,0:T(8,128)(2,1)S(1)}, bf16[4,96,384]{2,1,0:T(8,128)(2,1)S(1)}, u32[]{:S(2)}, u32[]{:S(2)}) %collective-permute-start.30) | collective-permute-done | bytes 294944 | tf_op jit(solution)/shard_map/ppermute | solution.py:704
  255.7 8.1 %collective-permute-done.31.refs_2_.refs_6_ = bf16[2,2,96,384]{3,2,1,0:T(8,128)(2,1)S(1)} collective-permute-done((bf16[2,2,96,384]{3,2,1,0:T(8,128)(2,1)S(1)}, bf16[2,2,96,384]{3,2,1,0:T(8,128)(2,1)S(1)}, u32[]{:S(2)}, u32[]{:S(2)}) %collective-permute-start.31) | collective-permute-done | bytes 294944 | tf_op jit(solution)/shard_map/ppermute | solution.py:704
  267.5 4.8 %collective-permute-start.38 = (bf16[2,96,384]{2,1,0:T(8,128)(2,1)S(1)}, bf16[2,96,384]{2,1,0:T(8,128)(2,1)S(1)}, u32[]{:S(2)}, u32[]{:S(2)}) collective-permute-start(bf16[2,96,384]{2,1,0:T(8,128)(2,1)S(1)} %get-tuple-element.169), channel_id=1, source_target_pairs={{0,4},{1,5},{2,6},{3,7},{4,0},{5,1},{6,2},{7,3},{8,12},{9,13},{10,... | collective-permute-start | bytes 442376 | tf_op jit(solution)/shard_map/ppermute | solution.py:704
  273.5 4.6 %collective-permute-done.40.refs_11_ = f32[32,768]{1,0:T(8,128)S(1)} collective-permute-done((f32[32,768]{1,0:T(8,128)S(1)}, f32[32,768]{1,0:T(8,128)S(1)}, u32[]{:S(2)}, u32[]{:S(2)}) %collective-permute-start.40) | collective-permute-done | bytes 98336 | tf_op jit(solution)/shard_map/ppermute | solution.py:704
  284.1 5.7 %collective-permute-done.45.refs_9_ = bf16[96,384]{1,0:T(8,128)(2,1)S(1)} collective-permute-done((bf16[96,384]{1,0:T(8,128)(2,1)S(1)}, bf16[96,384]{1,0:T(8,128)(2,1)S(1)}, u32[]{:S(2)}, u32[]{:S(2)}) %collective-permute-start.45) | collective-permute-done | bytes 73760 | tf_op jit(solution)/shard_map/ppermute | solution.py:704
  294.1 3.5 %collective-permute-done.47.refs_14_ = bf16[2,96,384]{2,1,0:T(8,128)(2,1)S(1)} collective-permute-done((bf16[2,96,384]{2,1,0:T(8,128)(2,1)S(1)}, bf16[2,96,384]{2,1,0:T(8,128)(2,1)S(1)}, u32[]{:S(2)}, u32[]{:S(2)}) %collective-permute-start.47) | collective-permute-done | bytes 147488 | tf_op jit(solution)/shard_map/ppermute | solution.py:700
  299.0 5.0 %shard_map.262 = (f32[2,1,256,768]{3,2,1,0:T(8,128)}, f32[2,1,256,768]{3,2,1,0:T(8,128)}, f32[2,96,3072]{2,1,0:T(8,128)}, f32[2,384,768]{2,1,0:T(8,128)}, f32[2,...) custom-call(s32[4]{0:T(128)S(1)} %pad_add_fusion.sc, ...), custom_call_target="tpu_custom_call" | custom-call | flops 5000000 | bytes 55000000 | tf_op jit(solution)/shard_map/pallas_call | solution.py:69
  (180 shorter events, 73.8 us)
Async XLA Ops:
  35.1 18.5 %collective-permute-start.3 = (bf16[2,256,384]{2,1,0:T(8,128)(2,1)S(1)}, bf16[2,256,384]{2,1,0:T(8,128)(2,1)S(1)}, u32[]{:S(2)}, u32[]{:S(2)}) collective-permute-start(bf16[2,256,384]{2,1,0:T(8,128)(2,1)S(1)} %get-tuple-element.103.refs_0_), channel_id=1, source_target_pairs={{0,8},{8,0},{16,24},{24,16},{1,9},{9,1},{17,25},{25,17},{2,10},{10... | collective-permute-start | bytes 1179656 | tf_op jit(solution)/shard_map/ppermute | solution.py:696
  35.3 20.7 %collective-permute-start.4 = (bf16[512,768]{1,0:T(8,128)(2,1)S(1)}, bf16[512,768]{1,0:T(8,128)(2,1)S(1)}, u32[]{:S(2)}, u32[]{:S(2)}) collective-permute-start(bf16[512,768]{1,0:T(8,128)(2,1)S(1)} %get-tuple-element.108.refs_1_.refs_2_), channel_id=1, source_target_pairs={{0,16},{16,0},{8,24},{24,8},{1,17},{17,1},{9,25},{25,9},{2,18},{18... | collective-permute-start | bytes 2359304 | tf_op jit(solution)/shard_map/ppermute | solution.py:700
  53.1 18.3 %collective-permute-start.5 = (bf16[2,256,384]{2,1,0:T(8,128)(2,1)S(1)}, bf16[2,256,384]{2,1,0:T(8,128)(2,1)S(1)}, u32[]{:S(2)}, u32[]{:S(2)}) collective-permute-start(bf16[2,256,384]{2,1,0:T(8,128)(2,1)S(1)} %get-tuple-element.106.refs_0_), channel_id=1, source_target_pairs={{0,8},{8,0},{16,24},{24,16},{1,9},{9,1},{17,25},{25,17},{2,10},{10... | collective-permute-start | bytes 1179656 | tf_op jit(solution)/shard_map/ppermute | solution.py:696
  58.7 23.1 %collective-permute-start.7 = (bf16[512,768]{1,0:T(8,128)(2,1)S(1)}, bf16[512,768]{1,0:T(8,128)(2,1)S(1)}, u32[]{:S(2)}, u32[]{:S(2)}) collective-permute-start(bf16[512,768]{1,0:T(8,128)(2,1)S(1)} %get-tuple-element.109.refs_0_.refs_1_.refs_2_), channel_id=1, source_target_pairs={{0,16},{16,0},{8,24},{24,8},{1,17},{17,1},{9,25},{25,9},{2,18},{18... | collective-permute-start | bytes 2359304 | tf_op jit(solution)/shard_map/ppermute | solution.py:700
  81.6 20.4 %collective-permute-start.6 = (bf16[2,256,768]{2,1,0:T(8,128)(2,1)S(1)}, bf16[2,256,768]{2,1,0:T(8,128)(2,1)S(1)}, u32[]{:S(2)}, u32[]{:S(2)}) collective-permute-start(bf16[2,256,768]{2,1,0:T(8,128)(2,1)S(1)} %get-tuple-element.112.refs_0_.refs_5_), channel_id=1, source_target_pairs={{0,8},{8,0},{16,24},{24,16},{1,9},{9,1},{17,25},{25,17},{2,10},{10... | collective-permute-start | bytes 2359304 | tf_op jit(solution)/shard_map/ppermute | solution.py:696
  101.5 19.3 %collective-permute-start.9 = (bf16[2,4,4,96,384]{4,3,2,1,0:T(8,128)(2,1)S(1)}, bf16[2,4,4,96,384]{4,3,2,1,0:T(8,128)(2,1)S(1)}, u32[]{:S(2)}, u32[]{:S(2)}) collective-permute-start(bf16[2,4,4,96,384]{4,3,2,1,0:T(8,128)(2,1)S(1)} %get-tuple-element.121), channel_id=1, source_target_pairs={{0,8},{8,0},{16,24},{24,16},{1,9},{9,1},{17,25},{25,17},{2,10},{10... | collective-permute-start | bytes 7077896 | tf_op jit(solution)/shard_map/ppermute | solution.py:696
  122.9 42.8 %collective-permute-start.12 = (bf16[4,4,96,384]{3,2,1,0:T(8,128)(2,1)S(1)}, bf16[4,4,96,384]{3,2,1,0:T(8,128)(2,1)S(1)}, u32[]{:S(2)}, u32[]{:S(2)}) collective-permute-start(bf16[4,4,96,384]{3,2,1,0:T(8,128)(2,1)S(1)} %get-tuple-element.123.refs_5_), channel_id=1, source_target_pairs={{0,1},{1,0},{2,3},{3,2},{4,5},{5,4},{6,7},{7,6},{8,9},{9,8},{10,11... | collective-permute-start | bytes 3538952 | tf_op jit(solution)/shard_map/ppermute | solution.py:704
  126.4 19.7 %collective-permute-start.10 = (bf16[2,256,768]{2,1,0:T(8,128)(2,1)S(1)}, bf16[2,256,768]{2,1,0:T(8,128)(2,1)S(1)}, u32[]{:S(2)}, u32[]{:S(2)}) collective-permute-start(bf16[2,256,768]{2,1,0:T(8,128)(2,1)S(1)} %get-tuple-element.124), channel_id=1, source_target_pairs={{0,16},{16,0},{8,24},{24,8},{1,17},{17,1},{9,25},{25,9},{2,18},{18... | collective-permute-start | bytes 2359304 | tf_op jit(solution)/shard_map/ppermute | solution.py:700
  138.5 41.7 %collective-permute-start.14 = (bf16[2,256,768]{2,1,0:T(8,128)(2,1)}, bf16[2,256,768]{2,1,0:T(8,128)(2,1)}, u32[]{:S(2)}, u32[]{:S(2)}) collective-permute-start(bf16[2,256,768]{2,1,0:T(8,128)(2,1)} %get-tuple-element.135.refs_0_.refs_5_), channel_id=1, source_target_pairs={{0,8},{8,0},{16,24},{24,16},{1,9},{9,1},{17,25},{25,17},{2,10},{10... | collective-permute-start | bytes 2359304 | tf_op jit(solution)/shard_map/ppermute | solution.py:696
  167.7 32.3 %collective-permute-start.16 = (bf16[2,4,96,384]{3,2,1,0:T(8,128)(2,1)S(1)}, bf16[2,4,96,384]{3,2,1,0:T(8,128)(2,1)S(1)}, u32[]{:S(2)}, u32[]{:S(2)}) collective-permute-start(bf16[2,4,96,384]{3,2,1,0:T(8,128)(2,1)S(1)} %shard_map.249.refs_10_), channel_id=1, source_target_pairs={{0,2},{1,3},{2,0},{3,1},{4,6},{5,7},{6,4},{7,5},{8,10},{9,11},{10,... | collective-permute-start | bytes 1769480 | tf_op jit(solution)/shard_map/ppermute | solution.py:704
  175.5 24.3 %collective-permute-start.17 = (bf16[2,2,2,96,384]{4,3,2,1,0:T(8,128)(2,1)S(1)}, bf16[2,2,2,96,384]{4,3,2,1,0:T(8,128)(2,1)S(1)}, u32[]{:S(2)}, u32[]{:S(2)}) collective-permute-start(bf16[2,2,2,96,384]{4,3,2,1,0:T(8,128)(2,1)S(1)} %get-tuple-element.146), channel_id=1, source_target_pairs={{0,2},{1,3},{2,0},{3,1},{4,6},{5,7},{6,4},{7,5},{8,10},{9,11},{10,... | collective-permute-start | bytes 1769480 | tf_op jit(solution)/shard_map/ppermute | solution.py:704
  176.0 24.0 %collective-permute-start.18 = (bf16[2,4,96,384]{3,2,1,0:T(8,128)(2,1)S(1)}, bf16[2,4,96,384]{3,2,1,0:T(8,128)(2,1)S(1)}, u32[]{:S(2)}, u32[]{:S(2)}) collective-permute-start(bf16[2,4,96,384]{3,2,1,0:T(8,128)(2,1)S(1)} %get-tuple-element.147), channel_id=1, source_target_pairs={{0,16},{16,0},{8,24},{24,8},{1,17},{17,1},{9,25},{25,9},{2,18},{18... | collective-permute-start | bytes 1769480 | tf_op jit(solution)/shard_map/ppermute | solution.py:700
  178.6 23.7 %collective-permute-start.13 = (bf16[256,768]{1,0:T(8,128)(2,1)S(1)}, bf16[256,768]{1,0:T(8,128)(2,1)S(1)}, u32[]{:S(2)}, u32[]{:S(2)}) collective-permute-start(bf16[256,768]{1,0:T(8,128)(2,1)S(1)} %get-tuple-element.134), channel_id=1, source_target_pairs={{0,16},{16,0},{8,24},{24,8},{1,17},{17,1},{9,25},{25,9},{2,18},{18... | collective-permute-start | bytes 1179656 | tf_op jit(solution)/shard_map/ppermute | solution.py:700
  180.2 30.4 %collective-permute-start.20 = (bf16[4,4,96,384]{3,2,1,0:T(8,128)(2,1)S(1)}, bf16[4,4,96,384]{3,2,1,0:T(8,128)(2,1)S(1)}, u32[]{:S(2)}, u32[]{:S(2)}) collective-permute-start(bf16[4,4,96,384]{3,2,1,0:T(8,128)(2,1)S(1)} %get-tuple-element.139.refs_8_), channel_id=1, source_target_pairs={{0,1},{1,0},{2,3},{3,2},{4,5},{5,4},{6,7},{7,6},{8,9},{9,8},{10,11... | collective-permute-start | bytes 3538952 | tf_op jit(solution)/shard_map/ppermute | solution.py:704
  206.0 19.2 %collective-permute-start.26 = (bf16[4,96,384]{2,1,0:T(8,128)(2,1)S(1)}, bf16[4,96,384]{2,1,0:T(8,128)(2,1)S(1)}, u32[]{:S(2)}, u32[]{:S(2)}) collective-permute-start(bf16[4,96,384]{2,1,0:T(8,128)(2,1)S(1)} %get-tuple-element.148.refs_8_), channel_id=1, source_target_pairs={{0,4},{1,5},{2,6},{3,7},{4,0},{5,1},{6,2},{7,3},{8,12},{9,13},{10,... | collective-permute-start | bytes 884744 | tf_op jit(solution)/shard_map/ppermute | solution.py:704
  208.5 17.0 %collective-permute-start.24 = (bf16[8,96,384]{2,1,0:T(8,128)(2,1)S(1)}, bf16[8,96,384]{2,1,0:T(8,128)(2,1)S(1)}, u32[]{:S(2)}, u32[]{:S(2)}) collective-permute-start(bf16[8,96,384]{2,1,0:T(8,128)(2,1)S(1)} %get-tuple-element.159), channel_id=1, source_target_pairs={{0,1},{1,0},{2,3},{3,2},{4,5},{5,4},{6,7},{7,6},{8,9},{9,8},{10,11... | collective-permute-start | bytes 1769480 | tf_op jit(solution)/shard_map/ppermute | solution.py:704
  210.1 27.8 %collective-permute-start.19 = (bf16[256,768]{1,0:T(8,128)(2,1)S(1)}, bf16[256,768]{1,0:T(8,128)(2,1)S(1)}, u32[]{:S(2)}, u32[]{:S(2)}) collective-permute-start(bf16[256,768]{1,0:T(8,128)(2,1)S(1)} %get-tuple-element.150), channel_id=1, source_target_pairs={{0,16},{16,0},{8,24},{24,8},{1,17},{17,1},{9,25},{25,9},{2,18},{18... | collective-permute-start | bytes 1179656 | tf_op jit(solution)/shard_map/ppermute | solution.py:700
  212.5 14.8 %collective-permute-start.27 = (f32[32,768]{1,0:T(8,128)S(1)}, f32[32,768]{1,0:T(8,128)S(1)}, u32[]{:S(2)}, u32[]{:S(2)}) collective-permute-start(f32[32,768]{1,0:T(8,128)S(1)} %get-tuple-element.160.refs_18_), channel_id=1, source_target_pairs={{0,4},{1,5},{2,6},{3,7},{4,0},{5,1},{6,2},{7,3},{8,12},{9,13},{10,... | collective-permute-start | bytes 294920 | tf_op jit(solution)/shard_map/ppermute | solution.py:704
  212.9 21.5 %collective-permute-start.25 = (bf16[2,4,96,384]{3,2,1,0:T(8,128)(2,1)S(1)}, bf16[2,4,96,384]{3,2,1,0:T(8,128)(2,1)S(1)}, u32[]{:S(2)}, u32[]{:S(2)}) collective-permute-start(bf16[2,4,96,384]{3,2,1,0:T(8,128)(2,1)S(1)} %get-tuple-element.154.refs_10_), channel_id=1, source_target_pairs={{0,2},{1,3},{2,0},{3,1},{4,6},{5,7},{6,4},{7,5},{8,10},{9,11},{10,... | collective-permute-start | bytes 1769480 | tf_op jit(solution)/shard_map/ppermute | solution.py:704
  225.2 13.5 %collective-permute-start.22 = (bf16[2,4,96,384]{3,2,1,0:T(8,128)(2,1)S(1)}, bf16[2,4,96,384]{3,2,1,0:T(8,128)(2,1)S(1)}, u32[]{:S(2)}, u32[]{:S(2)}) collective-permute-start(bf16[2,4,96,384]{3,2,1,0:T(8,128)(2,1)S(1)} %get-tuple-element.156), channel_id=1, source_target_pairs={{0,16},{16,0},{8,24},{24,8},{1,17},{17,1},{9,25},{25,9},{2,18},{18... | collective-permute-start | bytes 1769480 | tf_op jit(solution)/shard_map/ppermute | solution.py:700
  225.5 18.3 %collective-permute-start.23 = (bf16[4,2,96,384]{3,2,1,0:T(8,128)(2,1)S(1)}, bf16[4,2,96,384]{3,2,1,0:T(8,128)(2,1)S(1)}, u32[]{:S(2)}, u32[]{:S(2)}) collective-permute-start(bf16[4,2,96,384]{3,2,1,0:T(8,128)(2,1)S(1)} %get-tuple-element.158), channel_id=1, source_target_pairs={{0,1},{1,0},{2,3},{3,2},{4,5},{5,4},{6,7},{7,6},{8,9},{9,8},{10,11... | collective-permute-start | bytes 1769480 | tf_op jit(solution)/shard_map/ppermute | solution.py:704
  237.9 13.1 %collective-permute-start.34 = (bf16[4,96,384]{2,1,0:T(8,128)(2,1)S(1)}, bf16[4,96,384]{2,1,0:T(8,128)(2,1)S(1)}, u32[]{:S(2)}, u32[]{:S(2)}) collective-permute-start(bf16[4,96,384]{2,1,0:T(8,128)(2,1)S(1)} %get-tuple-element.167.refs_9_), channel_id=1, source_target_pairs={{0,16},{16,0},{8,24},{24,8},{1,17},{17,1},{9,25},{25,9},{2,18},{18... | collective-permute-start | bytes 884744 | tf_op jit(solution)/shard_map/ppermute | solution.py:700
  238.7 25.1 %collective-permute-start.32 = (bf16[6,96,384]{2,1,0:T(8,128)(2,1)S(1)}, bf16[6,96,384]{2,1,0:T(8,128)(2,1)S(1)}, u32[]{:S(2)}, u32[]{:S(2)}) collective-permute-start(bf16[6,96,384]{2,1,0:T(8,128)(2,1)S(1)} %get-tuple-element.165), channel_id=1, source_target_pairs={{0,4},{1,5},{2,6},{3,7},{4,0},{5,1},{6,2},{7,3},{8,12},{9,13},{10,... | collective-permute-start | bytes 1327112 | tf_op jit(solution)/shard_map/ppermute | solution.py:704
  250.4 13.5 %collective-permute-start.31 = (bf16[2,2,96,384]{3,2,1,0:T(8,128)(2,1)S(1)}, bf16[2,2,96,384]{3,2,1,0:T(8,128)(2,1)S(1)}, u32[]{:S(2)}, u32[]{:S(2)}) collective-permute-start(bf16[2,2,96,384]{3,2,1,0:T(8,128)(2,1)S(1)} %get-tuple-element.164), channel_id=1, source_target_pairs={{0,2},{1,3},{2,0},{3,1},{4,6},{5,7},{6,4},{7,5},{8,10},{9,11},{10,... | collective-permute-start | bytes 884744 | tf_op jit(solution)/shard_map/ppermute | solution.py:704
  (61 other events, 499.6 us)

commit v3 on v2

--- a/solution.py
+++ b/solution.py
@@ -47,7 +47,7 @@
     return (unit * gain + shift).astype(BF)
 
 
-def call(body, grid, in_specs, out_specs, out_shape, scratch, cost, deps=()):
+def call(body, grid, in_specs, out_specs, out_shape, scratch, cost, deps=(), aliases=None):
     count = len(in_specs)
 
     def with_deps(sc, *refs):
@@ -63,6 +63,7 @@
             scratch_shapes=scratch,
         ),
         out_shape=out_shape,
+        input_output_aliases=aliases or {},
         compiler_params=pltpu.CompilerParams(vmem_limit_bytes=32 * 1024 * 1024),
         cost_estimate=pl.CostEstimate(flops=int(5 * cost[0]), bytes_accessed=int(5 * cost[1]), transcendentals=0),
     )
@@ -788,25 +789,34 @@
     return share, far, near, to_core(far)
 
 
-def unpack_body(shares, sc, *refs):
-    (final_keep, final_got, input_keep, input_got, small), refs = refs[:5], refs[5:]
-    final, inputs, up, down, qkv, out, a_gain, a_shift, b_out, f_gain, f_shift, b_down, b_up = refs[-13:]
+def ffn_unpacked(sc, shares, up, down):
+    for n in range(4):
+        x, core = sc[X] ^ (n % 2), sc[C] ^ (n // 2)
+        for j in range(2):
+            at = pl.multiple_of(x * 4 * HALF + core * 2 * HALF + j * HALF, PAIR)
+            up[0, :, pl.ds(at, HALF)] = shares[n][j].astype(F32)
+            rows = pl.ds(pl.multiple_of(core * 2 * PART + j * PART, 8), PART)
+            down[0, rows, pl.ds(pl.multiple_of(x * HALF, PAIR), HALF)] = shares[n][2 + j].astype(F32)
+
+
+def unpack_early_body(sc, final_keep, final_got, input_keep, input_got, *refs):
+    final, inputs, up, down = refs[-4:]
     x = sc[X]
     for ref, mine, got in ((final, final_keep, final_got), (inputs, input_keep, input_got)):
         ref[x, 0] = mine[...]
         ref[1 - x, 0] = got[...].astype(F32)
+    ffn_unpacked(sc, refs[:4], up, down)
+
+
+def unpack_body(shares, sc, small, up_before, down_before, *refs):
+    up, down, qkv, out, a_gain, a_shift, b_out, f_gain, f_shift, b_down, b_up = refs[-11:]
+    ffn_unpacked(sc, refs[:4], up, down)
     for layer in range(2):
-        ffn, qv, ko = shares[layer]
+        qv, ko = shares[layer]
         for n in range(4):
             x, core = sc[X] ^ (n % 2), sc[C] ^ (n // 2)
-            for j in range(2):
-                at = pl.multiple_of(x * 4 * HALF + core * 2 * HALF + j * HALF, PAIR)
-                up[layer, :, pl.ds(at, HALF)] = refs[ffn[n]][j].astype(F32)
-                rows = pl.ds(pl.multiple_of(core * 2 * PART + j * PART, 8), PART)
-                down[layer, rows, pl.ds(pl.multiple_of(x * HALF, PAIR), HALF)] = refs[ffn[n]][2 + j].astype(F32)
             index, at = qv[n]
-            value = refs[index][...] if at is None else refs[index][at]
-            qkv[layer, :, pl.ds(pl.multiple_of(x * 2 * D + core * HALF, PAIR), HALF)] = value.astype(F32)
+            qkv[layer, :, pl.ds(pl.multiple_of(x * 2 * D + core * HALF, PAIR), HALF)] = refs[index][at].astype(F32)
         for n in range(2):
             side = pl.multiple_of((sc[C] ^ n) * HALF, PAIR)
             qkv[layer, :, pl.ds(pl.multiple_of(D + side, PAIR), HALF)] = refs[ko[n]][0].astype(F32)
@@ -826,18 +836,35 @@
         b_up[layer : layer + 1] = row
 
 
-def unpacked(scalars, rows, small, arrays, shares):
+FFN_GRADS = ((2, PART, FF), (2, 4 * PART, D))
+
+
+def unpacked_early(scalars, rows, arrays, layer):
     moved = ((2, 1, BLOCK, D),) * 2
-    dims = ((2, PART, FF), (2, 4 * PART, D), (2, PART, 3 * D), (2, PART, D)) + ((2, PART),) * 6 + ((2, 4 * PART),)
+    return call(
+        unpack_early_body,
+        (1,),
+        [whole((BLOCK, D))] * 4 + [whole(array.shape) for array in arrays],
+        [whole(d) for d in moved] + [at_layer((1,) + d[1:], layer) for d in FFN_GRADS],
+        [shape(d, F32) for d in moved] + [stored(d, F32) for d in FFN_GRADS],
+        [],
+        (1e6, 9e6),
+    )(scalars, *rows, *arrays)
+
+
+def unpacked(scalars, small, up, down, arrays, shares):
+    dims = ((2, PART, 3 * D), (2, PART, D)) + ((2, PART),) * 6 + ((2, 4 * PART),)
+    held = pl.BlockSpec(memory_space=pl.ANY)
     return call(
         partial(unpack_body, shares),
         (1,),
-        [whole((BLOCK, D))] * 4 + [whole((32, D))] + [whole(array.shape) for array in arrays],
-        [whole(d) for d in moved + dims],
-        [shape(d, F32) for d in moved + dims],
+        [whole((32, D)), held, held] + [whole(array.shape) for array in arrays],
+        [at_layer((1,) + d[1:], 0) for d in FFN_GRADS] + [whole(d) for d in dims],
+        [stored(d, F32) for d in FFN_GRADS] + [shape(d, F32) for d in dims],
         [],
         (1e6, 11e6),
-    )(scalars, *rows, small, *arrays)
+        aliases={2: 0, 3: 1},
+    )(scalars, small, from_hbm(up), from_hbm(down), *arrays)
 
 
 def on_device(
@@ -888,8 +915,11 @@
     kept = []
     own, own_spec, other, other_spec = stream, own_in, stream, other_in
     for layer in range(2):
+        seen = (own, own_spec, other, other_spec)
+        if layer == 0:
+            seen = (from_hbm(own), own_spec, from_hbm(other), other_spec)
         qkv, ctx, ctx_own, ctx_oth, lse = attention_forward(
-            scalars, layer, own, own_spec, other, other_spec, eps, ep_spec, a_gain, a_shift, qkv_weight
+            scalars, layer, *seen, eps, ep_spec, a_gain, a_shift, qkv_weight
         )
         ctx_rcv = to_core(ctx_oth)
         ctx_far = to_core(ctx_own)
@@ -971,14 +1001,14 @@
         g0_o = to_chip(g0)
         dh0, ds0, f_small0 = ffn_back(0, rows5(g0), local)
         ds0_rcv = to_core(ds0)
-        fk0, send = ffn_grads(0, rows5(g0), local, rows5(g0_o), local, dh0)
-        pinned.append(fk0)
-        (fz1,) = summed(z_sum(fk1, fg1, fy1), deps=[from_hbm(fk0)])
-        fg0 = to_core(send)
-        qk1, send, ok1, z_send = attn_grads(1, ds1, ds1_rcv, d_qkv1, [fz1])
+        qk1, send, ok1, z_send = attn_grads(1, ds1, ds1_rcv, d_qkv1, [ds0])
         pinned += [qk1, ok1]
         qg1, og1 = to_chip(send), to_dp(z_send, 2)
-        fy0, final_low = summed(y_sum(fk0, fg0), [[(final_low,)]], deps=[from_hbm(qk1)])
+        fk0, send = ffn_grads(0, rows5(g0), local, rows5(g0_o), local, dh0, [from_hbm(qk1)])
+        pinned.append(fk0)
+        fg0 = to_core(send)
+        (fz1,) = summed(z_sum(fk1, fg1, fy1), deps=[from_hbm(fk0)])
+        fy0, final_low = summed(y_sum(fk0, fg0), [[(final_low,)]], deps=[fz1])
         d_qkv0, part0, part0_oth = attn_back(0, ds0, ds0_rcv, [fy0])
         final_got = to_chip(final_low)
         fz1, fy0 = to_dp(fz1, 2), to_dp(fy0, 1)
@@ -1038,19 +1068,17 @@
         )
         qf0, ox0_got = to_dp(qf0, 4), to_chip(ox0)
 
+        final_out, input_out, ups, downs = unpacked_early(
+            scalars, (final_keep, final_got, input_keep, input_got), f1_all, 1
+        )
         both, o0 = summed(
             share(qk0, qg0, qy0, qz0, qf0) + [[(qk1, 0, 0), (qg1, 0, 0), (y1, 4), (qz1, 0), (qf1,)]],
             [[(ox0,), (ox0_got,)]],
-            deps=f0_all[1:],
-        )
-        arrays = f0_all + f1_all + gathered(both) + (o0, to_core(o0), o1, to_core(o1))
-        shares = (
-            ((0, 1, 2, 3), tuple((n, 0) for n in range(8, 12)), (12, 13)),
-            ((4, 5, 6, 7), tuple((n, 1) for n in range(8, 12)), (14, 15)),
-        )
-        (final_out, input_out, ups, downs, qkvs, outs, *vectors) = unpacked(
-            scalars, (final_keep, final_got, input_keep, input_got), small, arrays, shares
-        )
+            deps=f0_all[1:] + (from_hbm(ups),),
+        )
+        arrays = f0_all + gathered(both) + (o0, to_core(o0), o1, to_core(o1))
+        shares = ((tuple((n, 0) for n in range(4, 8)), (8, 9)), (tuple((n, 1) for n in range(4, 8)), (10, 11)))
+        (ups, downs, qkvs, outs, *vectors) = unpacked(scalars, small, ups, downs, arrays, shares)
         g_a_gain, g_a_shift, g_b_out, g_f_gain, g_f_shift, g_b_down, g_b_up = vectors
     else:
         final_got = to_chip(final_send)

time: 310 us -> 302 us (0.974)
  starting transfers between devices: 46.6 us -> 39.7 us
    ppermute x19, starting transfers between devices: 28.2 us -> 18.5 us  [to_dp(): return lax.ppermute(value, 'dp', [(i, i ^ distance) for i in range(8)])]
    ppermute x13, waiting for transfers between devices: 16.1 us -> 9.33 us  [to_chip(): return lax.ppermute(value, 'section', [(0, 2), (2, 0), (1, 3), (3, 1)])]
    pallas_call x26 -> x27, Pallas kernels: 199 us -> 202 us  [call(): return lambda *args: kernel(*args, *deps)]
  transfers between devices with their start and end apart: 52 -> 52, of which waited for: 13 -> 15; matrix products, arithmetic and copies ran while one was open for 0% -> 0% of each run, Pallas kernels for 53% -> 56%
where the time goes in v3:
time: 302 us; the launch traced here: 297 us
  Pallas kernels  202 us (67%)
  waiting for transfers between devices  50.7 us (17%)
  starting transfers between devices  39.7 us (13%)
  local copies, waits for them, and re-layouts  3.02 us (1%)
    pallas_call x27, Pallas kernels, call(): return lambda *args: kernel(*args, *deps)  202 us
    ppermute x19, waiting for transfers between devices, to_dp(): return lax.ppermute(value, 'dp', [(i, i ^ distance) for i in range(8)])  37.3 us
    ppermute x19, starting transfers between devices, to_dp(): return lax.ppermute(value, 'dp', [(i, i ^ distance) for i in range(8)])  18.5 us
    ppermute x13, starting transfers between devices, to_chip(): return lax.ppermute(value, 'section', [(0, 2), (2, 0), (1, 3), (3, 1)])  17.3 us
    ppermute x13, waiting for transfers between devices, to_chip(): return lax.ppermute(value, 'section', [(0, 2), (2, 0), (1, 3), (3, 1)])  9.33 us
  transfers between devices with their start and end apart: 52, of which 15 were waited for; matrix products, arithmetic and copies ran while one was open for 0% of the time, Pallas kernels for 56%

profile of v3, /device:TPU:0, one launch (start us, length us, event | category | flops | bytes accessed | tf_op | source)
XLA Modules:
  0.0 297.1 jit_solution(3794136289578751757)
XLA Ops:
  2.9 15.6 %shard_map.237 = (bf16[1024,1152]{1,0:T(8,128)(2,1)}, bf16[1024,384]{1,0:T(8,128)(2,1)}, bf16[2,256,384]{2,1,0:T(8,128)(2,1)S(1)}, bf16[2,256,384]{2,1,0:T(8,128)(2,1)S(1)}, f32[8,1024]{1,0:T(8,128)S(1)}) custom-call(s32[4]{0:T(128)S(1)} %pad_add_fusion.sc, bf16[2,2,2,256,768]{4,3,2,1,0:T(8,128)(2,1)} %bitcast.10, bf16[2,2,2,256,768]{4,3,2,1,0:T(8,128)(2,1)} %bitcast.11, ...), custom_call_target="tpu_custom_call" | custom-call | flops 20999999488 | bytes 40000000 | tf_op jit(solution)/shard_map/pallas_call | solution.py:70
  20.3 13.2 %shard_map.238 = (bf16[512,768]{1,0:T(8,128)(2,1)S(1)}, bf16[512,768]{1,0:T(8,128)(2,1)S(1)}, bf16[512,3072]{1,0:T(8,128)(2,1)}, bf16[512,3072]{1,0:T(8,128)(2,1)}, bf16[2,256,768]{2,1,0:T(8,128)(2,1)S(1)}) custom-call(s32[4]{0:T(128)S(1)} %pad_add_fusion.sc, bf16[2,256,384]{2,1,0:T(8,128)(2,1)S(1)} %get-tuple-element.105.refs_0_, ...), custom_call_target="tpu_custom_call" | custom-call | flops 27000000512 | bytes 100000000 | tf_op jit(solution)/shard_map/pallas_call | solution.py:70
  34.1 2.8 collective-permute-start.4
  36.9 14.9 %shard_map.239 = (bf16[1024,1152]{1,0:T(8,128)(2,1)}, bf16[1024,384]{1,0:T(8,128)(2,1)}, bf16[2,256,384]{2,1,0:T(8,128)(2,1)S(1)}, bf16[2,256,384]{2,1,0:T(8,128)(2,1)S(1)}, f32[8,1024]{1,0:T(8,128)S(1)}) custom-call(s32[4]{0:T(128)S(1)} %pad_add_fusion.sc, bf16[1,2,1,256,768]{4,3,2,1,0:T(8,128)(2,1)S(1)} %bitcast.16, ...), custom_call_target="tpu_custom_call" | custom-call | flops 20999999488 | bytes 40000000 | tf_op jit(solution)/shard_map/pallas_call | solution.py:70
  54.7 2.7 shard_map.240
  59.3 10.9 %shard_map.241 = (bf16[512,3072]{1,0:T(8,128)(2,1)S(1)}, bf16[512,3072]{1,0:T(8,128)(2,1)S(1)}, f32[256,768]{1,0:T(8,128)S(1)}, bf16[256,768]{1,0:T(8,128)(2,1)S(1)}) custom-call(s32[4]{0:T(128)S(1)} %pad_add_fusion.sc, bf16[512,768]{1,0:T(8,128)(2,1)S(1)} %get-tuple-element.111.refs_0_.refs_1_.refs_2_, ...), custom_call_target="tpu_custom_call" | custom-call | flops 24000000000 | bytes 90000000 | tf_op jit(solution)/shard_map/pallas_call | solution.py:70
  70.2 10.2 %shard_map.242 = (bf16[512,3072]{1,0:T(8,128)(2,1)S(1)}, bf16[2,256,768]{2,1,0:T(8,128)(2,1)S(1)}, f32[8,768]{1,0:T(8,128)S(1)}) custom-call(s32[4]{0:T(128)S(1)} %pad_add_fusion.sc, bf16[2,2,2,256,768]{4,3,2,1,0:T(8,128)(2,1)S(1)} %bitcast.20, bf16[512,768]{1,0:T(8,128)(2,1)S(1)} %get-tuple-element.111.refs_0_.refs_1_.refs_2_, ...), custom_call_target="tpu_custom_call" | custom-call | flops 24500000768 | bytes 90000000 | tf_op jit(solution)/shard_map/pallas_call | solution.py:70
  80.5 19.8 %shard_map.243 = (bf16[2,4,4,96,384]{4,3,2,1,0:T(8,128)(2,1)}, bf16[2,4,4,96,384]{4,3,2,1,0:T(8,128)(2,1)S(1)}) custom-call(s32[4]{0:T(128)S(1)} %pad_add_fusion.sc, bf16[2,2,2,256,768]{4,3,2,1,0:T(8,128)(2,1)S(1)} %bitcast.21, bf16[2,2,2,256,768]{4,3,2,1,0:T(8,128)(2,1)S(1)} %bitcast.22, bf16[512,768]{1,0:T(8,128)(2,1)S(1)} %get-tuple-element.111.refs_0_.refs_1_.refs_2_, ...), custom_call_target="tpu_custom_call" | custom-call | flops 43000000512 | bytes 110000000 | tf_op jit(solution)/shard_map/pallas_call | solution.py:70
  100.8 18.7 %shard_map.244 = (bf16[1024,1152]{1,0:T(8,128)(2,1)S(1)}, f32[2,256,768]{2,1,0:T(8,128)S(1)}, bf16[2,256,768]{2,1,0:T(8,128)(2,1)S(1)}) custom-call(s32[4]{0:T(128)S(1)} %pad_add_fusion.sc, bf16[2,256,768]{2,1,0:T(8,128)(2,1)S(1)} %get-tuple-element.114.refs_0_.refs_5_, bf16[2,256,768]{2,1,0:T(8,128)(2,1)S(1)} %collective-permute-done.6.refs_1_.refs_6_, ...), custom_call_target="tpu_custom_call" | custom-call | flops 42500001792 | bytes 60000000 | tf_op jit(solution)/shard_map/pallas_call | solution.py:70
  125.8 11.5 %shard_map.247 = (bf16[512,3072]{1,0:T(8,128)(2,1)S(1)}, bf16[2,256,768]{2,1,0:T(8,128)(2,1)}, f32[8,768]{1,0:T(8,128)S(1)}) custom-call(s32[4]{0:T(128)S(1)} %pad_add_fusion.sc, bf16[1,2,1,256,768]{4,3,2,1,0:T(8,128)(2,1)S(1)} %bitcast.25, bf16[512,768]{1,0:T(8,128)(2,1)S(1)} %copy-done.10, f32[2,1,768]{2,1,0:T(1,128)S(1)} %reshape.70.refs_5_.refs_1_.refs_2_.refs_4_, ...), custom_call_target="tpu_custom_call" | custom-call | flops 24500000768 | bytes 90000000 | tf_op jit(solution)/shard_map/pallas_call | solution.py:70
  137.3 6.8 %shard_map.248 = (bf16[2,4,96,384]{3,2,1,0:T(8,128)(2,1)}, bf16[2,4,96,384]{3,2,1,0:T(8,128)(2,1)}, bf16[2,2,2,96,384]{4,3,2,1,0:T(8,128)(2,1)}, bf16[2,2,2,96,384]{4,3,2,1,0:T(8,128)(2,1)}) custom-call(s32[4]{0:T(128)S(1)} %pad_add_fusion.sc, bf16[1,2,1,256,768]{4,3,2,1,0:T(8,128)(2,1)S(1)} %bitcast.19, bf16[1,2,1,256,768]{4,3,2,1,0:T(8,128)(2,1)S(1)} %bitcast.24, ...), custom_call_target="tpu_custom_call" | custom-call | flops 12499999744 | bytes 60000000 | tf_op jit(solution)/shard_map/pallas_call | solution.py:70
  147.2 19.3 %shard_map.249 = (bf16[2,4,4,96,384]{4,3,2,1,0:T(8,128)(2,1)}, bf16[2,4,4,96,384]{4,3,2,1,0:T(8,128)(2,1)S(1)}) custom-call(s32[4]{0:T(128)S(1)} %pad_add_fusion.sc, bf16[1,2,1,256,768]{4,3,2,1,0:T(8,128)(2,1)S(1)} %bitcast.26, bf16[1,2,1,256,768]{4,3,2,1,0:T(8,128)(2,1)S(1)} %bitcast.27, bf16[512,768]{1,0:T(8,128)(2,1)S(1)} %copy-done.10, ...), custom_call_target="tpu_custom_call" | custom-call | flops 43000000512 | bytes 110000000 | tf_op jit(solution)/shard_map/pallas_call | solution.py:70
  174.2 19.2 %shard_map.252 = (bf16[1024,1152]{1,0:T(8,128)(2,1)S(1)}, f32[2,256,768]{2,1,0:T(8,128)S(1)}, bf16[2,256,768]{2,1,0:T(8,128)(2,1)S(1)}) custom-call(s32[4]{0:T(128)S(1)} %pad_add_fusion.sc, bf16[2,256,768]{2,1,0:T(8,128)(2,1)} %get-tuple-element.132.refs_10_.refs_0_.refs_5_, bf16[2,256,768]{2,1,0:T(8,128)(2,1)} %collective-permute-done.14.refs_1_.refs_6_, ...), custom_call_target="tpu_custom_call" | custom-call | flops 42500001792 | bytes 60000000 | tf_op jit(solution)/shard_map/pallas_call | solution.py:70
  196.1 3.0 %shard_map.254 = (f32[256,768]{1,0:T(8,128)S(1)}, bf16[256,768]{1,0:T(8,128)(2,1)S(1)}, f32[32,768]{1,0:T(8,128)S(1)}) custom-call(s32[4]{0:T(128)S(1)} %pad_add_fusion.sc, bf16[2,256,768]{2,1,0:T(8,128)(2,1)} %get-tuple-element.132.refs_10_.refs_0_.refs_5_, f32[2,256,768]{2,1,0:T(8,128)S(1)} %get-tuple-element.142.refs_10_.refs_1_, ...), custom_call_target="tpu_custom_call" | custom-call | flops 1000000000 | bytes 25000000 | tf_op jit(solution)/shard_map/pallas_call | solution.py:70
  199.7 2.6 collective-permute-start.24
  208.0 7.7 %shard_map.256 = (bf16[2,4,96,384]{3,2,1,0:T(8,128)(2,1)}, bf16[2,4,96,384]{3,2,1,0:T(8,128)(2,1)S(1)}, bf16[4,2,96,384]{3,2,1,0:T(8,128)(2,1)}, bf16[4,2,96,384]{3,2,1,0:T(8,128)(2,1)S(1)}) custom-call(s32[4]{0:T(128)S(1)} %pad_add_fusion.sc, bf16[2,2,2,256,768]{4,3,2,1,0:T(8,128)(2,1)S(1)} %bitcast.14, bf16[2,2,2,256,768]{4,3,2,1,0:T(8,128)(2,1)S(1)} %bitcast.15, ...), custom_call_target="tpu_custom_call" | custom-call | flops 12499999744 | bytes 60000000 | tf_op jit(solution)/shard_map/pallas_call | solution.py:70
  221.1 9.0 %collective-permute-done.22.refs_3_.refs_12_ = bf16[2,4,96,384]{3,2,1,0:T(8,128)(2,1)S(1)} collective-permute-done((bf16[2,4,96,384]{3,2,1,0:T(8,128)(2,1)S(1)}, bf16[2,4,96,384]{3,2,1,0:T(8,128)(2,1)S(1)}, u32[]{:S(2)}, u32[]{:S(2)}) %collective-permute-start.22) | collective-permute-done | bytes 589856 | tf_op jit(solution)/shard_map/ppermute | solution.py:705
  241.8 3.5 %collective-permute-done.36.refs_19_ = f32[32,768]{1,0:T(8,128)S(1)} collective-permute-done((f32[32,768]{1,0:T(8,128)S(1)}, f32[32,768]{1,0:T(8,128)S(1)}, u32[]{:S(2)}, u32[]{:S(2)}) %collective-permute-start.36) | collective-permute-done | bytes 98336 | tf_op jit(solution)/shard_map/ppermute | solution.py:701
  245.8 4.3 %collective-permute-done.33.refs_5_.refs_8_.refs_2_ = bf16[4,96,384]{2,1,0:T(8,128)(2,1)S(1)} collective-permute-done((bf16[4,96,384]{2,1,0:T(8,128)(2,1)S(1)}, bf16[4,96,384]{2,1,0:T(8,128)(2,1)S(1)}, u32[]{:S(2)}, u32[]{:S(2)}) %collective-permute-start.33) | collective-permute-done | bytes 294944 | tf_op jit(solution)/shard_map/ppermute | solution.py:705
  250.2 9.0 %collective-permute-done.34.refs_2_.refs_6_ = bf16[2,2,96,384]{3,2,1,0:T(8,128)(2,1)S(1)} collective-permute-done((bf16[2,2,96,384]{3,2,1,0:T(8,128)(2,1)S(1)}, bf16[2,2,96,384]{3,2,1,0:T(8,128)(2,1)S(1)}, u32[]{:S(2)}, u32[]{:S(2)}) %collective-permute-start.34) | collective-permute-done | bytes 294944 | tf_op jit(solution)/shard_map/ppermute | solution.py:705
  265.7 6.9 %collective-permute-done.40.refs_11_ = f32[32,768]{1,0:T(8,128)S(1)} collective-permute-done((f32[32,768]{1,0:T(8,128)S(1)}, f32[32,768]{1,0:T(8,128)S(1)}, u32[]{:S(2)}, u32[]{:S(2)}) %collective-permute-start.40) | collective-permute-done | bytes 98336 | tf_op jit(solution)/shard_map/ppermute | solution.py:705
  278.6 3.3 %shard_map.258 = (f32[2,1,256,768]{3,2,1,0:T(8,128)}, f32[2,1,256,768]{3,2,1,0:T(8,128)}, f32[2,96,3072]{2,1,0:T(8,128)}, f32[2,384,768]{2,1,0:T(8,128)}) custom-call(s32[4]{0:T(128)S(1)} %pad_add_fusion.sc, f32[256,768]{1,0:T(8,128)S(1)} %get-tuple-element.112.refs_0_, bf16[256,768]{1,0:T(8,128)(2,1)S(1)} %copy-done.3, f32[256,768]{1,0:T(8,128)S(1)} %copy-done.5, ...), custom_call_target="tpu_custom_call" | custom-call | flops 5000000 | bytes 45000000 | tf_op jit(solution)/shard_map/pallas_call | solution.py:70
  288.4 3.4 %collective-permute-done.47.refs_8_ = bf16[2,96,384]{2,1,0:T(8,128)(2,1)S(1)} collective-permute-done((bf16[2,96,384]{2,1,0:T(8,128)(2,1)S(1)}, bf16[2,96,384]{2,1,0:T(8,128)(2,1)S(1)}, u32[]{:S(2)}, u32[]{:S(2)}) %collective-permute-start.47) | collective-permute-done | bytes 147488 | tf_op jit(solution)/shard_map/ppermute | solution.py:701
  293.2 3.3 %shard_map.263 = (f32[2,96,3072]{2,1,0:T(8,128)}, f32[2,384,768]{2,1,0:T(8,128)}, f32[2,96,2304]{2,1,0:T(8,128)}, f32[2,96,768]{2,1,0:T(8,128)}, f32[2,96]{1,0:T...) custom-call(s32[4]{0:T(128)S(1)} %pad_add_fusion.sc, ...), custom_call_target="tpu_custom_call", output_to_operand_aliasing={{0}: (2, {}), {1}: (3, {})} | custom-call | flops 5000000 | bytes 55000000 | tf_op jit(solution)/shard_map/pallas_call | solution.py:70
  (175 shorter events, 73.7 us)
Async XLA Ops:
  33.9 18.4 %collective-permute-start.3 = (bf16[2,256,384]{2,1,0:T(8,128)(2,1)S(1)}, bf16[2,256,384]{2,1,0:T(8,128)(2,1)S(1)}, u32[]{:S(2)}, u32[]{:S(2)}) collective-permute-start(bf16[2,256,384]{2,1,0:T(8,128)(2,1)S(1)} %get-tuple-element.105.refs_0_), channel_id=1, source_target_pairs={{0,8},{8,0},{16,24},{24,16},{1,9},{9,1},{17,25},{25,17},{2,10},{10... | collective-permute-start | bytes 1179656 | tf_op jit(solution)/shard_map/ppermute | solution.py:697
  34.1 20.7 %collective-permute-start.4 = (bf16[512,768]{1,0:T(8,128)(2,1)S(1)}, bf16[512,768]{1,0:T(8,128)(2,1)S(1)}, u32[]{:S(2)}, u32[]{:S(2)}) collective-permute-start(bf16[512,768]{1,0:T(8,128)(2,1)S(1)} %get-tuple-element.110.refs_1_.refs_2_), channel_id=1, source_target_pairs={{0,16},{16,0},{8,24},{24,8},{1,17},{17,1},{9,25},{25,9},{2,18},{18... | collective-permute-start | bytes 2359304 | tf_op jit(solution)/shard_map/ppermute | solution.py:701
  51.9 18.3 %collective-permute-start.5 = (bf16[2,256,384]{2,1,0:T(8,128)(2,1)S(1)}, bf16[2,256,384]{2,1,0:T(8,128)(2,1)S(1)}, u32[]{:S(2)}, u32[]{:S(2)}) collective-permute-start(bf16[2,256,384]{2,1,0:T(8,128)(2,1)S(1)} %get-tuple-element.108.refs_0_), channel_id=1, source_target_pairs={{0,8},{8,0},{16,24},{24,16},{1,9},{9,1},{17,25},{25,17},{2,10},{10... | collective-permute-start | bytes 1179656 | tf_op jit(solution)/shard_map/ppermute | solution.py:697
  57.5 23.1 %collective-permute-start.7 = (bf16[512,768]{1,0:T(8,128)(2,1)S(1)}, bf16[512,768]{1,0:T(8,128)(2,1)S(1)}, u32[]{:S(2)}, u32[]{:S(2)}) collective-permute-start(bf16[512,768]{1,0:T(8,128)(2,1)S(1)} %get-tuple-element.111.refs_0_.refs_1_.refs_2_), channel_id=1, source_target_pairs={{0,16},{16,0},{8,24},{24,8},{1,17},{17,1},{9,25},{25,9},{2,18},{18... | collective-permute-start | bytes 2359304 | tf_op jit(solution)/shard_map/ppermute | solution.py:701
  80.4 20.4 %collective-permute-start.6 = (bf16[2,256,768]{2,1,0:T(8,128)(2,1)S(1)}, bf16[2,256,768]{2,1,0:T(8,128)(2,1)S(1)}, u32[]{:S(2)}, u32[]{:S(2)}) collective-permute-start(bf16[2,256,768]{2,1,0:T(8,128)(2,1)S(1)} %get-tuple-element.114.refs_0_.refs_5_), channel_id=1, source_target_pairs={{0,8},{8,0},{16,24},{24,16},{1,9},{9,1},{17,25},{25,17},{2,10},{10... | collective-permute-start | bytes 2359304 | tf_op jit(solution)/shard_map/ppermute | solution.py:697
  100.3 19.3 %collective-permute-start.9 = (bf16[2,4,4,96,384]{4,3,2,1,0:T(8,128)(2,1)S(1)}, bf16[2,4,4,96,384]{4,3,2,1,0:T(8,128)(2,1)S(1)}, u32[]{:S(2)}, u32[]{:S(2)}) collective-permute-start(bf16[2,4,4,96,384]{4,3,2,1,0:T(8,128)(2,1)S(1)} %get-tuple-element.123), channel_id=1, source_target_pairs={{0,8},{8,0},{16,24},{24,16},{1,9},{9,1},{17,25},{25,17},{2,10},{10... | collective-permute-start | bytes 7077896 | tf_op jit(solution)/shard_map/ppermute | solution.py:697
  121.7 44.8 %collective-permute-start.12 = (bf16[4,4,96,384]{3,2,1,0:T(8,128)(2,1)S(1)}, bf16[4,4,96,384]{3,2,1,0:T(8,128)(2,1)S(1)}, u32[]{:S(2)}, u32[]{:S(2)}) collective-permute-start(bf16[4,4,96,384]{3,2,1,0:T(8,128)(2,1)S(1)} %get-tuple-element.125.refs_5_), channel_id=1, source_target_pairs={{0,1},{1,0},{2,3},{3,2},{4,5},{5,4},{6,7},{7,6},{8,9},{9,8},{10,11... | collective-permute-start | bytes 3538952 | tf_op jit(solution)/shard_map/ppermute | solution.py:705
  125.2 22.0 %collective-permute-start.10 = (bf16[2,256,768]{2,1,0:T(8,128)(2,1)S(1)}, bf16[2,256,768]{2,1,0:T(8,128)(2,1)S(1)}, u32[]{:S(2)}, u32[]{:S(2)}) collective-permute-start(bf16[2,256,768]{2,1,0:T(8,128)(2,1)S(1)} %get-tuple-element.126), channel_id=1, source_target_pairs={{0,16},{16,0},{8,24},{24,8},{1,17},{17,1},{9,25},{25,9},{2,18},{18... | collective-permute-start | bytes 2359304 | tf_op jit(solution)/shard_map/ppermute | solution.py:701
  137.3 36.4 %collective-permute-start.14 = (bf16[2,256,768]{2,1,0:T(8,128)(2,1)}, bf16[2,256,768]{2,1,0:T(8,128)(2,1)}, u32[]{:S(2)}, u32[]{:S(2)}) collective-permute-start(bf16[2,256,768]{2,1,0:T(8,128)(2,1)} %get-tuple-element.132.refs_10_.refs_0_.refs_5_), channel_id=1, source_target_pairs={{0,8},{8,0},{16,24},{24,16},{1,9},{9,1},{17,25},{25,17},{2,10},{10... | collective-permute-start | bytes 2359304 | tf_op jit(solution)/shard_map/ppermute | solution.py:697
  144.1 49.3 %collective-permute-start.17 = (bf16[2,2,2,96,384]{4,3,2,1,0:T(8,128)(2,1)}, bf16[2,2,2,96,384]{4,3,2,1,0:T(8,128)(2,1)}, u32[]{:S(2)}, u32[]{:S(2)}) collective-permute-start(bf16[2,2,2,96,384]{4,3,2,1,0:T(8,128)(2,1)} %get-tuple-element.148), channel_id=1, source_target_pairs={{0,2},{1,3},{2,0},{3,1},{4,6},{5,7},{6,4},{7,5},{8,10},{9,11},{10,... | collective-permute-start | bytes 1769480 | tf_op jit(solution)/shard_map/ppermute | solution.py:705
  145.7 47.8 %collective-permute-start.18 = (bf16[2,4,96,384]{3,2,1,0:T(8,128)(2,1)}, bf16[2,4,96,384]{3,2,1,0:T(8,128)(2,1)}, u32[]{:S(2)}, u32[]{:S(2)}) collective-permute-start(bf16[2,4,96,384]{3,2,1,0:T(8,128)(2,1)} %get-tuple-element.149), channel_id=1, source_target_pairs={{0,16},{16,0},{8,24},{24,8},{1,17},{17,1},{9,25},{25,9},{2,18},{18... | collective-permute-start | bytes 1769480 | tf_op jit(solution)/shard_map/ppermute | solution.py:701
  168.3 25.2 %collective-permute-start.16 = (bf16[2,4,96,384]{3,2,1,0:T(8,128)(2,1)S(1)}, bf16[2,4,96,384]{3,2,1,0:T(8,128)(2,1)S(1)}, u32[]{:S(2)}, u32[]{:S(2)}) collective-permute-start(bf16[2,4,96,384]{3,2,1,0:T(8,128)(2,1)S(1)} %shard_map.250.refs_3_), channel_id=1, source_target_pairs={{0,2},{1,3},{2,0},{3,1},{4,6},{5,7},{6,4},{7,5},{8,10},{9,11},{10,... | collective-permute-start | bytes 1769480 | tf_op jit(solution)/shard_map/ppermute | solution.py:705
  173.1 22.9 %collective-permute-start.13 = (bf16[256,768]{1,0:T(8,128)(2,1)S(1)}, bf16[256,768]{1,0:T(8,128)(2,1)S(1)}, u32[]{:S(2)}, u32[]{:S(2)}) collective-permute-start(bf16[256,768]{1,0:T(8,128)(2,1)S(1)} %get-tuple-element.137), channel_id=1, source_target_pairs={{0,16},{16,0},{8,24},{24,8},{1,17},{17,1},{9,25},{25,9},{2,18},{18... | collective-permute-start | bytes 1179656 | tf_op jit(solution)/shard_map/ppermute | solution.py:701
  173.7 31.6 %collective-permute-start.20 = (bf16[4,4,96,384]{3,2,1,0:T(8,128)(2,1)S(1)}, bf16[4,4,96,384]{3,2,1,0:T(8,128)(2,1)S(1)}, u32[]{:S(2)}, u32[]{:S(2)}) collective-permute-start(bf16[4,4,96,384]{3,2,1,0:T(8,128)(2,1)S(1)} %get-tuple-element.141.refs_8_), channel_id=1, source_target_pairs={{0,1},{1,0},{2,3},{3,2},{4,5},{5,4},{6,7},{7,6},{8,9},{9,8},{10,11... | collective-permute-start | bytes 3538952 | tf_op jit(solution)/shard_map/ppermute | solution.py:705
  199.7 18.3 %collective-permute-start.24 = (bf16[4,96,384]{2,1,0:T(8,128)(2,1)S(1)}, bf16[4,96,384]{2,1,0:T(8,128)(2,1)S(1)}, u32[]{:S(2)}, u32[]{:S(2)}) collective-permute-start(bf16[4,96,384]{2,1,0:T(8,128)(2,1)S(1)} %get-tuple-element.150.refs_8_), channel_id=1, source_target_pairs={{0,4},{1,5},{2,6},{3,7},{4,0},{5,1},{6,2},{7,3},{8,12},{9,13},{10,... | collective-permute-start | bytes 884744 | tf_op jit(solution)/shard_map/ppermute | solution.py:705
  202.3 17.3 %collective-permute-start.23 = (bf16[8,96,384]{2,1,0:T(8,128)(2,1)S(1)}, bf16[8,96,384]{2,1,0:T(8,128)(2,1)S(1)}, u32[]{:S(2)}, u32[]{:S(2)}) collective-permute-start(bf16[8,96,384]{2,1,0:T(8,128)(2,1)S(1)} %get-tuple-element.155), channel_id=1, source_target_pairs={{0,1},{1,0},{2,3},{3,2},{4,5},{5,4},{6,7},{7,6},{8,9},{9,8},{10,11... | collective-permute-start | bytes 1769480 | tf_op jit(solution)/shard_map/ppermute | solution.py:705
  203.8 29.3 %collective-permute-start.19 = (bf16[256,768]{1,0:T(8,128)(2,1)S(1)}, bf16[256,768]{1,0:T(8,128)(2,1)S(1)}, u32[]{:S(2)}, u32[]{:S(2)}) collective-permute-start(bf16[256,768]{1,0:T(8,128)(2,1)S(1)} %get-tuple-element.152), channel_id=1, source_target_pairs={{0,16},{16,0},{8,24},{24,8},{1,17},{17,1},{9,25},{25,9},{2,18},{18... | collective-permute-start | bytes 1179656 | tf_op jit(solution)/shard_map/ppermute | solution.py:701
  207.1 14.0 %collective-permute-start.25 = (f32[32,768]{1,0:T(8,128)S(1)}, f32[32,768]{1,0:T(8,128)S(1)}, u32[]{:S(2)}, u32[]{:S(2)}) collective-permute-start(f32[32,768]{1,0:T(8,128)S(1)} %get-tuple-element.156.refs_18_), channel_id=1, source_target_pairs={{0,4},{1,5},{2,6},{3,7},{4,0},{5,1},{6,2},{7,3},{8,12},{9,13},{10,... | collective-permute-start | bytes 294920 | tf_op jit(solution)/shard_map/ppermute | solution.py:705
  207.5 22.5 %collective-permute-start.22 = (bf16[2,4,96,384]{3,2,1,0:T(8,128)(2,1)S(1)}, bf16[2,4,96,384]{3,2,1,0:T(8,128)(2,1)S(1)}, u32[]{:S(2)}, u32[]{:S(2)}) collective-permute-start(bf16[2,4,96,384]{3,2,1,0:T(8,128)(2,1)S(1)} %get-tuple-element.154.refs_10_), channel_id=1, source_target_pairs={{0,2},{1,3},{2,0},{3,1},{4,6},{5,7},{6,4},{7,5},{8,10},{9,11},{10,... | collective-permute-start | bytes 1769480 | tf_op jit(solution)/shard_map/ppermute | solution.py:705
  218.0 16.3 %collective-permute-start.29 = (bf16[2,4,96,384]{3,2,1,0:T(8,128)(2,1)S(1)}, bf16[2,4,96,384]{3,2,1,0:T(8,128)(2,1)S(1)}, u32[]{:S(2)}, u32[]{:S(2)}) collective-permute-start(bf16[2,4,96,384]{3,2,1,0:T(8,128)(2,1)S(1)} %get-tuple-element.163), channel_id=1, source_target_pairs={{0,16},{16,0},{8,24},{24,8},{1,17},{17,1},{9,25},{25,9},{2,18},{18... | collective-permute-start | bytes 1769480 | tf_op jit(solution)/shard_map/ppermute | solution.py:701
  219.5 16.0 %collective-permute-start.30 = (bf16[4,2,96,384]{3,2,1,0:T(8,128)(2,1)S(1)}, bf16[4,2,96,384]{3,2,1,0:T(8,128)(2,1)S(1)}, u32[]{:S(2)}, u32[]{:S(2)}) collective-permute-start(bf16[4,2,96,384]{3,2,1,0:T(8,128)(2,1)S(1)} %get-tuple-element.165), channel_id=1, source_target_pairs={{0,1},{1,0},{2,3},{3,2},{4,5},{5,4},{6,7},{7,6},{8,9},{9,8},{10,11... | collective-permute-start | bytes 1769480 | tf_op jit(solution)/shard_map/ppermute | solution.py:705
  234.2 24.9 %collective-permute-start.35 = (bf16[6,96,384]{2,1,0:T(8,128)(2,1)S(1)}, bf16[6,96,384]{2,1,0:T(8,128)(2,1)S(1)}, u32[]{:S(2)}, u32[]{:S(2)}) collective-permute-start(bf16[6,96,384]{2,1,0:T(8,128)(2,1)S(1)} %get-tuple-element.170), channel_id=1, source_target_pairs={{0,4},{1,5},{2,6},{3,7},{4,0},{5,1},{6,2},{7,3},{8,12},{9,13},{10,... | collective-permute-start | bytes 1327112 | tf_op jit(solution)/shard_map/ppermute | solution.py:705
  245.3 13.9 %collective-permute-start.34 = (bf16[2,2,96,384]{3,2,1,0:T(8,128)(2,1)S(1)}, bf16[2,2,96,384]{3,2,1,0:T(8,128)(2,1)S(1)}, u32[]{:S(2)}, u32[]{:S(2)}) collective-permute-start(bf16[2,2,96,384]{3,2,1,0:T(8,128)(2,1)S(1)} %get-tuple-element.169), channel_id=1, source_target_pairs={{0,2},{1,3},{2,0},{3,1},{4,6},{5,7},{6,4},{7,5},{8,10},{9,11},{10,... | collective-permute-start | bytes 884744 | tf_op jit(solution)/shard_map/ppermute | solution.py:705
  245.8 13.3 %collective-permute-start.28 = (bf16[4,96,384]{2,1,0:T(8,128)(2,1)S(1)}, bf16[4,96,384]{2,1,0:T(8,128)(2,1)S(1)}, u32[]{:S(2)}, u32[]{:S(2)}) collective-permute-start(bf16[4,96,384]{2,1,0:T(8,128)(2,1)S(1)} %collective-permute-done.26.refs_5_.refs_20_), channel_id=1, source_target_pairs={{0,8},{8,0},{16,24},{24,16},{1,9},{9,1},{17,25},{25,17},{2,10},{10... | collective-permute-start | bytes 884744 | tf_op jit(solution)/shard_map/ppermute | solution.py:697
  (58 other events, 477.2 us)

commit v4 on v3

--- a/solution.py
+++ b/solution.py
@@ -430,7 +430,7 @@
 
 
 def ffn_weight_body(
-    sc, grad, grad_o, s2, s2_o, gain, shift, act, dh, w_up, b_up, w_down, keep, send, n_t, n_o, n_t_o, g_t, g_t_o
+    sc, grad, grad_o, s2, s2_o, gain, shift, act, dh, w_up, b_up, w_down, keep, send, n_t, n_o, g_t, acts, dhs
 ):
     t = pl.program_id(0)
     core = sc[C]
@@ -438,21 +438,24 @@
 
     @pl.when(t == 0)
     def _():
-        n_t[...] = norm_low(s2[...], gain[0], shift[0]).T
+        n_t[:, 0:ROWS] = norm_low(s2[...], gain[0], shift[0]).T
         other = norm_low(s2_o[...], gain[0], shift[0])
         n_o[...] = other
-        n_t_o[...] = other.T
+        n_t[:, ROWS : 2 * ROWS] = other.T
         x = sc[X]
-        g_t[...] = jnp.where(x == 0, low[:, 0:HALF], low[:, HALF:D]).T
-        g_t_o[...] = jnp.where(x == 0, low_o[:, 0:HALF], low_o[:, HALF:D]).T
+        g_t[:, 0:ROWS] = jnp.where(x == 0, low[:, 0:HALF], low[:, HALF:D]).T
+        g_t[:, ROWS : 2 * ROWS] = jnp.where(x == 0, low_o[:, 0:HALF], low_o[:, HALF:D]).T
 
     u = dot(n_o[...], w_up[0]) + b_up[0]
-    active_o, slope_o = gelu_parts(u)
+    acts[0:ROWS] = act[...]
 
     @pl.when(t < 2)
     def _():
-        dh_o = (dot_nt(low_o, w_down[0]) * slope_o).astype(BF)
-        g_up = (dot(n_t[...], dh[...]) + dot(n_t_o[...], dh_o)).astype(BF)
+        active_o, slope_o = gelu_parts(u)
+        acts[ROWS : 2 * ROWS] = active_o.astype(BF)
+        dhs[0:ROWS] = dh[...]
+        dhs[ROWS : 2 * ROWS] = (dot_nt(low_o, w_down[0]) * slope_o).astype(BF)
+        g_up = dot(n_t[...], dhs[...]).astype(BF)
         for ref, when in ((send, 0), (keep, 1)):
 
             @pl.when(t == when)
@@ -462,7 +465,11 @@
                     for j in range(2):
                         ref[py, pz, j] = g_up[piece * PART : (piece + 1) * PART, j * HALF : (j + 1) * HALF]
 
-    g_down = (dot(g_t[...], act[...]) + dot(g_t_o[...], active_o.astype(BF))).astype(BF).T
+    @pl.when(t >= 2)
+    def _():
+        acts[ROWS : 2 * ROWS] = gelu_parts(u)[0].astype(BF)
+
+    g_down = dot(g_t[...], acts[...]).astype(BF).T
     tile = ffn_tile(t, sc)
     for half in range(2):
         py, pz = place(sc, 2 * tile + half)
@@ -501,11 +508,11 @@
         [whole(packed), whole(packed)],
         [stored(packed, BF), shape(packed, BF)],
         [
-            pltpu.VMEM((D, ROWS), BF),
+            pltpu.VMEM((D, 2 * ROWS), BF),
             pltpu.VMEM((ROWS, D), BF),
-            pltpu.VMEM((D, ROWS), BF),
-            pltpu.VMEM((HALF, ROWS), BF),
-            pltpu.VMEM((HALF, ROWS), BF),
+            pltpu.VMEM((HALF, 2 * ROWS), BF),
+            pltpu.VMEM((2 * ROWS, BT), BF),
+            pltpu.VMEM((2 * ROWS, BT), BF),
         ],
         (8.6e9, 22e6),
         deps,

time: 302 us -> 300 us (level)
  no operation moved by 1% of the time
where the time goes in v4:
time: 300 us; the launch traced here: 295 us
  Pallas kernels  200 us (67%)
  waiting for transfers between devices  50.6 us (17%)
  starting transfers between devices  39.7 us (13%)
  local copies, waits for them, and re-layouts  3.02 us (1%)
    pallas_call x27, Pallas kernels, call(): return lambda *args: kernel(*args, *deps)  200 us
    ppermute x19, waiting for transfers between devices, to_dp(): return lax.ppermute(value, 'dp', [(i, i ^ distance) for i in range(8)])  37.2 us
    ppermute x19, starting transfers between devices, to_dp(): return lax.ppermute(value, 'dp', [(i, i ^ distance) for i in range(8)])  18.4 us
    ppermute x13, starting transfers between devices, to_chip(): return lax.ppermute(value, 'section', [(0, 2), (2, 0), (1, 3), (3, 1)])  17.4 us
    ppermute x13, waiting for transfers between devices, to_chip(): return lax.ppermute(value, 'section', [(0, 2), (2, 0), (1, 3), (3, 1)])  9.37 us
  transfers between devices with their start and end apart: 52, of which 15 were waited for; matrix products, arithmetic and copies ran while one was open for 0% of the time, Pallas kernels for 56%

profile of v4, /device:TPU:0, one launch (start us, length us, event | category | flops | bytes accessed | tf_op | source)
XLA Modules:
  0.0 294.8 jit_solution(2681589051656347073)
XLA Ops:
  2.9 15.6 %shard_map.237 = (bf16[1024,1152]{1,0:T(8,128)(2,1)}, bf16[1024,384]{1,0:T(8,128)(2,1)}, bf16[2,256,384]{2,1,0:T(8,128)(2,1)S(1)}, bf16[2,256,384]{2,1,0:T(8,128)(2,1)S(1)}, f32[8,1024]{1,0:T(8,128)S(1)}) custom-call(s32[4]{0:T(128)S(1)} %pad_add_fusion.sc, bf16[2,2,2,256,768]{4,3,2,1,0:T(8,128)(2,1)} %bitcast.10, bf16[2,2,2,256,768]{4,3,2,1,0:T(8,128)(2,1)} %bitcast.11, ...), custom_call_target="tpu_custom_call" | custom-call | flops 20999999488 | bytes 40000000 | tf_op jit(solution)/shard_map/pallas_call | solution.py:70
  20.3 13.2 %shard_map.238 = (bf16[512,768]{1,0:T(8,128)(2,1)S(1)}, bf16[512,768]{1,0:T(8,128)(2,1)S(1)}, bf16[512,3072]{1,0:T(8,128)(2,1)}, bf16[512,3072]{1,0:T(8,128)(2,1)}, bf16[2,256,768]{2,1,0:T(8,128)(2,1)S(1)}) custom-call(s32[4]{0:T(128)S(1)} %pad_add_fusion.sc, bf16[2,256,384]{2,1,0:T(8,128)(2,1)S(1)} %get-tuple-element.105.refs_0_, ...), custom_call_target="tpu_custom_call" | custom-call | flops 27000000512 | bytes 100000000 | tf_op jit(solution)/shard_map/pallas_call | solution.py:70
  34.1 2.8 collective-permute-start.4
  36.9 14.9 %shard_map.239 = (bf16[1024,1152]{1,0:T(8,128)(2,1)}, bf16[1024,384]{1,0:T(8,128)(2,1)}, bf16[2,256,384]{2,1,0:T(8,128)(2,1)S(1)}, bf16[2,256,384]{2,1,0:T(8,128)(2,1)S(1)}, f32[8,1024]{1,0:T(8,128)S(1)}) custom-call(s32[4]{0:T(128)S(1)} %pad_add_fusion.sc, bf16[1,2,1,256,768]{4,3,2,1,0:T(8,128)(2,1)S(1)} %bitcast.16, ...), custom_call_target="tpu_custom_call" | custom-call | flops 20999999488 | bytes 40000000 | tf_op jit(solution)/shard_map/pallas_call | solution.py:70
  54.7 2.7 shard_map.240
  59.3 10.9 %shard_map.241 = (bf16[512,3072]{1,0:T(8,128)(2,1)S(1)}, bf16[512,3072]{1,0:T(8,128)(2,1)S(1)}, f32[256,768]{1,0:T(8,128)S(1)}, bf16[256,768]{1,0:T(8,128)(2,1)S(1)}) custom-call(s32[4]{0:T(128)S(1)} %pad_add_fusion.sc, bf16[512,768]{1,0:T(8,128)(2,1)S(1)} %get-tuple-element.111.refs_0_.refs_1_.refs_2_, ...), custom_call_target="tpu_custom_call" | custom-call | flops 24000000000 | bytes 90000000 | tf_op jit(solution)/shard_map/pallas_call | solution.py:70
  70.2 10.2 %shard_map.242 = (bf16[512,3072]{1,0:T(8,128)(2,1)S(1)}, bf16[2,256,768]{2,1,0:T(8,128)(2,1)S(1)}, f32[8,768]{1,0:T(8,128)S(1)}) custom-call(s32[4]{0:T(128)S(1)} %pad_add_fusion.sc, bf16[2,2,2,256,768]{4,3,2,1,0:T(8,128)(2,1)S(1)} %bitcast.20, bf16[512,768]{1,0:T(8,128)(2,1)S(1)} %get-tuple-element.111.refs_0_.refs_1_.refs_2_, ...), custom_call_target="tpu_custom_call" | custom-call | flops 24500000768 | bytes 90000000 | tf_op jit(solution)/shard_map/pallas_call | solution.py:70
  80.5 18.7 %shard_map.243 = (bf16[2,4,4,96,384]{4,3,2,1,0:T(8,128)(2,1)}, bf16[2,4,4,96,384]{4,3,2,1,0:T(8,128)(2,1)S(1)}) custom-call(s32[4]{0:T(128)S(1)} %pad_add_fusion.sc, bf16[2,2,2,256,768]{4,3,2,1,0:T(8,128)(2,1)S(1)} %bitcast.21, bf16[2,2,2,256,768]{4,3,2,1,0:T(8,128)(2,1)S(1)} %bitcast.22, bf16[512,768]{1,0:T(8,128)(2,1)S(1)} %get-tuple-element.111.refs_0_.refs_1_.refs_2_, ...), custom_call_target="tpu_custom_call" | custom-call | flops 43000000512 | bytes 110000000 | tf_op jit(solution)/shard_map/pallas_call | solution.py:70
  99.7 18.7 %shard_map.244 = (bf16[1024,1152]{1,0:T(8,128)(2,1)S(1)}, f32[2,256,768]{2,1,0:T(8,128)S(1)}, bf16[2,256,768]{2,1,0:T(8,128)(2,1)S(1)}) custom-call(s32[4]{0:T(128)S(1)} %pad_add_fusion.sc, bf16[2,256,768]{2,1,0:T(8,128)(2,1)S(1)} %get-tuple-element.114.refs_0_.refs_5_, bf16[2,256,768]{2,1,0:T(8,128)(2,1)S(1)} %collective-permute-done.6.refs_1_.refs_6_, ...), custom_call_target="tpu_custom_call" | custom-call | flops 42500001792 | bytes 60000000 | tf_op jit(solution)/shard_map/pallas_call | solution.py:70
  124.7 11.5 %shard_map.247 = (bf16[512,3072]{1,0:T(8,128)(2,1)S(1)}, bf16[2,256,768]{2,1,0:T(8,128)(2,1)}, f32[8,768]{1,0:T(8,128)S(1)}) custom-call(s32[4]{0:T(128)S(1)} %pad_add_fusion.sc, bf16[1,2,1,256,768]{4,3,2,1,0:T(8,128)(2,1)S(1)} %bitcast.25, bf16[512,768]{1,0:T(8,128)(2,1)S(1)} %copy-done.10, f32[2,1,768]{2,1,0:T(1,128)S(1)} %reshape.70.refs_5_.refs_1_.refs_2_.refs_4_, ...), custom_call_target="tpu_custom_call" | custom-call | flops 24500000768 | bytes 90000000 | tf_op jit(solution)/shard_map/pallas_call | solution.py:70
  136.2 6.8 %shard_map.248 = (bf16[2,4,96,384]{3,2,1,0:T(8,128)(2,1)}, bf16[2,4,96,384]{3,2,1,0:T(8,128)(2,1)}, bf16[2,2,2,96,384]{4,3,2,1,0:T(8,128)(2,1)}, bf16[2,2,2,96,384]{4,3,2,1,0:T(8,128)(2,1)}) custom-call(s32[4]{0:T(128)S(1)} %pad_add_fusion.sc, bf16[1,2,1,256,768]{4,3,2,1,0:T(8,128)(2,1)S(1)} %bitcast.19, bf16[1,2,1,256,768]{4,3,2,1,0:T(8,128)(2,1)S(1)} %bitcast.24, ...), custom_call_target="tpu_custom_call" | custom-call | flops 12499999744 | bytes 60000000 | tf_op jit(solution)/shard_map/pallas_call | solution.py:70
  146.0 18.2 %shard_map.249 = (bf16[2,4,4,96,384]{4,3,2,1,0:T(8,128)(2,1)}, bf16[2,4,4,96,384]{4,3,2,1,0:T(8,128)(2,1)S(1)}) custom-call(s32[4]{0:T(128)S(1)} %pad_add_fusion.sc, bf16[1,2,1,256,768]{4,3,2,1,0:T(8,128)(2,1)S(1)} %bitcast.26, bf16[1,2,1,256,768]{4,3,2,1,0:T(8,128)(2,1)S(1)} %bitcast.27, bf16[512,768]{1,0:T(8,128)(2,1)S(1)} %copy-done.10, ...), custom_call_target="tpu_custom_call" | custom-call | flops 43000000512 | bytes 110000000 | tf_op jit(solution)/shard_map/pallas_call | solution.py:70
  172.0 19.2 %shard_map.252 = (bf16[1024,1152]{1,0:T(8,128)(2,1)S(1)}, f32[2,256,768]{2,1,0:T(8,128)S(1)}, bf16[2,256,768]{2,1,0:T(8,128)(2,1)S(1)}) custom-call(s32[4]{0:T(128)S(1)} %pad_add_fusion.sc, bf16[2,256,768]{2,1,0:T(8,128)(2,1)} %get-tuple-element.132.refs_10_.refs_0_.refs_5_, bf16[2,256,768]{2,1,0:T(8,128)(2,1)} %collective-permute-done.14.refs_1_.refs_6_, ...), custom_call_target="tpu_custom_call" | custom-call | flops 42500001792 | bytes 60000000 | tf_op jit(solution)/shard_map/pallas_call | solution.py:70
  193.8 3.0 %shard_map.254 = (f32[256,768]{1,0:T(8,128)S(1)}, bf16[256,768]{1,0:T(8,128)(2,1)S(1)}, f32[32,768]{1,0:T(8,128)S(1)}) custom-call(s32[4]{0:T(128)S(1)} %pad_add_fusion.sc, bf16[2,256,768]{2,1,0:T(8,128)(2,1)} %get-tuple-element.132.refs_10_.refs_0_.refs_5_, f32[2,256,768]{2,1,0:T(8,128)S(1)} %get-tuple-element.142.refs_10_.refs_1_, ...), custom_call_target="tpu_custom_call" | custom-call | flops 1000000000 | bytes 25000000 | tf_op jit(solution)/shard_map/pallas_call | solution.py:70
  197.4 2.6 collective-permute-start.24
  205.7 7.7 %shard_map.256 = (bf16[2,4,96,384]{3,2,1,0:T(8,128)(2,1)}, bf16[2,4,96,384]{3,2,1,0:T(8,128)(2,1)S(1)}, bf16[4,2,96,384]{3,2,1,0:T(8,128)(2,1)}, bf16[4,2,96,384]{3,2,1,0:T(8,128)(2,1)S(1)}) custom-call(s32[4]{0:T(128)S(1)} %pad_add_fusion.sc, bf16[2,2,2,256,768]{4,3,2,1,0:T(8,128)(2,1)S(1)} %bitcast.14, bf16[2,2,2,256,768]{4,3,2,1,0:T(8,128)(2,1)S(1)} %bitcast.15, ...), custom_call_target="tpu_custom_call" | custom-call | flops 12499999744 | bytes 60000000 | tf_op jit(solution)/shard_map/pallas_call | solution.py:70
  218.8 9.0 %collective-permute-done.22.refs_3_.refs_12_ = bf16[2,4,96,384]{3,2,1,0:T(8,128)(2,1)S(1)} collective-permute-done((bf16[2,4,96,384]{3,2,1,0:T(8,128)(2,1)S(1)}, bf16[2,4,96,384]{3,2,1,0:T(8,128)(2,1)S(1)}, u32[]{:S(2)}, u32[]{:S(2)}) %collective-permute-start.22) | collective-permute-done | bytes 589856 | tf_op jit(solution)/shard_map/ppermute | solution.py:712
  239.4 3.5 %collective-permute-done.36.refs_19_ = f32[32,768]{1,0:T(8,128)S(1)} collective-permute-done((f32[32,768]{1,0:T(8,128)S(1)}, f32[32,768]{1,0:T(8,128)S(1)}, u32[]{:S(2)}, u32[]{:S(2)}) %collective-permute-start.36) | collective-permute-done | bytes 98336 | tf_op jit(solution)/shard_map/ppermute | solution.py:708
  243.5 4.3 %collective-permute-done.33.refs_5_.refs_8_.refs_2_ = bf16[4,96,384]{2,1,0:T(8,128)(2,1)S(1)} collective-permute-done((bf16[4,96,384]{2,1,0:T(8,128)(2,1)S(1)}, bf16[4,96,384]{2,1,0:T(8,128)(2,1)S(1)}, u32[]{:S(2)}, u32[]{:S(2)}) %collective-permute-start.33) | collective-permute-done | bytes 294944 | tf_op jit(solution)/shard_map/ppermute | solution.py:712
  247.9 8.9 %collective-permute-done.34.refs_2_.refs_6_ = bf16[2,2,96,384]{3,2,1,0:T(8,128)(2,1)S(1)} collective-permute-done((bf16[2,2,96,384]{3,2,1,0:T(8,128)(2,1)S(1)}, bf16[2,2,96,384]{3,2,1,0:T(8,128)(2,1)S(1)}, u32[]{:S(2)}, u32[]{:S(2)}) %collective-permute-start.34) | collective-permute-done | bytes 294944 | tf_op jit(solution)/shard_map/ppermute | solution.py:712
  263.4 6.9 %collective-permute-done.40.refs_11_ = f32[32,768]{1,0:T(8,128)S(1)} collective-permute-done((f32[32,768]{1,0:T(8,128)S(1)}, f32[32,768]{1,0:T(8,128)S(1)}, u32[]{:S(2)}, u32[]{:S(2)}) %collective-permute-start.40) | collective-permute-done | bytes 98336 | tf_op jit(solution)/shard_map/ppermute | solution.py:712
  276.3 3.3 %shard_map.258 = (f32[2,1,256,768]{3,2,1,0:T(8,128)}, f32[2,1,256,768]{3,2,1,0:T(8,128)}, f32[2,96,3072]{2,1,0:T(8,128)}, f32[2,384,768]{2,1,0:T(8,128)}) custom-call(s32[4]{0:T(128)S(1)} %pad_add_fusion.sc, f32[256,768]{1,0:T(8,128)S(1)} %get-tuple-element.112.refs_0_, bf16[256,768]{1,0:T(8,128)(2,1)S(1)} %copy-done.3, f32[256,768]{1,0:T(8,128)S(1)} %copy-done.5, ...), custom_call_target="tpu_custom_call" | custom-call | flops 5000000 | bytes 45000000 | tf_op jit(solution)/shard_map/pallas_call | solution.py:70
  286.2 3.4 %collective-permute-done.47.refs_8_ = bf16[2,96,384]{2,1,0:T(8,128)(2,1)S(1)} collective-permute-done((bf16[2,96,384]{2,1,0:T(8,128)(2,1)S(1)}, bf16[2,96,384]{2,1,0:T(8,128)(2,1)S(1)}, u32[]{:S(2)}, u32[]{:S(2)}) %collective-permute-start.47) | collective-permute-done | bytes 147488 | tf_op jit(solution)/shard_map/ppermute | solution.py:708
  291.0 3.3 %shard_map.263 = (f32[2,96,3072]{2,1,0:T(8,128)}, f32[2,384,768]{2,1,0:T(8,128)}, f32[2,96,2304]{2,1,0:T(8,128)}, f32[2,96,768]{2,1,0:T(8,128)}, f32[2,96]{1,0:T...) custom-call(s32[4]{0:T(128)S(1)} %pad_add_fusion.sc, ...), custom_call_target="tpu_custom_call", output_to_operand_aliasing={{0}: (2, {}), {1}: (3, {})} | custom-call | flops 5000000 | bytes 55000000 | tf_op jit(solution)/shard_map/pallas_call | solution.py:70
  (175 shorter events, 73.7 us)
Async XLA Ops:
  33.9 18.4 %collective-permute-start.3 = (bf16[2,256,384]{2,1,0:T(8,128)(2,1)S(1)}, bf16[2,256,384]{2,1,0:T(8,128)(2,1)S(1)}, u32[]{:S(2)}, u32[]{:S(2)}) collective-permute-start(bf16[2,256,384]{2,1,0:T(8,128)(2,1)S(1)} %get-tuple-element.105.refs_0_), channel_id=1, source_target_pairs={{0,8},{8,0},{16,24},{24,16},{1,9},{9,1},{17,25},{25,17},{2,10},{10... | collective-permute-start | bytes 1179656 | tf_op jit(solution)/shard_map/ppermute | solution.py:704
  34.1 20.7 %collective-permute-start.4 = (bf16[512,768]{1,0:T(8,128)(2,1)S(1)}, bf16[512,768]{1,0:T(8,128)(2,1)S(1)}, u32[]{:S(2)}, u32[]{:S(2)}) collective-permute-start(bf16[512,768]{1,0:T(8,128)(2,1)S(1)} %get-tuple-element.110.refs_1_.refs_2_), channel_id=1, source_target_pairs={{0,16},{16,0},{8,24},{24,8},{1,17},{17,1},{9,25},{25,9},{2,18},{18... | collective-permute-start | bytes 2359304 | tf_op jit(solution)/shard_map/ppermute | solution.py:708
  51.9 18.3 %collective-permute-start.5 = (bf16[2,256,384]{2,1,0:T(8,128)(2,1)S(1)}, bf16[2,256,384]{2,1,0:T(8,128)(2,1)S(1)}, u32[]{:S(2)}, u32[]{:S(2)}) collective-permute-start(bf16[2,256,384]{2,1,0:T(8,128)(2,1)S(1)} %get-tuple-element.108.refs_0_), channel_id=1, source_target_pairs={{0,8},{8,0},{16,24},{24,16},{1,9},{9,1},{17,25},{25,17},{2,10},{10... | collective-permute-start | bytes 1179656 | tf_op jit(solution)/shard_map/ppermute | solution.py:704
  57.5 23.1 %collective-permute-start.7 = (bf16[512,768]{1,0:T(8,128)(2,1)S(1)}, bf16[512,768]{1,0:T(8,128)(2,1)S(1)}, u32[]{:S(2)}, u32[]{:S(2)}) collective-permute-start(bf16[512,768]{1,0:T(8,128)(2,1)S(1)} %get-tuple-element.111.refs_0_.refs_1_.refs_2_), channel_id=1, source_target_pairs={{0,16},{16,0},{8,24},{24,8},{1,17},{17,1},{9,25},{25,9},{2,18},{18... | collective-permute-start | bytes 2359304 | tf_op jit(solution)/shard_map/ppermute | solution.py:708
  80.4 19.2 %collective-permute-start.6 = (bf16[2,256,768]{2,1,0:T(8,128)(2,1)S(1)}, bf16[2,256,768]{2,1,0:T(8,128)(2,1)S(1)}, u32[]{:S(2)}, u32[]{:S(2)}) collective-permute-start(bf16[2,256,768]{2,1,0:T(8,128)(2,1)S(1)} %get-tuple-element.114.refs_0_.refs_5_), channel_id=1, source_target_pairs={{0,8},{8,0},{16,24},{24,16},{1,9},{9,1},{17,25},{25,17},{2,10},{10... | collective-permute-start | bytes 2359304 | tf_op jit(solution)/shard_map/ppermute | solution.py:704
  99.2 19.2 %collective-permute-start.9 = (bf16[2,4,4,96,384]{4,3,2,1,0:T(8,128)(2,1)S(1)}, bf16[2,4,4,96,384]{4,3,2,1,0:T(8,128)(2,1)S(1)}, u32[]{:S(2)}, u32[]{:S(2)}) collective-permute-start(bf16[2,4,4,96,384]{4,3,2,1,0:T(8,128)(2,1)S(1)} %get-tuple-element.123), channel_id=1, source_target_pairs={{0,8},{8,0},{16,24},{24,16},{1,9},{9,1},{17,25},{25,17},{2,10},{10... | collective-permute-start | bytes 7077896 | tf_op jit(solution)/shard_map/ppermute | solution.py:704
  120.6 43.6 %collective-permute-start.12 = (bf16[4,4,96,384]{3,2,1,0:T(8,128)(2,1)S(1)}, bf16[4,4,96,384]{3,2,1,0:T(8,128)(2,1)S(1)}, u32[]{:S(2)}, u32[]{:S(2)}) collective-permute-start(bf16[4,4,96,384]{3,2,1,0:T(8,128)(2,1)S(1)} %get-tuple-element.125.refs_5_), channel_id=1, source_target_pairs={{0,1},{1,0},{2,3},{3,2},{4,5},{5,4},{6,7},{7,6},{8,9},{9,8},{10,11... | collective-permute-start | bytes 3538952 | tf_op jit(solution)/shard_map/ppermute | solution.py:712
  124.1 22.0 %collective-permute-start.10 = (bf16[2,256,768]{2,1,0:T(8,128)(2,1)S(1)}, bf16[2,256,768]{2,1,0:T(8,128)(2,1)S(1)}, u32[]{:S(2)}, u32[]{:S(2)}) collective-permute-start(bf16[2,256,768]{2,1,0:T(8,128)(2,1)S(1)} %get-tuple-element.126), channel_id=1, source_target_pairs={{0,16},{16,0},{8,24},{24,8},{1,17},{17,1},{9,25},{25,9},{2,18},{18... | collective-permute-start | bytes 2359304 | tf_op jit(solution)/shard_map/ppermute | solution.py:708
  136.2 35.3 %collective-permute-start.14 = (bf16[2,256,768]{2,1,0:T(8,128)(2,1)}, bf16[2,256,768]{2,1,0:T(8,128)(2,1)}, u32[]{:S(2)}, u32[]{:S(2)}) collective-permute-start(bf16[2,256,768]{2,1,0:T(8,128)(2,1)} %get-tuple-element.132.refs_10_.refs_0_.refs_5_), channel_id=1, source_target_pairs={{0,8},{8,0},{16,24},{24,16},{1,9},{9,1},{17,25},{25,17},{2,10},{10... | collective-permute-start | bytes 2359304 | tf_op jit(solution)/shard_map/ppermute | solution.py:704
  143.0 48.2 %collective-permute-start.17 = (bf16[2,2,2,96,384]{4,3,2,1,0:T(8,128)(2,1)}, bf16[2,2,2,96,384]{4,3,2,1,0:T(8,128)(2,1)}, u32[]{:S(2)}, u32[]{:S(2)}) collective-permute-start(bf16[2,2,2,96,384]{4,3,2,1,0:T(8,128)(2,1)} %get-tuple-element.148), channel_id=1, source_target_pairs={{0,2},{1,3},{2,0},{3,1},{4,6},{5,7},{6,4},{7,5},{8,10},{9,11},{10,... | collective-permute-start | bytes 1769480 | tf_op jit(solution)/shard_map/ppermute | solution.py:712
  144.5 46.7 %collective-permute-start.18 = (bf16[2,4,96,384]{3,2,1,0:T(8,128)(2,1)}, bf16[2,4,96,384]{3,2,1,0:T(8,128)(2,1)}, u32[]{:S(2)}, u32[]{:S(2)}) collective-permute-start(bf16[2,4,96,384]{3,2,1,0:T(8,128)(2,1)} %get-tuple-element.149), channel_id=1, source_target_pairs={{0,16},{16,0},{8,24},{24,8},{1,17},{17,1},{9,25},{25,9},{2,18},{18... | collective-permute-start | bytes 1769480 | tf_op jit(solution)/shard_map/ppermute | solution.py:708
  166.0 25.2 %collective-permute-start.16 = (bf16[2,4,96,384]{3,2,1,0:T(8,128)(2,1)S(1)}, bf16[2,4,96,384]{3,2,1,0:T(8,128)(2,1)S(1)}, u32[]{:S(2)}, u32[]{:S(2)}) collective-permute-start(bf16[2,4,96,384]{3,2,1,0:T(8,128)(2,1)S(1)} %shard_map.250.refs_3_), channel_id=1, source_target_pairs={{0,2},{1,3},{2,0},{3,1},{4,6},{5,7},{6,4},{7,5},{8,10},{9,11},{10,... | collective-permute-start | bytes 1769480 | tf_op jit(solution)/shard_map/ppermute | solution.py:712
  170.8 22.9 %collective-permute-start.13 = (bf16[256,768]{1,0:T(8,128)(2,1)S(1)}, bf16[256,768]{1,0:T(8,128)(2,1)S(1)}, u32[]{:S(2)}, u32[]{:S(2)}) collective-permute-start(bf16[256,768]{1,0:T(8,128)(2,1)S(1)} %get-tuple-element.137), channel_id=1, source_target_pairs={{0,16},{16,0},{8,24},{24,8},{1,17},{17,1},{9,25},{25,9},{2,18},{18... | collective-permute-start | bytes 1179656 | tf_op jit(solution)/shard_map/ppermute | solution.py:708
  171.4 31.6 %collective-permute-start.20 = (bf16[4,4,96,384]{3,2,1,0:T(8,128)(2,1)S(1)}, bf16[4,4,96,384]{3,2,1,0:T(8,128)(2,1)S(1)}, u32[]{:S(2)}, u32[]{:S(2)}) collective-permute-start(bf16[4,4,96,384]{3,2,1,0:T(8,128)(2,1)S(1)} %get-tuple-element.141.refs_8_), channel_id=1, source_target_pairs={{0,1},{1,0},{2,3},{3,2},{4,5},{5,4},{6,7},{7,6},{8,9},{9,8},{10,11... | collective-permute-start | bytes 3538952 | tf_op jit(solution)/shard_map/ppermute | solution.py:712
  197.4 18.3 %collective-permute-start.24 = (bf16[4,96,384]{2,1,0:T(8,128)(2,1)S(1)}, bf16[4,96,384]{2,1,0:T(8,128)(2,1)S(1)}, u32[]{:S(2)}, u32[]{:S(2)}) collective-permute-start(bf16[4,96,384]{2,1,0:T(8,128)(2,1)S(1)} %get-tuple-element.150.refs_8_), channel_id=1, source_target_pairs={{0,4},{1,5},{2,6},{3,7},{4,0},{5,1},{6,2},{7,3},{8,12},{9,13},{10,... | collective-permute-start | bytes 884744 | tf_op jit(solution)/shard_map/ppermute | solution.py:712
  200.0 17.2 %collective-permute-start.23 = (bf16[8,96,384]{2,1,0:T(8,128)(2,1)S(1)}, bf16[8,96,384]{2,1,0:T(8,128)(2,1)S(1)}, u32[]{:S(2)}, u32[]{:S(2)}) collective-permute-start(bf16[8,96,384]{2,1,0:T(8,128)(2,1)S(1)} %get-tuple-element.155), channel_id=1, source_target_pairs={{0,1},{1,0},{2,3},{3,2},{4,5},{5,4},{6,7},{7,6},{8,9},{9,8},{10,11... | collective-permute-start | bytes 1769480 | tf_op jit(solution)/shard_map/ppermute | solution.py:712
  201.5 29.3 %collective-permute-start.19 = (bf16[256,768]{1,0:T(8,128)(2,1)S(1)}, bf16[256,768]{1,0:T(8,128)(2,1)S(1)}, u32[]{:S(2)}, u32[]{:S(2)}) collective-permute-start(bf16[256,768]{1,0:T(8,128)(2,1)S(1)} %get-tuple-element.152), channel_id=1, source_target_pairs={{0,16},{16,0},{8,24},{24,8},{1,17},{17,1},{9,25},{25,9},{2,18},{18... | collective-permute-start | bytes 1179656 | tf_op jit(solution)/shard_map/ppermute | solution.py:708
  204.8 14.0 %collective-permute-start.25 = (f32[32,768]{1,0:T(8,128)S(1)}, f32[32,768]{1,0:T(8,128)S(1)}, u32[]{:S(2)}, u32[]{:S(2)}) collective-permute-start(f32[32,768]{1,0:T(8,128)S(1)} %get-tuple-element.156.refs_18_), channel_id=1, source_target_pairs={{0,4},{1,5},{2,6},{3,7},{4,0},{5,1},{6,2},{7,3},{8,12},{9,13},{10,... | collective-permute-start | bytes 294920 | tf_op jit(solution)/shard_map/ppermute | solution.py:712
  205.2 22.5 %collective-permute-start.22 = (bf16[2,4,96,384]{3,2,1,0:T(8,128)(2,1)S(1)}, bf16[2,4,96,384]{3,2,1,0:T(8,128)(2,1)S(1)}, u32[]{:S(2)}, u32[]{:S(2)}) collective-permute-start(bf16[2,4,96,384]{3,2,1,0:T(8,128)(2,1)S(1)} %get-tuple-element.154.refs_10_), channel_id=1, source_target_pairs={{0,2},{1,3},{2,0},{3,1},{4,6},{5,7},{6,4},{7,5},{8,10},{9,11},{10,... | collective-permute-start | bytes 1769480 | tf_op jit(solution)/shard_map/ppermute | solution.py:712
  215.7 16.2 %collective-permute-start.29 = (bf16[2,4,96,384]{3,2,1,0:T(8,128)(2,1)S(1)}, bf16[2,4,96,384]{3,2,1,0:T(8,128)(2,1)S(1)}, u32[]{:S(2)}, u32[]{:S(2)}) collective-permute-start(bf16[2,4,96,384]{3,2,1,0:T(8,128)(2,1)S(1)} %get-tuple-element.163), channel_id=1, source_target_pairs={{0,16},{16,0},{8,24},{24,8},{1,17},{17,1},{9,25},{25,9},{2,18},{18... | collective-permute-start | bytes 1769480 | tf_op jit(solution)/shard_map/ppermute | solution.py:708
  217.2 16.0 %collective-permute-start.30 = (bf16[4,2,96,384]{3,2,1,0:T(8,128)(2,1)S(1)}, bf16[4,2,96,384]{3,2,1,0:T(8,128)(2,1)S(1)}, u32[]{:S(2)}, u32[]{:S(2)}) collective-permute-start(bf16[4,2,96,384]{3,2,1,0:T(8,128)(2,1)S(1)} %get-tuple-element.165), channel_id=1, source_target_pairs={{0,1},{1,0},{2,3},{3,2},{4,5},{5,4},{6,7},{7,6},{8,9},{9,8},{10,11... | collective-permute-start | bytes 1769480 | tf_op jit(solution)/shard_map/ppermute | solution.py:712
  231.9 24.9 %collective-permute-start.35 = (bf16[6,96,384]{2,1,0:T(8,128)(2,1)S(1)}, bf16[6,96,384]{2,1,0:T(8,128)(2,1)S(1)}, u32[]{:S(2)}, u32[]{:S(2)}) collective-permute-start(bf16[6,96,384]{2,1,0:T(8,128)(2,1)S(1)} %get-tuple-element.170), channel_id=1, source_target_pairs={{0,4},{1,5},{2,6},{3,7},{4,0},{5,1},{6,2},{7,3},{8,12},{9,13},{10,... | collective-permute-start | bytes 1327112 | tf_op jit(solution)/shard_map/ppermute | solution.py:712
  243.0 13.8 %collective-permute-start.34 = (bf16[2,2,96,384]{3,2,1,0:T(8,128)(2,1)S(1)}, bf16[2,2,96,384]{3,2,1,0:T(8,128)(2,1)S(1)}, u32[]{:S(2)}, u32[]{:S(2)}) collective-permute-start(bf16[2,2,96,384]{3,2,1,0:T(8,128)(2,1)S(1)} %get-tuple-element.169), channel_id=1, source_target_pairs={{0,2},{1,3},{2,0},{3,1},{4,6},{5,7},{6,4},{7,5},{8,10},{9,11},{10,... | collective-permute-start | bytes 884744 | tf_op jit(solution)/shard_map/ppermute | solution.py:712
  243.5 13.3 %collective-permute-start.28 = (bf16[4,96,384]{2,1,0:T(8,128)(2,1)S(1)}, bf16[4,96,384]{2,1,0:T(8,128)(2,1)S(1)}, u32[]{:S(2)}, u32[]{:S(2)}) collective-permute-start(bf16[4,96,384]{2,1,0:T(8,128)(2,1)S(1)} %collective-permute-done.26.refs_5_.refs_20_), channel_id=1, source_target_pairs={{0,8},{8,0},{16,24},{24,16},{1,9},{9,1},{17,25},{25,17},{2,10},{10... | collective-permute-start | bytes 884744 | tf_op jit(solution)/shard_map/ppermute | solution.py:704
  (58 other events, 477.4 us)

commit v5 on v4

--- a/solution.py
+++ b/solution.py
@@ -579,9 +579,9 @@
 
     for copy in copies:
         copy.wait()
+    parts = dot_nt(d_qkv[...], sides[...])
     for b in range(4):
-        rows = slice(b * BLOCK, (b + 1) * BLOCK)
-        part = dot_nt(d_qkv[rows], sides[...])
+        part = parts[b * BLOCK : (b + 1) * BLOCK]
 
         @pl.when(core == b % 2)
         def _():

time: 300 us -> 297 us (0.990)
  Pallas kernels: 200 us -> 197 us
  transfers between devices with their start and end apart: 52 -> 52, of which waited for: 15 -> 15; matrix products, arithmetic and copies ran while one was open for 0% -> 0% of each run, Pallas kernels for 56% -> 55%
where the time goes in v5:
time: 297 us; the launch traced here: 292 us
  Pallas kernels  197 us (66%)
  waiting for transfers between devices  50.6 us (17%)
  starting transfers between devices  39.7 us (13%)
  local copies, waits for them, and re-layouts  3.02 us (1%)
    pallas_call x27, Pallas kernels, call(): return lambda *args: kernel(*args, *deps)  197 us
    ppermute x19, waiting for transfers between devices, to_dp(): return lax.ppermute(value, 'dp', [(i, i ^ distance) for i in range(8)])  37.2 us
    ppermute x19, starting transfers between devices, to_dp(): return lax.ppermute(value, 'dp', [(i, i ^ distance) for i in range(8)])  18.4 us
    ppermute x13, starting transfers between devices, to_chip(): return lax.ppermute(value, 'section', [(0, 2), (2, 0), (1, 3), (3, 1)])  17.4 us
    ppermute x13, waiting for transfers between devices, to_chip(): return lax.ppermute(value, 'section', [(0, 2), (2, 0), (1, 3), (3, 1)])  9.33 us
  transfers between devices with their start and end apart: 52, of which 15 were waited for; matrix products, arithmetic and copies ran while one was open for 0% of the time, Pallas kernels for 55%

profile of v5, /device:TPU:0, one launch (start us, length us, event | category | flops | bytes accessed | tf_op | source)
XLA Modules:
  0.0 292.3 jit_solution(5234669041404924848)
XLA Ops:
  2.9 15.6 %shard_map.237 = (bf16[1024,1152]{1,0:T(8,128)(2,1)}, bf16[1024,384]{1,0:T(8,128)(2,1)}, bf16[2,256,384]{2,1,0:T(8,128)(2,1)S(1)}, bf16[2,256,384]{2,1,0:T(8,128)(2,1)S(1)}, f32[8,1024]{1,0:T(8,128)S(1)}) custom-call(s32[4]{0:T(128)S(1)} %pad_add_fusion.sc, bf16[2,2,2,256,768]{4,3,2,1,0:T(8,128)(2,1)} %bitcast.10, bf16[2,2,2,256,768]{4,3,2,1,0:T(8,128)(2,1)} %bitcast.11, ...), custom_call_target="tpu_custom_call" | custom-call | flops 20999999488 | bytes 40000000 | tf_op jit(solution)/shard_map/pallas_call | solution.py:70
  20.3 13.2 %shard_map.238 = (bf16[512,768]{1,0:T(8,128)(2,1)S(1)}, bf16[512,768]{1,0:T(8,128)(2,1)S(1)}, bf16[512,3072]{1,0:T(8,128)(2,1)}, bf16[512,3072]{1,0:T(8,128)(2,1)}, bf16[2,256,768]{2,1,0:T(8,128)(2,1)S(1)}) custom-call(s32[4]{0:T(128)S(1)} %pad_add_fusion.sc, bf16[2,256,384]{2,1,0:T(8,128)(2,1)S(1)} %get-tuple-element.105.refs_0_, ...), custom_call_target="tpu_custom_call" | custom-call | flops 27000000512 | bytes 100000000 | tf_op jit(solution)/shard_map/pallas_call | solution.py:70
  34.1 2.8 collective-permute-start.4
  36.9 14.9 %shard_map.239 = (bf16[1024,1152]{1,0:T(8,128)(2,1)}, bf16[1024,384]{1,0:T(8,128)(2,1)}, bf16[2,256,384]{2,1,0:T(8,128)(2,1)S(1)}, bf16[2,256,384]{2,1,0:T(8,128)(2,1)S(1)}, f32[8,1024]{1,0:T(8,128)S(1)}) custom-call(s32[4]{0:T(128)S(1)} %pad_add_fusion.sc, bf16[1,2,1,256,768]{4,3,2,1,0:T(8,128)(2,1)S(1)} %bitcast.16, ...), custom_call_target="tpu_custom_call" | custom-call | flops 20999999488 | bytes 40000000 | tf_op jit(solution)/shard_map/pallas_call | solution.py:70
  54.7 2.7 shard_map.240
  59.3 10.9 %shard_map.241 = (bf16[512,3072]{1,0:T(8,128)(2,1)S(1)}, bf16[512,3072]{1,0:T(8,128)(2,1)S(1)}, f32[256,768]{1,0:T(8,128)S(1)}, bf16[256,768]{1,0:T(8,128)(2,1)S(1)}) custom-call(s32[4]{0:T(128)S(1)} %pad_add_fusion.sc, bf16[512,768]{1,0:T(8,128)(2,1)S(1)} %get-tuple-element.111.refs_0_.refs_1_.refs_2_, ...), custom_call_target="tpu_custom_call" | custom-call | flops 24000000000 | bytes 90000000 | tf_op jit(solution)/shard_map/pallas_call | solution.py:70
  70.2 10.2 %shard_map.242 = (bf16[512,3072]{1,0:T(8,128)(2,1)S(1)}, bf16[2,256,768]{2,1,0:T(8,128)(2,1)S(1)}, f32[8,768]{1,0:T(8,128)S(1)}) custom-call(s32[4]{0:T(128)S(1)} %pad_add_fusion.sc, bf16[2,2,2,256,768]{4,3,2,1,0:T(8,128)(2,1)S(1)} %bitcast.20, bf16[512,768]{1,0:T(8,128)(2,1)S(1)} %get-tuple-element.111.refs_0_.refs_1_.refs_2_, ...), custom_call_target="tpu_custom_call" | custom-call | flops 24500000768 | bytes 90000000 | tf_op jit(solution)/shard_map/pallas_call | solution.py:70
  80.5 18.7 %shard_map.243 = (bf16[2,4,4,96,384]{4,3,2,1,0:T(8,128)(2,1)}, bf16[2,4,4,96,384]{4,3,2,1,0:T(8,128)(2,1)S(1)}) custom-call(s32[4]{0:T(128)S(1)} %pad_add_fusion.sc, bf16[2,2,2,256,768]{4,3,2,1,0:T(8,128)(2,1)S(1)} %bitcast.21, bf16[2,2,2,256,768]{4,3,2,1,0:T(8,128)(2,1)S(1)} %bitcast.22, bf16[512,768]{1,0:T(8,128)(2,1)S(1)} %get-tuple-element.111.refs_0_.refs_1_.refs_2_, ...), custom_call_target="tpu_custom_call" | custom-call | flops 43000000512 | bytes 110000000 | tf_op jit(solution)/shard_map/pallas_call | solution.py:70
  99.7 17.5 %shard_map.244 = (bf16[1024,1152]{1,0:T(8,128)(2,1)S(1)}, f32[2,256,768]{2,1,0:T(8,128)S(1)}, bf16[2,256,768]{2,1,0:T(8,128)(2,1)S(1)}) custom-call(s32[4]{0:T(128)S(1)} %pad_add_fusion.sc, bf16[2,256,768]{2,1,0:T(8,128)(2,1)S(1)} %get-tuple-element.114.refs_0_.refs_5_, bf16[2,256,768]{2,1,0:T(8,128)(2,1)S(1)} %collective-permute-done.6.refs_1_.refs_6_, ...), custom_call_target="tpu_custom_call" | custom-call | flops 42500001792 | bytes 60000000 | tf_op jit(solution)/shard_map/pallas_call | solution.py:70
  123.5 11.5 %shard_map.247 = (bf16[512,3072]{1,0:T(8,128)(2,1)S(1)}, bf16[2,256,768]{2,1,0:T(8,128)(2,1)}, f32[8,768]{1,0:T(8,128)S(1)}) custom-call(s32[4]{0:T(128)S(1)} %pad_add_fusion.sc, bf16[1,2,1,256,768]{4,3,2,1,0:T(8,128)(2,1)S(1)} %bitcast.25, bf16[512,768]{1,0:T(8,128)(2,1)S(1)} %copy-done.10, f32[2,1,768]{2,1,0:T(1,128)S(1)} %reshape.70.refs_5_.refs_1_.refs_2_.refs_4_, ...), custom_call_target="tpu_custom_call" | custom-call | flops 24500000768 | bytes 90000000 | tf_op jit(solution)/shard_map/pallas_call | solution.py:70
  135.0 6.8 %shard_map.248 = (bf16[2,4,96,384]{3,2,1,0:T(8,128)(2,1)}, bf16[2,4,96,384]{3,2,1,0:T(8,128)(2,1)}, bf16[2,2,2,96,384]{4,3,2,1,0:T(8,128)(2,1)}, bf16[2,2,2,96,384]{4,3,2,1,0:T(8,128)(2,1)}) custom-call(s32[4]{0:T(128)S(1)} %pad_add_fusion.sc, bf16[1,2,1,256,768]{4,3,2,1,0:T(8,128)(2,1)S(1)} %bitcast.19, bf16[1,2,1,256,768]{4,3,2,1,0:T(8,128)(2,1)S(1)} %bitcast.24, ...), custom_call_target="tpu_custom_call" | custom-call | flops 12499999744 | bytes 60000000 | tf_op jit(solution)/shard_map/pallas_call | solution.py:70
  144.9 18.2 %shard_map.249 = (bf16[2,4,4,96,384]{4,3,2,1,0:T(8,128)(2,1)}, bf16[2,4,4,96,384]{4,3,2,1,0:T(8,128)(2,1)S(1)}) custom-call(s32[4]{0:T(128)S(1)} %pad_add_fusion.sc, bf16[1,2,1,256,768]{4,3,2,1,0:T(8,128)(2,1)S(1)} %bitcast.26, bf16[1,2,1,256,768]{4,3,2,1,0:T(8,128)(2,1)S(1)} %bitcast.27, bf16[512,768]{1,0:T(8,128)(2,1)S(1)} %copy-done.10, ...), custom_call_target="tpu_custom_call" | custom-call | flops 43000000512 | bytes 110000000 | tf_op jit(solution)/shard_map/pallas_call | solution.py:70
  170.8 18.0 %shard_map.252 = (bf16[1024,1152]{1,0:T(8,128)(2,1)S(1)}, f32[2,256,768]{2,1,0:T(8,128)S(1)}, bf16[2,256,768]{2,1,0:T(8,128)(2,1)S(1)}) custom-call(s32[4]{0:T(128)S(1)} %pad_add_fusion.sc, bf16[2,256,768]{2,1,0:T(8,128)(2,1)} %get-tuple-element.132.refs_10_.refs_0_.refs_5_, bf16[2,256,768]{2,1,0:T(8,128)(2,1)} %collective-permute-done.14.refs_1_.refs_6_, ...), custom_call_target="tpu_custom_call" | custom-call | flops 42500001792 | bytes 60000000 | tf_op jit(solution)/shard_map/pallas_call | solution.py:70
  191.4 3.0 %shard_map.254 = (f32[256,768]{1,0:T(8,128)S(1)}, bf16[256,768]{1,0:T(8,128)(2,1)S(1)}, f32[32,768]{1,0:T(8,128)S(1)}) custom-call(s32[4]{0:T(128)S(1)} %pad_add_fusion.sc, bf16[2,256,768]{2,1,0:T(8,128)(2,1)} %get-tuple-element.132.refs_10_.refs_0_.refs_5_, f32[2,256,768]{2,1,0:T(8,128)S(1)} %get-tuple-element.142.refs_10_.refs_1_, ...), custom_call_target="tpu_custom_call" | custom-call | flops 1000000000 | bytes 25000000 | tf_op jit(solution)/shard_map/pallas_call | solution.py:70
  195.0 2.6 collective-permute-start.24
  203.3 7.7 %shard_map.256 = (bf16[2,4,96,384]{3,2,1,0:T(8,128)(2,1)}, bf16[2,4,96,384]{3,2,1,0:T(8,128)(2,1)S(1)}, bf16[4,2,96,384]{3,2,1,0:T(8,128)(2,1)}, bf16[4,2,96,384]{3,2,1,0:T(8,128)(2,1)S(1)}) custom-call(s32[4]{0:T(128)S(1)} %pad_add_fusion.sc, bf16[2,2,2,256,768]{4,3,2,1,0:T(8,128)(2,1)S(1)} %bitcast.14, bf16[2,2,2,256,768]{4,3,2,1,0:T(8,128)(2,1)S(1)} %bitcast.15, ...), custom_call_target="tpu_custom_call" | custom-call | flops 12499999744 | bytes 60000000 | tf_op jit(solution)/shard_map/pallas_call | solution.py:70
  216.4 9.0 %collective-permute-done.22.refs_3_.refs_12_ = bf16[2,4,96,384]{3,2,1,0:T(8,128)(2,1)S(1)} collective-permute-done((bf16[2,4,96,384]{3,2,1,0:T(8,128)(2,1)S(1)}, bf16[2,4,96,384]{3,2,1,0:T(8,128)(2,1)S(1)}, u32[]{:S(2)}, u32[]{:S(2)}) %collective-permute-start.22) | collective-permute-done | bytes 589856 | tf_op jit(solution)/shard_map/ppermute | solution.py:712
  237.1 3.4 %collective-permute-done.36.refs_19_ = f32[32,768]{1,0:T(8,128)S(1)} collective-permute-done((f32[32,768]{1,0:T(8,128)S(1)}, f32[32,768]{1,0:T(8,128)S(1)}, u32[]{:S(2)}, u32[]{:S(2)}) %collective-permute-start.36) | collective-permute-done | bytes 98336 | tf_op jit(solution)/shard_map/ppermute | solution.py:708
  241.2 4.5 %collective-permute-done.33.refs_5_.refs_8_.refs_2_ = bf16[4,96,384]{2,1,0:T(8,128)(2,1)S(1)} collective-permute-done((bf16[4,96,384]{2,1,0:T(8,128)(2,1)S(1)}, bf16[4,96,384]{2,1,0:T(8,128)(2,1)S(1)}, u32[]{:S(2)}, u32[]{:S(2)}) %collective-permute-start.33) | collective-permute-done | bytes 294944 | tf_op jit(solution)/shard_map/ppermute | solution.py:712
  245.7 8.6 %collective-permute-done.34.refs_2_.refs_6_ = bf16[2,2,96,384]{3,2,1,0:T(8,128)(2,1)S(1)} collective-permute-done((bf16[2,2,96,384]{3,2,1,0:T(8,128)(2,1)S(1)}, bf16[2,2,96,384]{3,2,1,0:T(8,128)(2,1)S(1)}, u32[]{:S(2)}, u32[]{:S(2)}) %collective-permute-start.34) | collective-permute-done | bytes 294944 | tf_op jit(solution)/shard_map/ppermute | solution.py:712
  260.6 7.1 %collective-permute-done.40.refs_11_ = f32[32,768]{1,0:T(8,128)S(1)} collective-permute-done((f32[32,768]{1,0:T(8,128)S(1)}, f32[32,768]{1,0:T(8,128)S(1)}, u32[]{:S(2)}, u32[]{:S(2)}) %collective-permute-start.40) | collective-permute-done | bytes 98336 | tf_op jit(solution)/shard_map/ppermute | solution.py:712
  273.7 3.3 %shard_map.258 = (f32[2,1,256,768]{3,2,1,0:T(8,128)}, f32[2,1,256,768]{3,2,1,0:T(8,128)}, f32[2,96,3072]{2,1,0:T(8,128)}, f32[2,384,768]{2,1,0:T(8,128)}) custom-call(s32[4]{0:T(128)S(1)} %pad_add_fusion.sc, f32[256,768]{1,0:T(8,128)S(1)} %get-tuple-element.112.refs_0_, bf16[256,768]{1,0:T(8,128)(2,1)S(1)} %copy-done.3, f32[256,768]{1,0:T(8,128)S(1)} %copy-done.5, ...), custom_call_target="tpu_custom_call" | custom-call | flops 5000000 | bytes 45000000 | tf_op jit(solution)/shard_map/pallas_call | solution.py:70
  283.6 3.5 %collective-permute-done.47.refs_8_ = bf16[2,96,384]{2,1,0:T(8,128)(2,1)S(1)} collective-permute-done((bf16[2,96,384]{2,1,0:T(8,128)(2,1)S(1)}, bf16[2,96,384]{2,1,0:T(8,128)(2,1)S(1)}, u32[]{:S(2)}, u32[]{:S(2)}) %collective-permute-start.47) | collective-permute-done | bytes 147488 | tf_op jit(solution)/shard_map/ppermute | solution.py:708
  288.5 3.3 %shard_map.263 = (f32[2,96,3072]{2,1,0:T(8,128)}, f32[2,384,768]{2,1,0:T(8,128)}, f32[2,96,2304]{2,1,0:T(8,128)}, f32[2,96,768]{2,1,0:T(8,128)}, f32[2,96]{1,0:T...) custom-call(s32[4]{0:T(128)S(1)} %pad_add_fusion.sc, ...), custom_call_target="tpu_custom_call", output_to_operand_aliasing={{0}: (2, {}), {1}: (3, {})} | custom-call | flops 5000000 | bytes 55000000 | tf_op jit(solution)/shard_map/pallas_call | solution.py:70
  (175 shorter events, 73.6 us)
Async XLA Ops:
  33.9 18.4 %collective-permute-start.3 = (bf16[2,256,384]{2,1,0:T(8,128)(2,1)S(1)}, bf16[2,256,384]{2,1,0:T(8,128)(2,1)S(1)}, u32[]{:S(2)}, u32[]{:S(2)}) collective-permute-start(bf16[2,256,384]{2,1,0:T(8,128)(2,1)S(1)} %get-tuple-element.105.refs_0_), channel_id=1, source_target_pairs={{0,8},{8,0},{16,24},{24,16},{1,9},{9,1},{17,25},{25,17},{2,10},{10... | collective-permute-start | bytes 1179656 | tf_op jit(solution)/shard_map/ppermute | solution.py:704
  34.1 20.7 %collective-permute-start.4 = (bf16[512,768]{1,0:T(8,128)(2,1)S(1)}, bf16[512,768]{1,0:T(8,128)(2,1)S(1)}, u32[]{:S(2)}, u32[]{:S(2)}) collective-permute-start(bf16[512,768]{1,0:T(8,128)(2,1)S(1)} %get-tuple-element.110.refs_1_.refs_2_), channel_id=1, source_target_pairs={{0,16},{16,0},{8,24},{24,8},{1,17},{17,1},{9,25},{25,9},{2,18},{18... | collective-permute-start | bytes 2359304 | tf_op jit(solution)/shard_map/ppermute | solution.py:708
  51.9 18.3 %collective-permute-start.5 = (bf16[2,256,384]{2,1,0:T(8,128)(2,1)S(1)}, bf16[2,256,384]{2,1,0:T(8,128)(2,1)S(1)}, u32[]{:S(2)}, u32[]{:S(2)}) collective-permute-start(bf16[2,256,384]{2,1,0:T(8,128)(2,1)S(1)} %get-tuple-element.108.refs_0_), channel_id=1, source_target_pairs={{0,8},{8,0},{16,24},{24,16},{1,9},{9,1},{17,25},{25,17},{2,10},{10... | collective-permute-start | bytes 1179656 | tf_op jit(solution)/shard_map/ppermute | solution.py:704
  57.5 23.1 %collective-permute-start.7 = (bf16[512,768]{1,0:T(8,128)(2,1)S(1)}, bf16[512,768]{1,0:T(8,128)(2,1)S(1)}, u32[]{:S(2)}, u32[]{:S(2)}) collective-permute-start(bf16[512,768]{1,0:T(8,128)(2,1)S(1)} %get-tuple-element.111.refs_0_.refs_1_.refs_2_), channel_id=1, source_target_pairs={{0,16},{16,0},{8,24},{24,8},{1,17},{17,1},{9,25},{25,9},{2,18},{18... | collective-permute-start | bytes 2359304 | tf_op jit(solution)/shard_map/ppermute | solution.py:708
  80.4 19.2 %collective-permute-start.6 = (bf16[2,256,768]{2,1,0:T(8,128)(2,1)S(1)}, bf16[2,256,768]{2,1,0:T(8,128)(2,1)S(1)}, u32[]{:S(2)}, u32[]{:S(2)}) collective-permute-start(bf16[2,256,768]{2,1,0:T(8,128)(2,1)S(1)} %get-tuple-element.114.refs_0_.refs_5_), channel_id=1, source_target_pairs={{0,8},{8,0},{16,24},{24,16},{1,9},{9,1},{17,25},{25,17},{2,10},{10... | collective-permute-start | bytes 2359304 | tf_op jit(solution)/shard_map/ppermute | solution.py:704
  99.2 18.1 %collective-permute-start.9 = (bf16[2,4,4,96,384]{4,3,2,1,0:T(8,128)(2,1)S(1)}, bf16[2,4,4,96,384]{4,3,2,1,0:T(8,128)(2,1)S(1)}, u32[]{:S(2)}, u32[]{:S(2)}) collective-permute-start(bf16[2,4,4,96,384]{4,3,2,1,0:T(8,128)(2,1)S(1)} %get-tuple-element.123), channel_id=1, source_target_pairs={{0,8},{8,0},{16,24},{24,16},{1,9},{9,1},{17,25},{25,17},{2,10},{10... | collective-permute-start | bytes 7077896 | tf_op jit(solution)/shard_map/ppermute | solution.py:704
  119.4 43.6 %collective-permute-start.12 = (bf16[4,4,96,384]{3,2,1,0:T(8,128)(2,1)S(1)}, bf16[4,4,96,384]{3,2,1,0:T(8,128)(2,1)S(1)}, u32[]{:S(2)}, u32[]{:S(2)}) collective-permute-start(bf16[4,4,96,384]{3,2,1,0:T(8,128)(2,1)S(1)} %get-tuple-element.125.refs_5_), channel_id=1, source_target_pairs={{0,1},{1,0},{2,3},{3,2},{4,5},{5,4},{6,7},{7,6},{8,9},{9,8},{10,11... | collective-permute-start | bytes 3538952 | tf_op jit(solution)/shard_map/ppermute | solution.py:712
  122.9 22.0 %collective-permute-start.10 = (bf16[2,256,768]{2,1,0:T(8,128)(2,1)S(1)}, bf16[2,256,768]{2,1,0:T(8,128)(2,1)S(1)}, u32[]{:S(2)}, u32[]{:S(2)}) collective-permute-start(bf16[2,256,768]{2,1,0:T(8,128)(2,1)S(1)} %get-tuple-element.126), channel_id=1, source_target_pairs={{0,16},{16,0},{8,24},{24,8},{1,17},{17,1},{9,25},{25,9},{2,18},{18... | collective-permute-start | bytes 2359304 | tf_op jit(solution)/shard_map/ppermute | solution.py:708
  135.0 35.3 %collective-permute-start.14 = (bf16[2,256,768]{2,1,0:T(8,128)(2,1)}, bf16[2,256,768]{2,1,0:T(8,128)(2,1)}, u32[]{:S(2)}, u32[]{:S(2)}) collective-permute-start(bf16[2,256,768]{2,1,0:T(8,128)(2,1)} %get-tuple-element.132.refs_10_.refs_0_.refs_5_), channel_id=1, source_target_pairs={{0,8},{8,0},{16,24},{24,16},{1,9},{9,1},{17,25},{25,17},{2,10},{10... | collective-permute-start | bytes 2359304 | tf_op jit(solution)/shard_map/ppermute | solution.py:704
  141.8 47.0 %collective-permute-start.17 = (bf16[2,2,2,96,384]{4,3,2,1,0:T(8,128)(2,1)}, bf16[2,2,2,96,384]{4,3,2,1,0:T(8,128)(2,1)}, u32[]{:S(2)}, u32[]{:S(2)}) collective-permute-start(bf16[2,2,2,96,384]{4,3,2,1,0:T(8,128)(2,1)} %get-tuple-element.148), channel_id=1, source_target_pairs={{0,2},{1,3},{2,0},{3,1},{4,6},{5,7},{6,4},{7,5},{8,10},{9,11},{10,... | collective-permute-start | bytes 1769480 | tf_op jit(solution)/shard_map/ppermute | solution.py:712
  143.4 45.5 %collective-permute-start.18 = (bf16[2,4,96,384]{3,2,1,0:T(8,128)(2,1)}, bf16[2,4,96,384]{3,2,1,0:T(8,128)(2,1)}, u32[]{:S(2)}, u32[]{:S(2)}) collective-permute-start(bf16[2,4,96,384]{3,2,1,0:T(8,128)(2,1)} %get-tuple-element.149), channel_id=1, source_target_pairs={{0,16},{16,0},{8,24},{24,8},{1,17},{17,1},{9,25},{25,9},{2,18},{18... | collective-permute-start | bytes 1769480 | tf_op jit(solution)/shard_map/ppermute | solution.py:708
  164.8 24.0 %collective-permute-start.16 = (bf16[2,4,96,384]{3,2,1,0:T(8,128)(2,1)S(1)}, bf16[2,4,96,384]{3,2,1,0:T(8,128)(2,1)S(1)}, u32[]{:S(2)}, u32[]{:S(2)}) collective-permute-start(bf16[2,4,96,384]{3,2,1,0:T(8,128)(2,1)S(1)} %shard_map.250.refs_3_), channel_id=1, source_target_pairs={{0,2},{1,3},{2,0},{3,1},{4,6},{5,7},{6,4},{7,5},{8,10},{9,11},{10,... | collective-permute-start | bytes 1769480 | tf_op jit(solution)/shard_map/ppermute | solution.py:712
  169.7 21.7 %collective-permute-start.13 = (bf16[256,768]{1,0:T(8,128)(2,1)S(1)}, bf16[256,768]{1,0:T(8,128)(2,1)S(1)}, u32[]{:S(2)}, u32[]{:S(2)}) collective-permute-start(bf16[256,768]{1,0:T(8,128)(2,1)S(1)} %get-tuple-element.137), channel_id=1, source_target_pairs={{0,16},{16,0},{8,24},{24,8},{1,17},{17,1},{9,25},{25,9},{2,18},{18... | collective-permute-start | bytes 1179656 | tf_op jit(solution)/shard_map/ppermute | solution.py:708
  170.3 30.4 %collective-permute-start.20 = (bf16[4,4,96,384]{3,2,1,0:T(8,128)(2,1)S(1)}, bf16[4,4,96,384]{3,2,1,0:T(8,128)(2,1)S(1)}, u32[]{:S(2)}, u32[]{:S(2)}) collective-permute-start(bf16[4,4,96,384]{3,2,1,0:T(8,128)(2,1)S(1)} %get-tuple-element.141.refs_8_), channel_id=1, source_target_pairs={{0,1},{1,0},{2,3},{3,2},{4,5},{5,4},{6,7},{7,6},{8,9},{9,8},{10,11... | collective-permute-start | bytes 3538952 | tf_op jit(solution)/shard_map/ppermute | solution.py:712
  195.0 18.3 %collective-permute-start.24 = (bf16[4,96,384]{2,1,0:T(8,128)(2,1)S(1)}, bf16[4,96,384]{2,1,0:T(8,128)(2,1)S(1)}, u32[]{:S(2)}, u32[]{:S(2)}) collective-permute-start(bf16[4,96,384]{2,1,0:T(8,128)(2,1)S(1)} %get-tuple-element.150.refs_8_), channel_id=1, source_target_pairs={{0,4},{1,5},{2,6},{3,7},{4,0},{5,1},{6,2},{7,3},{8,12},{9,13},{10,... | collective-permute-start | bytes 884744 | tf_op jit(solution)/shard_map/ppermute | solution.py:712
  197.6 17.2 %collective-permute-start.23 = (bf16[8,96,384]{2,1,0:T(8,128)(2,1)S(1)}, bf16[8,96,384]{2,1,0:T(8,128)(2,1)S(1)}, u32[]{:S(2)}, u32[]{:S(2)}) collective-permute-start(bf16[8,96,384]{2,1,0:T(8,128)(2,1)S(1)} %get-tuple-element.155), channel_id=1, source_target_pairs={{0,1},{1,0},{2,3},{3,2},{4,5},{5,4},{6,7},{7,6},{8,9},{9,8},{10,11... | collective-permute-start | bytes 1769480 | tf_op jit(solution)/shard_map/ppermute | solution.py:712
  199.1 29.2 %collective-permute-start.19 = (bf16[256,768]{1,0:T(8,128)(2,1)S(1)}, bf16[256,768]{1,0:T(8,128)(2,1)S(1)}, u32[]{:S(2)}, u32[]{:S(2)}) collective-permute-start(bf16[256,768]{1,0:T(8,128)(2,1)S(1)} %get-tuple-element.152), channel_id=1, source_target_pairs={{0,16},{16,0},{8,24},{24,8},{1,17},{17,1},{9,25},{25,9},{2,18},{18... | collective-permute-start | bytes 1179656 | tf_op jit(solution)/shard_map/ppermute | solution.py:708
  202.5 14.0 %collective-permute-start.25 = (f32[32,768]{1,0:T(8,128)S(1)}, f32[32,768]{1,0:T(8,128)S(1)}, u32[]{:S(2)}, u32[]{:S(2)}) collective-permute-start(f32[32,768]{1,0:T(8,128)S(1)} %get-tuple-element.156.refs_18_), channel_id=1, source_target_pairs={{0,4},{1,5},{2,6},{3,7},{4,0},{5,1},{6,2},{7,3},{8,12},{9,13},{10,... | collective-permute-start | bytes 294920 | tf_op jit(solution)/shard_map/ppermute | solution.py:712
  202.9 22.5 %collective-permute-start.22 = (bf16[2,4,96,384]{3,2,1,0:T(8,128)(2,1)S(1)}, bf16[2,4,96,384]{3,2,1,0:T(8,128)(2,1)S(1)}, u32[]{:S(2)}, u32[]{:S(2)}) collective-permute-start(bf16[2,4,96,384]{3,2,1,0:T(8,128)(2,1)S(1)} %get-tuple-element.154.refs_10_), channel_id=1, source_target_pairs={{0,2},{1,3},{2,0},{3,1},{4,6},{5,7},{6,4},{7,5},{8,10},{9,11},{10,... | collective-permute-start | bytes 1769480 | tf_op jit(solution)/shard_map/ppermute | solution.py:712
  213.3 16.3 %collective-permute-start.29 = (bf16[2,4,96,384]{3,2,1,0:T(8,128)(2,1)S(1)}, bf16[2,4,96,384]{3,2,1,0:T(8,128)(2,1)S(1)}, u32[]{:S(2)}, u32[]{:S(2)}) collective-permute-start(bf16[2,4,96,384]{3,2,1,0:T(8,128)(2,1)S(1)} %get-tuple-element.163), channel_id=1, source_target_pairs={{0,16},{16,0},{8,24},{24,8},{1,17},{17,1},{9,25},{25,9},{2,18},{18... | collective-permute-start | bytes 1769480 | tf_op jit(solution)/shard_map/ppermute | solution.py:708
  214.8 16.0 %collective-permute-start.30 = (bf16[4,2,96,384]{3,2,1,0:T(8,128)(2,1)S(1)}, bf16[4,2,96,384]{3,2,1,0:T(8,128)(2,1)S(1)}, u32[]{:S(2)}, u32[]{:S(2)}) collective-permute-start(bf16[4,2,96,384]{3,2,1,0:T(8,128)(2,1)S(1)} %get-tuple-element.165), channel_id=1, source_target_pairs={{0,1},{1,0},{2,3},{3,2},{4,5},{5,4},{6,7},{7,6},{8,9},{9,8},{10,11... | collective-permute-start | bytes 1769480 | tf_op jit(solution)/shard_map/ppermute | solution.py:712
  229.6 24.7 %collective-permute-start.35 = (bf16[6,96,384]{2,1,0:T(8,128)(2,1)S(1)}, bf16[6,96,384]{2,1,0:T(8,128)(2,1)S(1)}, u32[]{:S(2)}, u32[]{:S(2)}) collective-permute-start(bf16[6,96,384]{2,1,0:T(8,128)(2,1)S(1)} %get-tuple-element.170), channel_id=1, source_target_pairs={{0,4},{1,5},{2,6},{3,7},{4,0},{5,1},{6,2},{7,3},{8,12},{9,13},{10,... | collective-permute-start | bytes 1327112 | tf_op jit(solution)/shard_map/ppermute | solution.py:712
  240.5 13.8 %collective-permute-start.34 = (bf16[2,2,96,384]{3,2,1,0:T(8,128)(2,1)S(1)}, bf16[2,2,96,384]{3,2,1,0:T(8,128)(2,1)S(1)}, u32[]{:S(2)}, u32[]{:S(2)}) collective-permute-start(bf16[2,2,96,384]{3,2,1,0:T(8,128)(2,1)S(1)} %get-tuple-element.169), channel_id=1, source_target_pairs={{0,2},{1,3},{2,0},{3,1},{4,6},{5,7},{6,4},{7,5},{8,10},{9,11},{10,... | collective-permute-start | bytes 884744 | tf_op jit(solution)/shard_map/ppermute | solution.py:712
  241.2 13.2 %collective-permute-start.28 = (bf16[4,96,384]{2,1,0:T(8,128)(2,1)S(1)}, bf16[4,96,384]{2,1,0:T(8,128)(2,1)S(1)}, u32[]{:S(2)}, u32[]{:S(2)}) collective-permute-start(bf16[4,96,384]{2,1,0:T(8,128)(2,1)S(1)} %collective-permute-done.26.refs_5_.refs_20_), channel_id=1, source_target_pairs={{0,8},{8,0},{16,24},{24,16},{1,9},{9,1},{17,25},{25,17},{2,10},{10... | collective-permute-start | bytes 884744 | tf_op jit(solution)/shard_map/ppermute | solution.py:704
  (58 other events, 477.8 us)

commit v6 on v5

--- a/solution.py
+++ b/solution.py
@@ -527,9 +527,8 @@
     copies = weight_copies(layer, core, weights, sides, sems)
     for copy in copies:
         copy.start()
-    for b in range(4):
-        rows = slice(b * BLOCK, (b + 1) * BLOCK)
-        d_ctx[rows] = dot_nt(in_order(gr_own, gr_rcv, b, core), w_out[0]).astype(BF)
+    grad_rows = jnp.concatenate([in_order(gr_own, gr_rcv, b, core) for b in range(4)])
+    d_ctx[...] = dot_nt(grad_rows, w_out[0]).astype(BF)
     product = d_ctx[...].astype(F32) * ctx[...].astype(F32)
     high = product.astype(BF)
     rest = (product - high.astype(F32)).astype(BF)

time: 297 us -> 298 us (level)
  no operation moved by 1% of the time
where the time goes in v6:
time: 298 us; the launch traced here: 293 us
  Pallas kernels  197 us (66%)
  waiting for transfers between devices  50.7 us (17%)
  starting transfers between devices  39.8 us (13%)
  local copies, waits for them, and re-layouts  3.02 us (1%)
    pallas_call x27, Pallas kernels, call(): return lambda *args: kernel(*args, *deps)  197 us
    ppermute x19, waiting for transfers between devices, to_dp(): return lax.ppermute(value, 'dp', [(i, i ^ distance) for i in range(8)])  37.2 us
    ppermute x19, starting transfers between devices, to_dp(): return lax.ppermute(value, 'dp', [(i, i ^ distance) for i in range(8)])  18.2 us
    ppermute x13, starting transfers between devices, to_chip(): return lax.ppermute(value, 'section', [(0, 2), (2, 0), (1, 3), (3, 1)])  17.7 us
    ppermute x13, waiting for transfers between devices, to_chip(): return lax.ppermute(value, 'section', [(0, 2), (2, 0), (1, 3), (3, 1)])  9.44 us
  transfers between devices with their start and end apart: 52, of which 15 were waited for; matrix products, arithmetic and copies ran while one was open for 0% of the time, Pallas kernels for 55%

profile of v6, /device:TPU:0, one launch (start us, length us, event | category | flops | bytes accessed | tf_op | source)
XLA Modules:
  0.0 292.6 jit_solution(17667664741976296505)
XLA Ops:
  2.9 15.6 %shard_map.237 = (bf16[1024,1152]{1,0:T(8,128)(2,1)}, bf16[1024,384]{1,0:T(8,128)(2,1)}, bf16[2,256,384]{2,1,0:T(8,128)(2,1)S(1)}, bf16[2,256,384]{2,1,0:T(8,128)(2,1)S(1)}, f32[8,1024]{1,0:T(8,128)S(1)}) custom-call(s32[4]{0:T(128)S(1)} %pad_add_fusion.sc, bf16[2,2,2,256,768]{4,3,2,1,0:T(8,128)(2,1)} %bitcast.10, bf16[2,2,2,256,768]{4,3,2,1,0:T(8,128)(2,1)} %bitcast.11, ...), custom_call_target="tpu_custom_call" | custom-call | flops 20999999488 | bytes 40000000 | tf_op jit(solution)/shard_map/pallas_call | solution.py:70
  20.3 13.2 %shard_map.238 = (bf16[512,768]{1,0:T(8,128)(2,1)S(1)}, bf16[512,768]{1,0:T(8,128)(2,1)S(1)}, bf16[512,3072]{1,0:T(8,128)(2,1)}, bf16[512,3072]{1,0:T(8,128)(2,1)}, bf16[2,256,768]{2,1,0:T(8,128)(2,1)S(1)}) custom-call(s32[4]{0:T(128)S(1)} %pad_add_fusion.sc, bf16[2,256,384]{2,1,0:T(8,128)(2,1)S(1)} %get-tuple-element.105.refs_0_, ...), custom_call_target="tpu_custom_call" | custom-call | flops 27000000512 | bytes 100000000 | tf_op jit(solution)/shard_map/pallas_call | solution.py:70
  34.1 2.8 collective-permute-start.4
  36.9 14.9 %shard_map.239 = (bf16[1024,1152]{1,0:T(8,128)(2,1)}, bf16[1024,384]{1,0:T(8,128)(2,1)}, bf16[2,256,384]{2,1,0:T(8,128)(2,1)S(1)}, bf16[2,256,384]{2,1,0:T(8,128)(2,1)S(1)}, f32[8,1024]{1,0:T(8,128)S(1)}) custom-call(s32[4]{0:T(128)S(1)} %pad_add_fusion.sc, bf16[1,2,1,256,768]{4,3,2,1,0:T(8,128)(2,1)S(1)} %bitcast.16, ...), custom_call_target="tpu_custom_call" | custom-call | flops 20999999488 | bytes 40000000 | tf_op jit(solution)/shard_map/pallas_call | solution.py:70
  54.7 2.7 shard_map.240
  59.3 10.9 %shard_map.241 = (bf16[512,3072]{1,0:T(8,128)(2,1)S(1)}, bf16[512,3072]{1,0:T(8,128)(2,1)S(1)}, f32[256,768]{1,0:T(8,128)S(1)}, bf16[256,768]{1,0:T(8,128)(2,1)S(1)}) custom-call(s32[4]{0:T(128)S(1)} %pad_add_fusion.sc, bf16[512,768]{1,0:T(8,128)(2,1)S(1)} %get-tuple-element.111.refs_0_.refs_1_.refs_2_, ...), custom_call_target="tpu_custom_call" | custom-call | flops 24000000000 | bytes 90000000 | tf_op jit(solution)/shard_map/pallas_call | solution.py:70
  70.2 10.2 %shard_map.242 = (bf16[512,3072]{1,0:T(8,128)(2,1)S(1)}, bf16[2,256,768]{2,1,0:T(8,128)(2,1)S(1)}, f32[8,768]{1,0:T(8,128)S(1)}) custom-call(s32[4]{0:T(128)S(1)} %pad_add_fusion.sc, bf16[2,2,2,256,768]{4,3,2,1,0:T(8,128)(2,1)S(1)} %bitcast.20, bf16[512,768]{1,0:T(8,128)(2,1)S(1)} %get-tuple-element.111.refs_0_.refs_1_.refs_2_, ...), custom_call_target="tpu_custom_call" | custom-call | flops 24500000768 | bytes 90000000 | tf_op jit(solution)/shard_map/pallas_call | solution.py:70
  80.5 18.7 %shard_map.243 = (bf16[2,4,4,96,384]{4,3,2,1,0:T(8,128)(2,1)}, bf16[2,4,4,96,384]{4,3,2,1,0:T(8,128)(2,1)S(1)}) custom-call(s32[4]{0:T(128)S(1)} %pad_add_fusion.sc, bf16[2,2,2,256,768]{4,3,2,1,0:T(8,128)(2,1)S(1)} %bitcast.21, bf16[2,2,2,256,768]{4,3,2,1,0:T(8,128)(2,1)S(1)} %bitcast.22, bf16[512,768]{1,0:T(8,128)(2,1)S(1)} %get-tuple-element.111.refs_0_.refs_1_.refs_2_, ...), custom_call_target="tpu_custom_call" | custom-call | flops 43000000512 | bytes 110000000 | tf_op jit(solution)/shard_map/pallas_call | solution.py:70
  99.7 17.5 %shard_map.244 = (bf16[1024,1152]{1,0:T(8,128)(2,1)S(1)}, f32[2,256,768]{2,1,0:T(8,128)S(1)}, bf16[2,256,768]{2,1,0:T(8,128)(2,1)S(1)}) custom-call(s32[4]{0:T(128)S(1)} %pad_add_fusion.sc, bf16[2,256,768]{2,1,0:T(8,128)(2,1)S(1)} %get-tuple-element.114.refs_0_.refs_5_, bf16[2,256,768]{2,1,0:T(8,128)(2,1)S(1)} %collective-permute-done.6.refs_1_.refs_6_, ...), custom_call_target="tpu_custom_call" | custom-call | flops 42500001792 | bytes 60000000 | tf_op jit(solution)/shard_map/pallas_call | solution.py:70
  123.6 11.5 %shard_map.247 = (bf16[512,3072]{1,0:T(8,128)(2,1)S(1)}, bf16[2,256,768]{2,1,0:T(8,128)(2,1)}, f32[8,768]{1,0:T(8,128)S(1)}) custom-call(s32[4]{0:T(128)S(1)} %pad_add_fusion.sc, bf16[1,2,1,256,768]{4,3,2,1,0:T(8,128)(2,1)S(1)} %bitcast.25, bf16[512,768]{1,0:T(8,128)(2,1)S(1)} %copy-done.10, f32[2,1,768]{2,1,0:T(1,128)S(1)} %reshape.70.refs_5_.refs_1_.refs_2_.refs_4_, ...), custom_call_target="tpu_custom_call" | custom-call | flops 24500000768 | bytes 90000000 | tf_op jit(solution)/shard_map/pallas_call | solution.py:70
  135.1 6.8 %shard_map.248 = (bf16[2,4,96,384]{3,2,1,0:T(8,128)(2,1)}, bf16[2,4,96,384]{3,2,1,0:T(8,128)(2,1)}, bf16[2,2,2,96,384]{4,3,2,1,0:T(8,128)(2,1)}, bf16[2,2,2,96,384]{4,3,2,1,0:T(8,128)(2,1)}) custom-call(s32[4]{0:T(128)S(1)} %pad_add_fusion.sc, bf16[1,2,1,256,768]{4,3,2,1,0:T(8,128)(2,1)S(1)} %bitcast.19, bf16[1,2,1,256,768]{4,3,2,1,0:T(8,128)(2,1)S(1)} %bitcast.24, ...), custom_call_target="tpu_custom_call" | custom-call | flops 12499999744 | bytes 60000000 | tf_op jit(solution)/shard_map/pallas_call | solution.py:70
  144.9 18.2 %shard_map.249 = (bf16[2,4,4,96,384]{4,3,2,1,0:T(8,128)(2,1)}, bf16[2,4,4,96,384]{4,3,2,1,0:T(8,128)(2,1)S(1)}) custom-call(s32[4]{0:T(128)S(1)} %pad_add_fusion.sc, bf16[1,2,1,256,768]{4,3,2,1,0:T(8,128)(2,1)S(1)} %bitcast.26, bf16[1,2,1,256,768]{4,3,2,1,0:T(8,128)(2,1)S(1)} %bitcast.27, bf16[512,768]{1,0:T(8,128)(2,1)S(1)} %copy-done.10, ...), custom_call_target="tpu_custom_call" | custom-call | flops 43000000512 | bytes 110000000 | tf_op jit(solution)/shard_map/pallas_call | solution.py:70
  170.8 18.1 %shard_map.252 = (bf16[1024,1152]{1,0:T(8,128)(2,1)S(1)}, f32[2,256,768]{2,1,0:T(8,128)S(1)}, bf16[2,256,768]{2,1,0:T(8,128)(2,1)S(1)}) custom-call(s32[4]{0:T(128)S(1)} %pad_add_fusion.sc, bf16[2,256,768]{2,1,0:T(8,128)(2,1)} %get-tuple-element.132.refs_10_.refs_0_.refs_5_, bf16[2,256,768]{2,1,0:T(8,128)(2,1)} %collective-permute-done.14.refs_1_.refs_6_, ...), custom_call_target="tpu_custom_call" | custom-call | flops 42500001792 | bytes 60000000 | tf_op jit(solution)/shard_map/pallas_call | solution.py:70
  191.6 3.0 %shard_map.254 = (f32[256,768]{1,0:T(8,128)S(1)}, bf16[256,768]{1,0:T(8,128)(2,1)S(1)}, f32[32,768]{1,0:T(8,128)S(1)}) custom-call(s32[4]{0:T(128)S(1)} %pad_add_fusion.sc, bf16[2,256,768]{2,1,0:T(8,128)(2,1)} %get-tuple-element.132.refs_10_.refs_0_.refs_5_, f32[2,256,768]{2,1,0:T(8,128)S(1)} %get-tuple-element.142.refs_10_.refs_1_, ...), custom_call_target="tpu_custom_call" | custom-call | flops 1000000000 | bytes 25000000 | tf_op jit(solution)/shard_map/pallas_call | solution.py:70
  195.2 2.6 collective-permute-start.24
  203.5 7.7 %shard_map.256 = (bf16[2,4,96,384]{3,2,1,0:T(8,128)(2,1)}, bf16[2,4,96,384]{3,2,1,0:T(8,128)(2,1)S(1)}, bf16[4,2,96,384]{3,2,1,0:T(8,128)(2,1)}, bf16[4,2,96,384]{3,2,1,0:T(8,128)(2,1)S(1)}) custom-call(s32[4]{0:T(128)S(1)} %pad_add_fusion.sc, bf16[2,2,2,256,768]{4,3,2,1,0:T(8,128)(2,1)S(1)} %bitcast.14, bf16[2,2,2,256,768]{4,3,2,1,0:T(8,128)(2,1)S(1)} %bitcast.15, ...), custom_call_target="tpu_custom_call" | custom-call | flops 12499999744 | bytes 60000000 | tf_op jit(solution)/shard_map/pallas_call | solution.py:70
  216.6 9.0 %collective-permute-done.22.refs_3_.refs_12_ = bf16[2,4,96,384]{3,2,1,0:T(8,128)(2,1)S(1)} collective-permute-done((bf16[2,4,96,384]{3,2,1,0:T(8,128)(2,1)S(1)}, bf16[2,4,96,384]{3,2,1,0:T(8,128)(2,1)S(1)}, u32[]{:S(2)}, u32[]{:S(2)}) %collective-permute-start.22) | collective-permute-done | bytes 589856 | tf_op jit(solution)/shard_map/ppermute | solution.py:711
  237.2 3.5 %collective-permute-done.36.refs_19_ = f32[32,768]{1,0:T(8,128)S(1)} collective-permute-done((f32[32,768]{1,0:T(8,128)S(1)}, f32[32,768]{1,0:T(8,128)S(1)}, u32[]{:S(2)}, u32[]{:S(2)}) %collective-permute-start.36) | collective-permute-done | bytes 98336 | tf_op jit(solution)/shard_map/ppermute | solution.py:707
  241.3 4.4 %collective-permute-done.33.refs_5_.refs_8_.refs_2_ = bf16[4,96,384]{2,1,0:T(8,128)(2,1)S(1)} collective-permute-done((bf16[4,96,384]{2,1,0:T(8,128)(2,1)S(1)}, bf16[4,96,384]{2,1,0:T(8,128)(2,1)S(1)}, u32[]{:S(2)}, u32[]{:S(2)}) %collective-permute-start.33) | collective-permute-done | bytes 294944 | tf_op jit(solution)/shard_map/ppermute | solution.py:711
  245.7 8.7 %collective-permute-done.34.refs_2_.refs_6_ = bf16[2,2,96,384]{3,2,1,0:T(8,128)(2,1)S(1)} collective-permute-done((bf16[2,2,96,384]{3,2,1,0:T(8,128)(2,1)S(1)}, bf16[2,2,96,384]{3,2,1,0:T(8,128)(2,1)S(1)}, u32[]{:S(2)}, u32[]{:S(2)}) %collective-permute-start.34) | collective-permute-done | bytes 294944 | tf_op jit(solution)/shard_map/ppermute | solution.py:711
  261.0 7.1 %collective-permute-done.40.refs_11_ = f32[32,768]{1,0:T(8,128)S(1)} collective-permute-done((f32[32,768]{1,0:T(8,128)S(1)}, f32[32,768]{1,0:T(8,128)S(1)}, u32[]{:S(2)}, u32[]{:S(2)}) %collective-permute-start.40) | collective-permute-done | bytes 98336 | tf_op jit(solution)/shard_map/ppermute | solution.py:711
  274.1 3.3 %shard_map.258 = (f32[2,1,256,768]{3,2,1,0:T(8,128)}, f32[2,1,256,768]{3,2,1,0:T(8,128)}, f32[2,96,3072]{2,1,0:T(8,128)}, f32[2,384,768]{2,1,0:T(8,128)}) custom-call(s32[4]{0:T(128)S(1)} %pad_add_fusion.sc, f32[256,768]{1,0:T(8,128)S(1)} %get-tuple-element.112.refs_0_, bf16[256,768]{1,0:T(8,128)(2,1)S(1)} %copy-done.3, f32[256,768]{1,0:T(8,128)S(1)} %copy-done.5, ...), custom_call_target="tpu_custom_call" | custom-call | flops 5000000 | bytes 45000000 | tf_op jit(solution)/shard_map/pallas_call | solution.py:70
  283.9 3.5 %collective-permute-done.47.refs_8_ = bf16[2,96,384]{2,1,0:T(8,128)(2,1)S(1)} collective-permute-done((bf16[2,96,384]{2,1,0:T(8,128)(2,1)S(1)}, bf16[2,96,384]{2,1,0:T(8,128)(2,1)S(1)}, u32[]{:S(2)}, u32[]{:S(2)}) %collective-permute-start.47) | collective-permute-done | bytes 147488 | tf_op jit(solution)/shard_map/ppermute | solution.py:707
  288.8 3.3 %shard_map.263 = (f32[2,96,3072]{2,1,0:T(8,128)}, f32[2,384,768]{2,1,0:T(8,128)}, f32[2,96,2304]{2,1,0:T(8,128)}, f32[2,96,768]{2,1,0:T(8,128)}, f32[2,96]{1,0:T...) custom-call(s32[4]{0:T(128)S(1)} %pad_add_fusion.sc, ...), custom_call_target="tpu_custom_call", output_to_operand_aliasing={{0}: (2, {}), {1}: (3, {})} | custom-call | flops 5000000 | bytes 55000000 | tf_op jit(solution)/shard_map/pallas_call | solution.py:70
  (175 shorter events, 73.8 us)
Async XLA Ops:
  33.9 18.4 %collective-permute-start.3 = (bf16[2,256,384]{2,1,0:T(8,128)(2,1)S(1)}, bf16[2,256,384]{2,1,0:T(8,128)(2,1)S(1)}, u32[]{:S(2)}, u32[]{:S(2)}) collective-permute-start(bf16[2,256,384]{2,1,0:T(8,128)(2,1)S(1)} %get-tuple-element.105.refs_0_), channel_id=1, source_target_pairs={{0,8},{8,0},{16,24},{24,16},{1,9},{9,1},{17,25},{25,17},{2,10},{10... | collective-permute-start | bytes 1179656 | tf_op jit(solution)/shard_map/ppermute | solution.py:703
  34.1 20.7 %collective-permute-start.4 = (bf16[512,768]{1,0:T(8,128)(2,1)S(1)}, bf16[512,768]{1,0:T(8,128)(2,1)S(1)}, u32[]{:S(2)}, u32[]{:S(2)}) collective-permute-start(bf16[512,768]{1,0:T(8,128)(2,1)S(1)} %get-tuple-element.110.refs_1_.refs_2_), channel_id=1, source_target_pairs={{0,16},{16,0},{8,24},{24,8},{1,17},{17,1},{9,25},{25,9},{2,18},{18... | collective-permute-start | bytes 2359304 | tf_op jit(solution)/shard_map/ppermute | solution.py:707
  51.9 18.3 %collective-permute-start.5 = (bf16[2,256,384]{2,1,0:T(8,128)(2,1)S(1)}, bf16[2,256,384]{2,1,0:T(8,128)(2,1)S(1)}, u32[]{:S(2)}, u32[]{:S(2)}) collective-permute-start(bf16[2,256,384]{2,1,0:T(8,128)(2,1)S(1)} %get-tuple-element.108.refs_0_), channel_id=1, source_target_pairs={{0,8},{8,0},{16,24},{24,16},{1,9},{9,1},{17,25},{25,17},{2,10},{10... | collective-permute-start | bytes 1179656 | tf_op jit(solution)/shard_map/ppermute | solution.py:703
  57.5 23.1 %collective-permute-start.7 = (bf16[512,768]{1,0:T(8,128)(2,1)S(1)}, bf16[512,768]{1,0:T(8,128)(2,1)S(1)}, u32[]{:S(2)}, u32[]{:S(2)}) collective-permute-start(bf16[512,768]{1,0:T(8,128)(2,1)S(1)} %get-tuple-element.111.refs_0_.refs_1_.refs_2_), channel_id=1, source_target_pairs={{0,16},{16,0},{8,24},{24,8},{1,17},{17,1},{9,25},{25,9},{2,18},{18... | collective-permute-start | bytes 2359304 | tf_op jit(solution)/shard_map/ppermute | solution.py:707
  80.4 19.2 %collective-permute-start.6 = (bf16[2,256,768]{2,1,0:T(8,128)(2,1)S(1)}, bf16[2,256,768]{2,1,0:T(8,128)(2,1)S(1)}, u32[]{:S(2)}, u32[]{:S(2)}) collective-permute-start(bf16[2,256,768]{2,1,0:T(8,128)(2,1)S(1)} %get-tuple-element.114.refs_0_.refs_5_), channel_id=1, source_target_pairs={{0,8},{8,0},{16,24},{24,16},{1,9},{9,1},{17,25},{25,17},{2,10},{10... | collective-permute-start | bytes 2359304 | tf_op jit(solution)/shard_map/ppermute | solution.py:703
  99.2 18.1 %collective-permute-start.9 = (bf16[2,4,4,96,384]{4,3,2,1,0:T(8,128)(2,1)S(1)}, bf16[2,4,4,96,384]{4,3,2,1,0:T(8,128)(2,1)S(1)}, u32[]{:S(2)}, u32[]{:S(2)}) collective-permute-start(bf16[2,4,4,96,384]{4,3,2,1,0:T(8,128)(2,1)S(1)} %get-tuple-element.123), channel_id=1, source_target_pairs={{0,8},{8,0},{16,24},{24,16},{1,9},{9,1},{17,25},{25,17},{2,10},{10... | collective-permute-start | bytes 7077896 | tf_op jit(solution)/shard_map/ppermute | solution.py:703
  119.5 43.6 %collective-permute-start.12 = (bf16[4,4,96,384]{3,2,1,0:T(8,128)(2,1)S(1)}, bf16[4,4,96,384]{3,2,1,0:T(8,128)(2,1)S(1)}, u32[]{:S(2)}, u32[]{:S(2)}) collective-permute-start(bf16[4,4,96,384]{3,2,1,0:T(8,128)(2,1)S(1)} %get-tuple-element.125.refs_5_), channel_id=1, source_target_pairs={{0,1},{1,0},{2,3},{3,2},{4,5},{5,4},{6,7},{7,6},{8,9},{9,8},{10,11... | collective-permute-start | bytes 3538952 | tf_op jit(solution)/shard_map/ppermute | solution.py:711
  122.9 22.0 %collective-permute-start.10 = (bf16[2,256,768]{2,1,0:T(8,128)(2,1)S(1)}, bf16[2,256,768]{2,1,0:T(8,128)(2,1)S(1)}, u32[]{:S(2)}, u32[]{:S(2)}) collective-permute-start(bf16[2,256,768]{2,1,0:T(8,128)(2,1)S(1)} %get-tuple-element.126), channel_id=1, source_target_pairs={{0,16},{16,0},{8,24},{24,8},{1,17},{17,1},{9,25},{25,9},{2,18},{18... | collective-permute-start | bytes 2359304 | tf_op jit(solution)/shard_map/ppermute | solution.py:707
  135.0 35.3 %collective-permute-start.14 = (bf16[2,256,768]{2,1,0:T(8,128)(2,1)}, bf16[2,256,768]{2,1,0:T(8,128)(2,1)}, u32[]{:S(2)}, u32[]{:S(2)}) collective-permute-start(bf16[2,256,768]{2,1,0:T(8,128)(2,1)} %get-tuple-element.132.refs_10_.refs_0_.refs_5_), channel_id=1, source_target_pairs={{0,8},{8,0},{16,24},{24,16},{1,9},{9,1},{17,25},{25,17},{2,10},{10... | collective-permute-start | bytes 2359304 | tf_op jit(solution)/shard_map/ppermute | solution.py:703
  141.9 47.1 %collective-permute-start.17 = (bf16[2,2,2,96,384]{4,3,2,1,0:T(8,128)(2,1)}, bf16[2,2,2,96,384]{4,3,2,1,0:T(8,128)(2,1)}, u32[]{:S(2)}, u32[]{:S(2)}) collective-permute-start(bf16[2,2,2,96,384]{4,3,2,1,0:T(8,128)(2,1)} %get-tuple-element.148), channel_id=1, source_target_pairs={{0,2},{1,3},{2,0},{3,1},{4,6},{5,7},{6,4},{7,5},{8,10},{9,11},{10,... | collective-permute-start | bytes 1769480 | tf_op jit(solution)/shard_map/ppermute | solution.py:711
  143.4 45.6 %collective-permute-start.18 = (bf16[2,4,96,384]{3,2,1,0:T(8,128)(2,1)}, bf16[2,4,96,384]{3,2,1,0:T(8,128)(2,1)}, u32[]{:S(2)}, u32[]{:S(2)}) collective-permute-start(bf16[2,4,96,384]{3,2,1,0:T(8,128)(2,1)} %get-tuple-element.149), channel_id=1, source_target_pairs={{0,16},{16,0},{8,24},{24,8},{1,17},{17,1},{9,25},{25,9},{2,18},{18... | collective-permute-start | bytes 1769480 | tf_op jit(solution)/shard_map/ppermute | solution.py:707
  164.9 24.1 %collective-permute-start.16 = (bf16[2,4,96,384]{3,2,1,0:T(8,128)(2,1)S(1)}, bf16[2,4,96,384]{3,2,1,0:T(8,128)(2,1)S(1)}, u32[]{:S(2)}, u32[]{:S(2)}) collective-permute-start(bf16[2,4,96,384]{3,2,1,0:T(8,128)(2,1)S(1)} %shard_map.250.refs_3_), channel_id=1, source_target_pairs={{0,2},{1,3},{2,0},{3,1},{4,6},{5,7},{6,4},{7,5},{8,10},{9,11},{10,... | collective-permute-start | bytes 1769480 | tf_op jit(solution)/shard_map/ppermute | solution.py:711
  169.7 21.8 %collective-permute-start.13 = (bf16[256,768]{1,0:T(8,128)(2,1)S(1)}, bf16[256,768]{1,0:T(8,128)(2,1)S(1)}, u32[]{:S(2)}, u32[]{:S(2)}) collective-permute-start(bf16[256,768]{1,0:T(8,128)(2,1)S(1)} %get-tuple-element.137), channel_id=1, source_target_pairs={{0,16},{16,0},{8,24},{24,8},{1,17},{17,1},{9,25},{25,9},{2,18},{18... | collective-permute-start | bytes 1179656 | tf_op jit(solution)/shard_map/ppermute | solution.py:707
  170.3 30.4 %collective-permute-start.20 = (bf16[4,4,96,384]{3,2,1,0:T(8,128)(2,1)S(1)}, bf16[4,4,96,384]{3,2,1,0:T(8,128)(2,1)S(1)}, u32[]{:S(2)}, u32[]{:S(2)}) collective-permute-start(bf16[4,4,96,384]{3,2,1,0:T(8,128)(2,1)S(1)} %get-tuple-element.141.refs_8_), channel_id=1, source_target_pairs={{0,1},{1,0},{2,3},{3,2},{4,5},{5,4},{6,7},{7,6},{8,9},{9,8},{10,11... | collective-permute-start | bytes 3538952 | tf_op jit(solution)/shard_map/ppermute | solution.py:711
  195.2 18.3 %collective-permute-start.24 = (bf16[4,96,384]{2,1,0:T(8,128)(2,1)S(1)}, bf16[4,96,384]{2,1,0:T(8,128)(2,1)S(1)}, u32[]{:S(2)}, u32[]{:S(2)}) collective-permute-start(bf16[4,96,384]{2,1,0:T(8,128)(2,1)S(1)} %get-tuple-element.150.refs_8_), channel_id=1, source_target_pairs={{0,4},{1,5},{2,6},{3,7},{4,0},{5,1},{6,2},{7,3},{8,12},{9,13},{10,... | collective-permute-start | bytes 884744 | tf_op jit(solution)/shard_map/ppermute | solution.py:711
  197.8 17.2 %collective-permute-start.23 = (bf16[8,96,384]{2,1,0:T(8,128)(2,1)S(1)}, bf16[8,96,384]{2,1,0:T(8,128)(2,1)S(1)}, u32[]{:S(2)}, u32[]{:S(2)}) collective-permute-start(bf16[8,96,384]{2,1,0:T(8,128)(2,1)S(1)} %get-tuple-element.155), channel_id=1, source_target_pairs={{0,1},{1,0},{2,3},{3,2},{4,5},{5,4},{6,7},{7,6},{8,9},{9,8},{10,11... | collective-permute-start | bytes 1769480 | tf_op jit(solution)/shard_map/ppermute | solution.py:711
  199.3 29.3 %collective-permute-start.19 = (bf16[256,768]{1,0:T(8,128)(2,1)S(1)}, bf16[256,768]{1,0:T(8,128)(2,1)S(1)}, u32[]{:S(2)}, u32[]{:S(2)}) collective-permute-start(bf16[256,768]{1,0:T(8,128)(2,1)S(1)} %get-tuple-element.152), channel_id=1, source_target_pairs={{0,16},{16,0},{8,24},{24,8},{1,17},{17,1},{9,25},{25,9},{2,18},{18... | collective-permute-start | bytes 1179656 | tf_op jit(solution)/shard_map/ppermute | solution.py:707
  202.6 14.0 %collective-permute-start.25 = (f32[32,768]{1,0:T(8,128)S(1)}, f32[32,768]{1,0:T(8,128)S(1)}, u32[]{:S(2)}, u32[]{:S(2)}) collective-permute-start(f32[32,768]{1,0:T(8,128)S(1)} %get-tuple-element.156.refs_18_), channel_id=1, source_target_pairs={{0,4},{1,5},{2,6},{3,7},{4,0},{5,1},{6,2},{7,3},{8,12},{9,13},{10,... | collective-permute-start | bytes 294920 | tf_op jit(solution)/shard_map/ppermute | solution.py:711
  203.0 22.5 %collective-permute-start.22 = (bf16[2,4,96,384]{3,2,1,0:T(8,128)(2,1)S(1)}, bf16[2,4,96,384]{3,2,1,0:T(8,128)(2,1)S(1)}, u32[]{:S(2)}, u32[]{:S(2)}) collective-permute-start(bf16[2,4,96,384]{3,2,1,0:T(8,128)(2,1)S(1)} %get-tuple-element.154.refs_10_), channel_id=1, source_target_pairs={{0,2},{1,3},{2,0},{3,1},{4,6},{5,7},{6,4},{7,5},{8,10},{9,11},{10,... | collective-permute-start | bytes 1769480 | tf_op jit(solution)/shard_map/ppermute | solution.py:711
  213.5 16.2 %collective-permute-start.29 = (bf16[2,4,96,384]{3,2,1,0:T(8,128)(2,1)S(1)}, bf16[2,4,96,384]{3,2,1,0:T(8,128)(2,1)S(1)}, u32[]{:S(2)}, u32[]{:S(2)}) collective-permute-start(bf16[2,4,96,384]{3,2,1,0:T(8,128)(2,1)S(1)} %get-tuple-element.163), channel_id=1, source_target_pairs={{0,16},{16,0},{8,24},{24,8},{1,17},{17,1},{9,25},{25,9},{2,18},{18... | collective-permute-start | bytes 1769480 | tf_op jit(solution)/shard_map/ppermute | solution.py:707
  215.0 16.0 %collective-permute-start.30 = (bf16[4,2,96,384]{3,2,1,0:T(8,128)(2,1)S(1)}, bf16[4,2,96,384]{3,2,1,0:T(8,128)(2,1)S(1)}, u32[]{:S(2)}, u32[]{:S(2)}) collective-permute-start(bf16[4,2,96,384]{3,2,1,0:T(8,128)(2,1)S(1)} %get-tuple-element.165), channel_id=1, source_target_pairs={{0,1},{1,0},{2,3},{3,2},{4,5},{5,4},{6,7},{7,6},{8,9},{9,8},{10,11... | collective-permute-start | bytes 1769480 | tf_op jit(solution)/shard_map/ppermute | solution.py:711
  229.7 24.6 %collective-permute-start.35 = (bf16[6,96,384]{2,1,0:T(8,128)(2,1)S(1)}, bf16[6,96,384]{2,1,0:T(8,128)(2,1)S(1)}, u32[]{:S(2)}, u32[]{:S(2)}) collective-permute-start(bf16[6,96,384]{2,1,0:T(8,128)(2,1)S(1)} %get-tuple-element.170), channel_id=1, source_target_pairs={{0,4},{1,5},{2,6},{3,7},{4,0},{5,1},{6,2},{7,3},{8,12},{9,13},{10,... | collective-permute-start | bytes 1327112 | tf_op jit(solution)/shard_map/ppermute | solution.py:711
  240.8 13.6 %collective-permute-start.34 = (bf16[2,2,96,384]{3,2,1,0:T(8,128)(2,1)S(1)}, bf16[2,2,96,384]{3,2,1,0:T(8,128)(2,1)S(1)}, u32[]{:S(2)}, u32[]{:S(2)}) collective-permute-start(bf16[2,2,96,384]{3,2,1,0:T(8,128)(2,1)S(1)} %get-tuple-element.169), channel_id=1, source_target_pairs={{0,2},{1,3},{2,0},{3,1},{4,6},{5,7},{6,4},{7,5},{8,10},{9,11},{10,... | collective-permute-start | bytes 884744 | tf_op jit(solution)/shard_map/ppermute | solution.py:711
  241.3 13.1 %collective-permute-start.28 = (bf16[4,96,384]{2,1,0:T(8,128)(2,1)S(1)}, bf16[4,96,384]{2,1,0:T(8,128)(2,1)S(1)}, u32[]{:S(2)}, u32[]{:S(2)}) collective-permute-start(bf16[4,96,384]{2,1,0:T(8,128)(2,1)S(1)} %collective-permute-done.26.refs_5_.refs_20_), channel_id=1, source_target_pairs={{0,8},{8,0},{16,24},{24,16},{1,9},{9,1},{17,25},{25,17},{2,10},{10... | collective-permute-start | bytes 884744 | tf_op jit(solution)/shard_map/ppermute | solution.py:703
  (58 other events, 478.8 us)
